TPU v7x, 32 devices: a whole 2x2x4 slice. The times are simulated.
32 devices in a mesh: prow: 4 (over z), pcol: 8 (over y, x, core).
Axes of the slice: x: 2, y: 2, z: 4, core: 2. Of those that a mesh axis runs over, the one named last changes fastest.
Arguments:
- matrix: bfloat16 [4, 1024, 2, 2048], P(None, 'prow', None, 'pcol'), may hold values from -6 to 6
- pivots: int32 [4, 256], replicated, may hold values from 0 to 4095, as said below
- lower_inverse: bfloat16 [4, 256, 256], replicated, as said below
- upper_inverse: bfloat16 [4, 256, 256], replicated, as said below
Outputs:
- factored: bfloat16 [4, 1024, 2, 2048], P(None, 'prow', None, 'pcol')
Inputs may be any that keep to these rules, and one draw needn't show every extreme that they name: For step s and each i, pivots[s, i] is either s * 256 + i or a row index of s * 256 + 256 or more; the pivots of one step that differ from s * 256 + i are distinct. lower_inverse[s] is unit lower triangular. upper_inverse[s] is upper triangular.
All inputs are finite; a program needn't handle non-finite values.
Results may differ from a plain program's by a relative error of at most 0.0071.
Values may be sent and summed in bfloat16 or wider, within the bound.
No kernel may reach another device: no remote copies, remote signals or barrier semaphores. Data moves between devices by JAX's collectives and lax.ppermute only.
A program may use at most 64 MiB of HBM per device.

v0:
```python
import jax
import jax.numpy as jnp
from jax import lax
from jax.sharding import PartitionSpec as P


def spread(value, axis, source):
    kept = jnp.where(lax.axis_index(axis) == source, value, 0).astype(value.dtype)
    return lax.psum(kept, axis)


def local(matrix, pivots, lower_inverse, upper_inverse):
    row_blocks = matrix.shape[0]
    block_size = matrix.shape[1]
    col_blocks = matrix.shape[2]
    local_rows = row_blocks * block_size
    local_cols = col_blocks * block_size
    matrix_loc = matrix.reshape(local_rows, local_cols)
    row_count = lax.axis_size("prow")
    col_count = lax.axis_size("pcol")
    my_row = lax.axis_index("prow")
    my_col = lax.axis_index("pcol")
    row_iota = jnp.arange(local_rows, dtype=jnp.int32)
    col_iota = jnp.arange(local_cols, dtype=jnp.int32)
    global_row = (row_iota // block_size * row_count + my_row) * block_size + row_iota % block_size
    global_col = (col_iota // block_size * col_count + my_col) * block_size + col_iota % block_size
    for step_num in range(pivots.shape[0]):
        begin_at = step_num * block_size
        trail_at = begin_at + block_size
        diag_root = step_num % row_count
        diag_local = step_num // row_count * block_size
        panel_root = step_num % col_count
        panel_local = step_num // col_count * block_size
        targets = begin_at + jnp.arange(block_size, dtype=jnp.int32)
        chosen = pivots[step_num]
        chosen_block = chosen // block_size
        chosen_owner = chosen_block % row_count
        is_mine = chosen_owner == my_row
        chosen_local = chosen_block // row_count * block_size + chosen % block_size
        picked = jnp.take(matrix_loc, jnp.where(is_mine, chosen_local, 0), axis=0)
        picked = jnp.where(is_mine[:, None], picked, jnp.zeros_like(picked))
        diag_rows = matrix_loc[diag_local : diag_local + block_size]
        own_diag = jnp.where(my_row == diag_root, diag_rows, jnp.zeros_like(diag_rows))
        summed_rows, summed_diag = (
            lax.psum(picked, "prow").astype(jnp.float32),
            lax.psum(own_diag, "prow").astype(jnp.float32),
        )
        new_rows = summed_rows.astype(jnp.bfloat16)
        old_diag = summed_diag.astype(jnp.bfloat16)
        moved_rows = is_mine & (chosen != targets)
        matrix_loc = matrix_loc.at[jnp.where(moved_rows, chosen_local, local_rows)].set(
            old_diag, mode="drop"
        )
        diag_after = matrix_loc[diag_local : diag_local + block_size]
        matrix_loc = matrix_loc.at[diag_local : diag_local + block_size].set(
            jnp.where(my_row == diag_root, new_rows, diag_after)
        )
        upper_full = jnp.dot(
            lower_inverse[step_num], new_rows, preferred_element_type=jnp.float32
        ).astype(jnp.bfloat16)
        col_live = global_col >= trail_at
        upper_use = jnp.where(col_live[None, :], upper_full, jnp.zeros_like(upper_full))
        panel_own = matrix_loc[:, panel_local : panel_local + block_size]
        received = spread(panel_own, "pcol", panel_root)
        left_full = jnp.dot(
            received, upper_inverse[step_num], preferred_element_type=jnp.float32
        ).astype(jnp.bfloat16)
        row_live = global_row >= trail_at
        left_use = jnp.where(row_live[:, None], left_full, jnp.zeros_like(left_full))
        matrix_loc = (
            matrix_loc.astype(jnp.float32)
            - jnp.dot(left_use, upper_use, preferred_element_type=jnp.float32)
        ).astype(jnp.bfloat16)
        panel_now = matrix_loc[:, panel_local : panel_local + block_size]
        panel_put = jnp.where(row_live[:, None] & (my_col == panel_root), left_full, panel_now)
        matrix_loc = matrix_loc.at[:, panel_local : panel_local + block_size].set(panel_put)
        diag_now = matrix_loc[diag_local : diag_local + block_size]
        diag_put = jnp.where(col_live[None, :] & (my_row == diag_root), upper_full, diag_now)
        matrix_loc = matrix_loc.at[diag_local : diag_local + block_size].set(diag_put)
    return matrix_loc.reshape(matrix.shape)


def solution(mesh):
    placed = (P(None, "prow", None, "pcol"), P(), P(), P())
    return jax.shard_map(
        local, mesh=mesh, in_specs=placed, out_specs=P(None, "prow", None, "pcol"), check_vma=False
    )
```

profile of v0, /device:TPU:0, one launch (start us, length us, event | category | flops | bytes accessed | tf_op | source)
XLA Modules:
  0.0 428.3 jit_solution(5177741146964202113)
XLA Ops:
  6.5 0.8 fusion.102
  7.4 1.5 copy.17
  8.9 1.2 broadcast_select_fusion
  10.1 0.7 copy.18
  10.8 1.2 gather_fusion
  11.9 0.8 select_select_fusion.7
  12.8 0.0 all-reduce.27.cloned.1.call-update
  12.8 0.0 all-reduce.13.cloned.1.call-start
  12.9 0.1 compare_select_fusion
  13.0 41.2 %all-reduce.27.cloned.1.call-done = (bf16[256,512]{1,0:T(8,128)(2,1)}, bf16[256,512]{1,0:T(8,128)(2,1)}) async-done(((bf16[256,512]{1,0:T(8,128)(2,1)}, bf16[256,512]{1,0:T(8,128)(2,1)}), (bf16[256,512]{1,0:T(8,128)(2,1)}, bf16[256,512]{1,0:T(8,128)(2,1)})) %all-reduce.27.cloned.1.call-update) | async-done | bytes 524304 | tf_op jit(solution)/shard_map/psum | solution.py:46
  54.2 2.5 scatter_fusion
  56.7 0.1 fusion.20
  56.8 0.8 slice_select_fusion.3
  57.6 0.0 all-reduce.13.cloned.1.call-update
  57.6 0.0 all-reduce.25.cloned.1.call-start
  57.7 0.6 compare_reduce_fusion
  58.4 0.2 fusion
  58.6 53.7 %all-reduce.13.cloned.1.call-done = bf16[1024,256]{1,0:T(8,128)(2,1)} async-done(((bf16[1024,256]{1,0:T(8,128)(2,1)}), bf16[1024,256]{1,0:T(8,128)(2,1)}) %all-reduce.13.cloned.1.call-update) | async-done | bytes 524304 | tf_op jit(solution)/shard_map/psum | solution.py:9
  112.3 1.3 convolution_convert_fusion.3
  113.6 0.5 subtract_convert_fusion.3
  114.1 1.0 fusion.4
  115.1 0.8 broadcast_select_fusion.3
  115.9 1.2 gather_fusion.1
  117.1 0.8 select_select_fusion.6
  118.0 0.0 all-reduce.15.cloned.1.call-start
  118.1 37.8 %all-reduce.25.cloned.1.call-done = (bf16[256,512]{1,0:T(8,128)(2,1)}, bf16[256,512]{1,0:T(8,128)(2,1)}) async-done(((bf16[256,512]{1,0:T(8,128)(2,1)}, bf16[256,512]{1,0:T(8,128)(2,1)}), (bf16[256,512]{1,0:T(8,128)(2,1)}, bf16[256,512]{1,0:T(8,128)(2,1)})) %all-reduce.25.cloned.1.call-update) | async-done | bytes 524304 | tf_op jit(solution)/shard_map/psum | solution.py:46
  155.9 2.5 scatter_fusion.1
  158.4 0.1 fusion.19
  158.5 0.8 slice_select_fusion.2
  159.4 0.0 all-reduce.23.cloned.1.call-start
  159.4 0.2 fusion.1
  159.7 54.3 %all-reduce.15.cloned.1.call-done = bf16[1024,256]{1,0:T(8,128)(2,1)} async-done(((bf16[1024,256]{1,0:T(8,128)(2,1)}), bf16[1024,256]{1,0:T(8,128)(2,1)}) %all-reduce.15.cloned.1.call-update) | async-done | bytes 524304 | tf_op jit(solution)/shard_map/psum | solution.py:9
  214.0 1.3 convolution_convert_fusion.2
  215.3 0.5 subtract_convert_fusion.2
  215.8 1.0 fusion.5
  216.8 0.8 broadcast_select_fusion.2
  217.7 1.2 gather_fusion.2
  218.8 0.8 select_select_fusion.5
  219.7 0.0 all-reduce.17.cloned.1.call-start
  219.8 37.8 %all-reduce.23.cloned.1.call-done = (bf16[256,512]{1,0:T(8,128)(2,1)}, bf16[256,512]{1,0:T(8,128)(2,1)}) async-done(((bf16[256,512]{1,0:T(8,128)(2,1)}, bf16[256,512]{1,0:T(8,128)(2,1)}), (bf16[256,512]{1,0:T(8,128)(2,1)}, bf16[256,512]{1,0:T(8,128)(2,1)})) %all-reduce.23.cloned.1.call-update) | async-done | bytes 524304 | tf_op jit(solution)/shard_map/psum | solution.py:46
  257.6 2.5 scatter_fusion.2
  260.2 0.1 fusion.18
  260.2 0.8 slice_select_fusion.1
  261.1 0.2 all-reduce.21.cloned.1.call-start
  261.4 0.2 fusion.2
  261.6 54.1 %all-reduce.17.cloned.1.call-done = bf16[1024,256]{1,0:T(8,128)(2,1)} async-done(((bf16[1024,256]{1,0:T(8,128)(2,1)}), bf16[1024,256]{1,0:T(8,128)(2,1)}) %all-reduce.17.cloned.1.call-update) | async-done | bytes 524304 | tf_op jit(solution)/shard_map/psum | solution.py:9
  315.7 1.3 convolution_convert_fusion.1
  317.1 0.5 subtract_convert_fusion.1
  317.6 1.0 fusion.6
  318.6 0.8 broadcast_select_fusion.1
  319.4 1.2 gather_fusion.3
  320.5 0.8 select_select_fusion.4
  321.4 0.0 all-reduce.19.cloned.1.call-start
  321.5 37.9 %all-reduce.21.cloned.1.call-done = (bf16[256,512]{1,0:T(8,128)(2,1)}, bf16[256,512]{1,0:T(8,128)(2,1)}) async-done(((bf16[256,512]{1,0:T(8,128)(2,1)}, bf16[256,512]{1,0:T(8,128)(2,1)}), (bf16[256,512]{1,0:T(8,128)(2,1)}, bf16[256,512]{1,0:T(8,128)(2,1)})) %all-reduce.21.cloned.1.call-update) | async-done | bytes 524304 | tf_op jit(solution)/shard_map/psum | solution.py:46
  359.4 2.5 scatter_fusion.3
  361.9 0.1 fusion.17
  362.0 0.8 slice_select_fusion
  362.8 0.2 fusion.3
  363.1 54.4 %all-reduce.19.cloned.1.call-done = bf16[1024,256]{1,0:T(8,128)(2,1)} async-done(((bf16[1024,256]{1,0:T(8,128)(2,1)}), bf16[1024,256]{1,0:T(8,128)(2,1)}) %all-reduce.19.cloned.1.call-update) | async-done | bytes 524304 | tf_op jit(solution)/shard_map/psum | solution.py:9
  417.5 1.3 convolution_convert_fusion
  418.8 0.5 subtract_convert_fusion
  419.3 1.0 fusion.7
  420.3 0.1 fusion.16
  420.4 1.1 reshape.1224
  (41 shorter events, 0.4 us)
Async XLA Ops:
  6.5 47.6 %all-reduce.27.cloned.1.call-start = ((), (), s32[]{:S(2)}) async-start(), calls=%async_computation.7 | async-start | bytes 1048576 | tf_op jit(solution)/shard_map/psum | solution.py:46
  11.9 1.0 copy-start.6
  12.8 99.5 %all-reduce.13.cloned.1.call-start = ((), (), s32[]{:S(2)}) async-start(), calls=%async_computation | async-start | bytes 1048576 | tf_op jit(solution)/shard_map/psum | solution.py:9
  54.2 2.5 copy-start
  56.7 1.7 copy-start.4
  56.8 55.5 %copy-start.5 = (bf16[4,256,256]{2,1,0:T(8,128)(2,1)S(1)}, bf16[4,256,256]{2,1,0:T(8,128)(2,1)}, u32[]{:S(2)}) copy-start(bf16[4,256,256]{2,1,0:T(8,128)(2,1)} %param.33) | copy-start | bytes 1572868
  57.6 98.3 %all-reduce.25.cloned.1.call-start = ((), (), s32[]{:S(2)}) async-start(), calls=%async_computation.6 | async-start | bytes 1048576 | tf_op jit(solution)/shard_map/psum | solution.py:46
  118.0 96.1 %all-reduce.15.cloned.1.call-start = ((), (), s32[]{:S(2)}) async-start(), calls=%async_computation.1 | async-start | bytes 1048576 | tf_op jit(solution)/shard_map/psum | solution.py:9
  155.9 2.5 copy-start.1
  159.4 98.3 %all-reduce.23.cloned.1.call-start = ((), (), s32[]{:S(2)}) async-start(), calls=%async_computation.5 | async-start | bytes 1048576 | tf_op jit(solution)/shard_map/psum | solution.py:46
  219.7 96.0 %all-reduce.17.cloned.1.call-start = ((), (), s32[]{:S(2)}) async-start(), calls=%async_computation.2 | async-start | bytes 1048576 | tf_op jit(solution)/shard_map/psum | solution.py:9
  257.6 2.5 copy-start.2
  261.1 98.3 %all-reduce.21.cloned.1.call-start = ((), (), s32[]{:S(2)}) async-start(), calls=%async_computation.4 | async-start | bytes 1048576 | tf_op jit(solution)/shard_map/psum | solution.py:46
  321.4 96.1 %all-reduce.19.cloned.1.call-start = ((), (), s32[]{:S(2)}) async-start(), calls=%async_computation.3 | async-start | bytes 1048576 | tf_op jit(solution)/shard_map/psum | solution.py:9
  359.4 2.5 copy-start.3
Sparse Core Ops, SparseCore 0:
  12.9 41.1 all-reduce.26
  57.8 54.4 all-reduce.12
  118.1 37.7 all-reduce.24
  159.5 54.4 all-reduce.14
  219.8 37.7 all-reduce.22
  261.2 54.4 all-reduce.16
  321.5 37.8 all-reduce.20
  363.0 54.4 all-reduce.18
where the time goes:
time: 429 us; the launch traced here: 428 us
  waiting for transfers between devices  371 us (86%)
  local copies, waits for them, and re-layouts  18.8 us (4%)
  other arithmetic  15.7 us (4%)
  between operations  13.9 us (3%)
  matrix products  8.15 us (2%)
    psum x4, waiting for transfers between devices, spread(): return lax.psum(kept, axis)  217 us
    psum x4, waiting for transfers between devices, local(): lax.psum(own_diag, 'prow').astype(jnp.float32)  155 us
    scatter x4, local copies, waits for them, and re-layouts, local(): matrix_loc.at[jnp.where(moved_rows, chosen_local, local_rows)]  9.99 us
  transfers between devices with their start and end apart: 8, of which 8 were waited for; matrix products, arithmetic and copies ran while one was open for 0% of the time, Pallas kernels for 0%

commit v1 on v0

--- a/solution.py
+++ b/solution.py
@@ -1,7 +1,18 @@
+import functools
+
 import jax
 import jax.numpy as jnp
 from jax import lax
+from jax.experimental import pallas as pl
+from jax.experimental.pallas import tpu as pltpu
 from jax.sharding import PartitionSpec as P
+
+BF16 = jnp.bfloat16
+F32 = jnp.float32
+I32 = jnp.int32
+VMEM_BYTES = 44 * 1024 * 1024
+MOVE_ROWS = 96
+MOVE_SLOTS = 128
 
 
 def spread(value, axis, source):
@@ -9,7 +20,7 @@
     return lax.psum(kept, axis)
 
 
-def local(matrix, pivots, lower_inverse, upper_inverse):
+def stepwise(matrix, pivots, lower_inverse, upper_inverse):
     row_blocks = matrix.shape[0]
     block_size = matrix.shape[1]
     col_blocks = matrix.shape[2]
@@ -41,12 +52,7 @@
         picked = jnp.where(is_mine[:, None], picked, jnp.zeros_like(picked))
         diag_rows = matrix_loc[diag_local : diag_local + block_size]
         own_diag = jnp.where(my_row == diag_root, diag_rows, jnp.zeros_like(diag_rows))
-        summed_rows, summed_diag = (
-            lax.psum(picked, "prow").astype(jnp.float32),
-            lax.psum(own_diag, "prow").astype(jnp.float32),
-        )
-        new_rows = summed_rows.astype(jnp.bfloat16)
-        old_diag = summed_diag.astype(jnp.bfloat16)
+        new_rows, old_diag = lax.psum(picked, "prow"), lax.psum(own_diag, "prow")
         moved_rows = is_mine & (chosen != targets)
         matrix_loc = matrix_loc.at[jnp.where(moved_rows, chosen_local, local_rows)].set(
             old_diag, mode="drop"
@@ -80,6 +86,347 @@
     return matrix_loc.reshape(matrix.shape)
 
 
+def iota(shape, dim):
+    return lax.broadcasted_iota(I32, shape, dim)
+
+
+def dot(a, b):
+    return jnp.dot(a, b, preferred_element_type=F32)
+
+
+def one_hot(hit):
+    return jnp.where(hit, 1.0, 0.0).astype(BF16)
+
+
+def to_col(row, size):
+    eye = iota((size, size), 0) == iota((size, size), 1)
+    return jnp.sum(jnp.where(eye, jnp.broadcast_to(row, (size, size)), 0), axis=1, keepdims=True)
+
+
+def find(col, base, x, size):
+    hit = col == x
+    place = jnp.sum(jnp.where(hit, iota((size, size), 0) + (base + 1), 0), axis=0, keepdims=True)
+    return jnp.where(place > 0, place - 1, x)
+
+
+def look(col, base, x, size):
+    hit = iota((size, size), 0) + base == x
+    return jnp.sum(jnp.where(hit, col, 0), axis=0, keepdims=True)
+
+
+def before(rows, size):
+    tri = one_hot(iota((size, size), 0) < iota((size, size), 1))
+    stacked = jnp.concatenate([one_hot(r) for r in rows], axis=0)
+    counts = dot(stacked, tri)
+    k = rows[0].shape[0]
+    return [counts[i * k : (i + 1) * k] for i in range(len(rows))]
+
+
+def pick_kernel(cfg, piv_ref, m0_ref, m1_ref, meta_ref, pack0_ref, pack1_ref):
+    nb, steps, n_row, cap, local_rows = cfg
+    my_row = lax.axis_index("prow")
+    piv = [piv_ref[t : t + 1, :] for t in range(steps)]
+    cols = [to_col(piv[t], nb) for t in range(steps - 1)]
+    owners, places = [], []
+    for t in range(steps):
+        x = piv[t]
+        for s in range(t - 1, -1, -1):
+            x = find(cols[s], s * nb, x, nb)
+        block = x // nb
+        owners.append(block % n_row)
+        places.append(block // n_row * nb + x % nb)
+    lanes = -(-n_row // 8) * 8
+    member = [iota((lanes, nb), 0) == w for w in owners]
+    counts = before(member, nb)
+    base = jnp.zeros((lanes, 1), F32)
+    ranks = []
+    for t in range(steps):
+        ranks.append(
+            jnp.sum(jnp.where(member[t], counts[t] + base, 0.0), axis=0, keepdims=True).astype(I32)
+        )
+        base = base + jnp.sum(jnp.where(member[t], 1.0, 0.0), axis=1, keepdims=True)
+    for t in range(steps):
+        meta_ref[t : t + 1, :] = owners[t] * cap + ranks[t]
+    over = jnp.max(base, axis=0, keepdims=True).astype(I32)
+    meta_ref[steps : steps + 1, :] = jnp.broadcast_to(over, (1, nb))
+    slot = iota((cap, nb), 0)
+    total = jnp.zeros((cap, nb), I32)
+    for t in range(steps):
+        key = jnp.where(owners[t] == my_row, ranks[t], -1)
+        total = total + jnp.where(slot == key, places[t] + 1, 0)
+    source = jnp.sum(total, axis=1, keepdims=True) - 1
+    chosen = one_hot(source == iota((cap, local_rows), 1))
+    pack0_ref[...] = dot(chosen, m0_ref[...]).astype(BF16)
+    pack1_ref[...] = dot(chosen, m1_ref[...]).astype(BF16)
+
+
+def move_kernel(cfg, piv_ref, meta_ref, move_ref):
+    nb, steps, n_row, cap = cfg
+    piv = [piv_ref[t : t + 1, :] for t in range(steps)]
+    cols = [to_col(piv[t], nb) for t in range(steps)]
+    lanes = -(-n_row // 8) * 8
+    dests, member = [], []
+    for t in range(steps):
+        at = iota((1, nb), 1) + t * nb
+        x = at
+        for s in range(t):
+            x = find(cols[s], s * nb, x, nb)
+        x = jnp.where(x == at, piv[t], x)
+        for s in range(t + 1, steps):
+            inside = (x >= s * nb) & (x < (s + 1) * nb)
+            x = jnp.where(inside, look(cols[s], s * nb, x, nb), find(cols[s], s * nb, x, nb))
+        block = x // nb
+        dest = jnp.where(x >= steps * nb, block % n_row, -1)
+        move_ref[t : t + 1, :] = dest
+        move_ref[2 * steps + t : 2 * steps + t + 1, :] = block // n_row * nb + x % nb
+        member.append(iota((lanes, nb), 0) == dest)
+    counts = before(member, nb)
+    most = jnp.zeros((lanes, 1), F32)
+    for t in range(steps):
+        move_ref[steps + t : steps + t + 1, :] = jnp.sum(
+            jnp.where(member[t], counts[t], 0.0), axis=0, keepdims=True
+        ).astype(I32)
+        most = jnp.maximum(most, jnp.sum(jnp.where(member[t], 1.0, 0.0), axis=1, keepdims=True))
+    over = jnp.max(most, axis=0, keepdims=True).astype(I32)
+    bad = (over > MOVE_ROWS) | (meta_ref[steps : steps + 1, :] > cap)
+    move_ref[3 * steps : 3 * steps + 1, :] = jnp.where(bad, 1, 0)
+
+
+def order_rows(meta_ref, buf_ref, t, nb):
+    pos = to_col(meta_ref[t : t + 1, :], nb)
+    hot = one_hot(pos == iota((nb, buf_ref.shape[0]), 1))
+    return dot(hot, buf_ref[...]).astype(BF16)
+
+
+def order_kernel(cfg, meta_ref, buf_ref, top_ref, off_ref):
+    nb, steps = cfg
+    my_col = lax.axis_index("pcol")
+    for t in range(steps):
+        top_ref[t * nb : (t + 1) * nb, :] = order_rows(meta_ref, buf_ref, t, nb)
+    for j in range(steps - 1):
+        block = jnp.where(my_col <= j, j + 1, j)
+        rows = pl.ds(pl.multiple_of(block * nb, nb), nb)
+        off_ref[j * nb : (j + 1) * nb, :] = top_ref[rows, :]
+
+
+def factor_kernel(
+    cfg, meta_ref, move_ref, top0_ref, buf1_ref, m0_ref, m1_ref, raw_a, raw_b, off_a, off_b,
+    linv_ref, uinv_ref, res_ref, top_ref, send_ref, raw, off, l_own, l_top, u_top, upper, first,
+    diag, sems,
+):
+    nb, steps, n_row, local_rows = cfg
+    my_row = lax.axis_index("prow")
+    my_col = lax.axis_index("pcol")
+    low = my_col & 3
+    copies = []
+    for i, (src, at, mask) in enumerate(
+        [(off_a, 0, 0), (off_a, 1, 2), (off_b, 0, 1), (off_b, 1, 3)]
+    ):
+        copies.append(pltpu.make_async_copy(src.at[at], off.at[low ^ mask], sems.at[i]))
+    for i, (src, at, mask) in enumerate(
+        [(raw_a, 0, 0), (raw_a, 1, 2), (raw_b, 0, 1), (raw_b, 1, 3)]
+    ):
+        copies.append(pltpu.make_async_copy(src.at[at], raw.at[low ^ mask], sems.at[4 + i]))
+    for c in copies:
+        c.start()
+    wide = steps * nb
+    for t in range(steps):
+        first[t * nb : (t + 1) * nb, :nb] = top0_ref[t * nb : (t + 1) * nb, :]
+        first[t * nb : (t + 1) * nb, nb:] = order_rows(meta_ref, buf1_ref, t, nb)
+    for c in copies:
+        c.wait()
+    for t in range(steps):
+        here = slice(t * nb, (t + 1) * nb)
+        done = slice(0, t * nb)
+        for s in range(t):
+            sel = slice(s * nb, (s + 1) * nb)
+            acc = off[t, sel, :].astype(F32)
+            if s > 0:
+                acc = acc - dot(l_top[sel, : s * nb], u_top[: s * nb, here])
+            u_top[sel, here] = dot(linv_ref[s], acc.astype(BF16)).astype(BF16)
+        if t < steps - 1:
+            acc = off[t, t * nb :, :].astype(F32)
+            if t > 0:
+                acc = acc - dot(l_top[(t + 1) * nb :, done], u_top[done, here])
+            l_top[(t + 1) * nb :, here] = dot(acc.astype(BF16), uinv_ref[t]).astype(BF16)
+        for k in range(local_rows // nb):
+            rows = slice(k * nb, (k + 1) * nb)
+            acc = raw[t, rows, :].astype(F32)
+            if t > 0:
+                acc = acc - dot(l_own[rows, done], u_top[done, here])
+            l_own[rows, here] = dot(acc.astype(BF16), uinv_ref[t]).astype(BF16)
+        acc = first[here, :].astype(F32)
+        if t > 0:
+            acc = acc - dot(l_top[here, done], upper[done, :])
+        acc = acc.astype(BF16)
+        diag[here, :] = acc[:, :nb]
+        upper[here, :] = dot(linv_ref[t], acc).astype(BF16)
+    in_panel = my_col < steps
+    panel = pl.ds(pl.multiple_of(jnp.minimum(my_col, steps - 1) * nb, nb), nb)
+    for k in range(local_rows // nb):
+        rows = slice(k * nb, (k + 1) * nb)
+        prod = dot(l_own[rows, :], upper[...])
+        left = (m0_ref[rows, :].astype(F32) - prod[:, :nb]).astype(BF16)
+        res_ref[rows, :nb] = jnp.where(in_panel, l_own[rows, panel], left)
+        res_ref[rows, nb:] = (m1_ref[rows, :].astype(F32) - prod[:, nb:]).astype(BF16)
+    block = pl.ds(pl.multiple_of(jnp.minimum(my_row, steps - 1) * nb, nb), nb)
+    own_upper = upper[block, :]
+    left = jnp.where(my_col == my_row, diag[block, :], own_upper[:, :nb])
+    left = jnp.where(in_panel & (my_col < my_row), l_top[block, panel], left)
+    top_ref[:, :nb] = left
+    top_ref[:, nb:] = own_upper[:, nb:]
+    here = iota((steps, nb), 0) == my_row
+    dest = jnp.sum(jnp.where(here, move_ref[:steps, :] + 1, 0), axis=0, keepdims=True) - 1
+    rank = jnp.sum(jnp.where(here, move_ref[steps : 2 * steps, :], 0), axis=0, keepdims=True)
+    for k in range(n_row):
+        key = jnp.where(dest == lax.rem(my_row + k, n_row), rank, -1)
+        hot = one_hot(key == iota((MOVE_ROWS, nb), 0))
+        send_ref[k] = dot(hot, res_ref[:nb, :]).astype(BF16)
+
+
+def place_kernel(cfg, move_ref, res_ref, top_ref, *refs):
+    nb, steps, n_row, local_rows = cfg
+    recv, out_ref, slots = refs[:n_row], refs[n_row], refs[n_row + 1]
+    my_row = lax.axis_index("prow")
+    slots[...] = jnp.zeros_like(slots)
+    targets = []
+    for k in range(n_row):
+        slots[k * MOVE_SLOTS : k * MOVE_SLOTS + MOVE_ROWS, :] = recv[k][...]
+        source = lax.rem(my_row + n_row - k, n_row)
+        here = iota((steps, nb), 0) == source
+        dest = jnp.sum(jnp.where(here, move_ref[:steps, :] + 1, 0), axis=0, keepdims=True) - 1
+        rank = jnp.sum(jnp.where(here, move_ref[steps : 2 * steps, :], 0), axis=0, keepdims=True)
+        place = jnp.sum(
+            jnp.where(here, move_ref[2 * steps : 3 * steps, :], 0), axis=0, keepdims=True
+        )
+        key = jnp.where(dest == my_row, rank, -1)
+        hot = one_hot(key == iota((MOVE_SLOTS, nb), 0))
+        row = iota((8, nb), 0)
+        parts = jnp.where(row == 0, place // 128, jnp.where(row == 1, place % 128, 1))
+        found = lax.dot_general(
+            parts.astype(F32).astype(BF16), hot, (((1,), (1,)), ((), ())),
+            preferred_element_type=F32,
+        )
+        at = found[0:1] * 128.0 + found[1:2]
+        targets.append(jnp.where(found[2:3] > 0.5, at, -1.0).astype(I32))
+    target = jnp.concatenate(targets, axis=1)
+    for k in range(local_rows // nb):
+        rows = slice(k * nb, (k + 1) * nb)
+        hit = iota((nb, n_row * MOVE_SLOTS), 0) + k * nb == target
+        moved = dot(one_hot(hit), slots[...]).astype(BF16)
+        any_hit = jnp.sum(jnp.where(hit, 1.0, 0.0), axis=1, keepdims=True) > 0.5
+        value = jnp.where(any_hit, moved, res_ref[rows, :])
+        if k == 0:
+            value = jnp.where(my_row < steps, top_ref[...], value)
+        out_ref[rows, :] = value
+
+
+def call(kernel, outs, ins, scratch=(), any_at=()):
+    vmem = pl.BlockSpec(memory_space=pltpu.VMEM)
+    anywhere = pl.BlockSpec(memory_space=pl.ANY)
+    return pl.pallas_call(
+        kernel,
+        out_shape=outs,
+        in_specs=[anywhere if i in any_at else vmem for i in range(len(ins))],
+        out_specs=jax.tree.map(lambda _: vmem, outs),
+        scratch_shapes=list(scratch),
+        compiler_params=pltpu.CompilerParams(vmem_limit_bytes=VMEM_BYTES),
+    )(*ins)
+
+
+def shape(*dims, dtype=BF16):
+    return jax.ShapeDtypeStruct(dims, dtype)
+
+
+def local(matrix, pivots, lower_inverse, upper_inverse):
+    row_blocks, nb, col_blocks, _ = matrix.shape
+    steps = pivots.shape[0]
+    n_row = lax.axis_size("prow")
+    n_col = lax.axis_size("pcol")
+    if steps != 4 or col_blocks != 2 or n_row < steps or n_col < 8 or n_col % 4:
+        return stepwise(matrix, pivots, lower_inverse, upper_inverse)
+    my_col = lax.axis_index("pcol")
+    local_rows = row_blocks * nb
+    cap = -(-(steps * nb // n_row + 64) // 16) * 16
+    m0 = matrix[:, :, 0, :].reshape(local_rows, nb)
+    m1 = matrix[:, :, 1, :].reshape(local_rows, nb)
+
+    def from_panels(value, mask):
+        return lax.ppermute(value, "pcol", [(i, i ^ mask) for i in range(steps)])
+
+    def swap_cores(value):
+        return lax.ppermute(value, "pcol", [(i, i ^ 1) for i in range(n_col)])
+
+    on_panel = my_col < steps
+    fours = range(4, n_col, 4)
+    raw_x = from_panels(m0, 2)
+    raw_far = functools.reduce(jnp.add, [from_panels(m0, mask) for mask in fours])
+
+    meta, pack0, pack1 = call(
+        functools.partial(pick_kernel, (nb, steps, n_row, cap, local_rows)),
+        (shape(8, nb, dtype=I32), shape(cap, nb), shape(cap, nb)),
+        (pivots, m0, m1),
+    )
+    buf0 = lax.all_gather(pack0, "prow", tiled=True)
+    top0, off = call(
+        functools.partial(order_kernel, (nb, steps)),
+        (shape(steps * nb, nb), shape((steps - 1) * nb, nb)),
+        (meta, buf0),
+    )
+    raw_far_x = lax.ppermute(raw_far, "pcol", [(i, i ^ 2) for i in range(steps, n_col)])
+    off_x = from_panels(off, 2)
+    off_far = functools.reduce(jnp.add, [from_panels(off, mask) for mask in fours])
+    off_far_x = functools.reduce(jnp.add, [from_panels(off, mask + 2) for mask in fours])
+    pack1, _ = lax.optimization_barrier((pack1, off))
+    buf1 = lax.all_gather(pack1, "prow", tiled=True)
+    move = call(
+        functools.partial(move_kernel, (nb, steps, n_row, cap)),
+        shape(16, nb, dtype=I32),
+        (pivots, meta),
+    )
+    raw_a = jnp.stack([jnp.where(on_panel, m0, raw_far), jnp.where(on_panel, raw_x, raw_far_x)])
+    raw_b = swap_cores(raw_a)
+    off_a = jnp.stack([jnp.where(on_panel, off, off_far), jnp.where(on_panel, off_x, off_far_x)])
+    off_b = swap_cores(off_a)
+    top_rows = steps * nb
+    res, top, send = call(
+        functools.partial(factor_kernel, (nb, steps, n_row, local_rows)),
+        (shape(local_rows, 2 * nb), shape(nb, 2 * nb), shape(n_row, MOVE_ROWS, 2 * nb)),
+        (meta, move, top0, buf1, m0, m1, raw_a, raw_b, off_a, off_b, lower_inverse, upper_inverse),
+        scratch=(
+            pltpu.VMEM((steps, local_rows, nb), BF16),
+            pltpu.VMEM((steps, top_rows - nb, nb), BF16),
+            pltpu.VMEM((local_rows, top_rows), BF16),
+            pltpu.VMEM((top_rows, top_rows), BF16),
+            pltpu.VMEM((top_rows, top_rows), BF16),
+            pltpu.VMEM((top_rows, 2 * nb), BF16),
+            pltpu.VMEM((top_rows, 2 * nb), BF16),
+            pltpu.VMEM((top_rows, nb), BF16),
+            pltpu.SemaphoreType.DMA((8,)),
+        ),
+        any_at=(6, 7, 8, 9),
+    )
+    recv = [send[0]] + [
+        lax.ppermute(send[k], "prow", [(i, (i + k) % n_row) for i in range(n_row)])
+        for k in range(1, n_row)
+    ]
+
+    def finish():
+        out = call(
+            functools.partial(place_kernel, (nb, steps, n_row, local_rows)),
+            shape(local_rows, 2 * nb),
+            (move, res, top, *recv),
+            scratch=(pltpu.VMEM((n_row * MOVE_SLOTS, 2 * nb), BF16),),
+        )
+        return out.reshape(matrix.shape)
+
+    return lax.cond(
+        move[3 * steps, 0] > 0,
+        lambda: stepwise(matrix, pivots, lower_inverse, upper_inverse),
+        finish,
+    )
+
+
 def solution(mesh):
     placed = (P(None, "prow", None, "pcol"), P(), P(), P())
     return jax.shard_map(

time: 429 us -> 116 us (0.27)
  waiting for transfers between devices: 371 us -> 25 us
  blocking collectives: 0 us -> 35.3 us
  starting transfers between devices: 0.48 us -> 19.3 us
  Pallas kernels: 0 us -> 14.7 us
  other arithmetic: 15.7 us -> 1.44 us
  local copies, waits for them, and re-layouts: 18.8 us -> 5.3 us
  matrix products: 8.15 us -> 0 us
    psum x8 -> x0, waiting for transfers between devices: 371 us -> none  [the longest x4 217 us: spread(): return lax.psum(kept, axis)]
    all_gather x0 -> x2, blocking collectives: none -> 35.3 us  [the longest x1 18.1 us: local(): buf0 = lax.all_gather(pack0, 'prow', tiled=True)]
    ppermute x0 -> x11, waiting for transfers between devices: none -> 25 us  [the longest x5 18.9 us: from_panels(): return lax.ppermute(value, 'pcol', [(i, i ^ mask) for i in range(steps)])]
    ppermute x0 -> x11, starting transfers between devices: none -> 19.3 us  [the longest x5 14.9 us: from_panels(): return lax.ppermute(value, 'pcol', [(i, i ^ mask) for i in range(steps)])]
    pallas_call x0 -> x5, Pallas kernels: none -> 14.7 us  [call(): pl.pallas_call(kernel, out_shape=outs, in_specs=[anywhere if i in any_at...]
    select_n x13 -> x0, other arithmetic: 10.4 us -> none  [the longest x4 3.63 us: local(): jnp.where(my_row == diag_root, diag_rows, jnp.zeros_like(diag_rows))]
    scatter x4 -> x0, local copies, waits for them, and re-layouts: 9.99 us -> none  [local(): matrix_loc.at[jnp.where(moved_rows, chosen_local, local_rows)]]
    dot_general x12 -> x0, matrix products: 8.15 us -> none  [the longest x4 5.3 us: local(): jnp.dot(received, upper_inverse[step_num], preferred_element_type=jnp.flo...]
  transfers between devices with their start and end apart: 8 -> 11, of which waited for: 8 -> 6; matrix products, arithmetic and copies ran while one was open for 0% -> 2% of each run, Pallas kernels for 0% -> 3%
where the time goes in v1:
time: 116 us; the launch traced here: 115 us
  blocking collectives  35.3 us (30%)
  waiting for transfers between devices  25 us (22%)
  starting transfers between devices  19.3 us (17%)
  Pallas kernels  14.7 us (13%)
  between operations  14.2 us (12%)
  local copies, waits for them, and re-layouts  5.3 us (5%)
  other arithmetic  1.44 us (1%)
    ppermute x5, waiting for transfers between devices, from_panels(): return lax.ppermute(value, 'pcol', [(i, i ^ mask) for i in range(steps)])  18.9 us
    all_gather x1, blocking collectives, local(): buf0 = lax.all_gather(pack0, 'prow', tiled=True)  18.1 us
    all_gather x1, blocking collectives, local(): buf1 = lax.all_gather(pack1, 'prow', tiled=True)  17.2 us
    ppermute x5, starting transfers between devices, from_panels(): return lax.ppermute(value, 'pcol', [(i, i ^ mask) for i in range(steps)])  14.9 us
    pallas_call x5, Pallas kernels, call(): pl.pallas_call(kernel, out_shape=outs, in_specs=[anywhere if i in any_at...  14.7 us
    ppermute x3, waiting for transfers between devices, local(): lax.ppermute(send[k], 'prow', [(i, (i + k) % n_row) for i in range(n_row)])  6.1 us
    slice x1, local copies, waits for them, and re-layouts, local(): m1 = matrix[:, :, 1, :].reshape(local_rows, nb)  3.3 us
    ppermute x3, starting transfers between devices, local(): lax.ppermute(send[k], 'prow', [(i, (i + k) % n_row) for i in range(n_row)])  2.86 us
  transfers between devices with their start and end apart: 11, of which 6 were waited for; matrix products, arithmetic and copies ran while one was open for 2% of the time, Pallas kernels for 3%

profile of v1, /device:TPU:0, one launch (start us, length us, event | category | flops | bytes accessed | tf_op | source)
XLA Modules:
  0.0 115.3 jit_solution(5711078532187683367)
XLA Ops:
  6.5 3.3 %fusion.103 = (bf16[4,256,1,256]{3,2,1,0:T(2,128)(2,1)S(1)}, bf16[4,256,1,256]{3,2,1,0:T(2,128)(2,1)S(1)}) fusion(bf16[4,256,2,256]{3,2,1,0:T(2,128)(2,1)} %param.32), kind=kLoop, calls=%fused_computation.298 | loop fusion | bytes 2097152 | tf_op jit(solution)/shard_map/slice | solution.py:352
  9.8 0.1 copy.21
  9.9 0.0 copy-start.6
  10.0 4.9 %collective-permute-start = (bf16[1024,256]{1,0:T(8,128)(2,1)S(1)}, bf16[1024,256]{1,0:T(8,128)(2,1)S(1)}, u32[]{:S(2)}, u32[]{:S(2)}) collective-permute-start(bf16[1024,256]{1,0:T(8,128)(2,1)S(1)} %bitcast.138), channel_id=1, source_target_pairs={{0,4},{1,5},{2,6},{3,7},{8,12},{9,13},{10,14},{11,15},{16,20},{17,... | collective-permute-start | bytes 1572872 | tf_op jit(solution)/shard_map/ppermute | solution.py:355
  14.9 0.1 copy.22
  15.0 0.0 copy-done.6
  15.0 1.2 %shard_map.48 = (s32[8,256]{1,0:T(8,128)S(1)}, bf16[320,256]{1,0:T(8,128)(2,1)S(1)}, bf16[320,256]{1,0:T(8,128)(2,1)S(1)}) custom-call(s32[4,256]{1,0:T(4,128)S(1)} %copy-done.6, bf16[1024,256]{1,0:T(8,128)(2,1)S(1)} %bitcast.139, bf16[1024,256]{1,0:T(8,128)(2,1)S(1)} %bitcast.142), custom_call_target="tpu_custom_call" | custom-call | tf_op jit(solution)/shard_map/pallas_call | solution.py:327
  16.2 18.1 %all_gather.6.buf_ref = bf16[1280,256]{1,0:T(8,128)(2,1)S(1)} all-gather(bf16[320,256]{1,0:T(8,128)(2,1)S(1)} %get-tuple-element.198), channel_id=1, replica_groups=mesh['prow'=4,'pcol'=8] {'prow'}, dimensions={0}, use_global_device_ids=true | all-gather | bytes 819200 | tf_op jit(solution)/shard_map/all_gather | solution.py:370
  34.3 1.1 shard_map.50
  35.3 2.1 %collective-permute-start.4 = (bf16[768,256]{1,0:T(8,128)(2,1)S(1)}, bf16[768,256]{1,0:T(8,128)(2,1)}, u32[]{:S(2)}, u32[]{:S(2)}) collective-permute-start(bf16[768,256]{1,0:T(8,128)(2,1)S(1)} %get-tuple-element.201), channel_id=1, source_target_pairs={{0,4},{1,5},{2,6},{3,7},{8,12},{9,13},{10,14},{11,15},{16,20},{17,... | collective-permute-start | bytes 1179656 | tf_op jit(solution)/shard_map/ppermute | solution.py:355
  37.4 3.4 %collective-permute-start.1 = (bf16[1024,256]{1,0:T(8,128)(2,1)S(1)}, bf16[1024,256]{1,0:T(8,128)(2,1)S(1)}, u32[]{:S(2)}, u32[]{:S(2)}) collective-permute-start(bf16[1024,256]{1,0:T(8,128)(2,1)S(1)} %bitcast.140), channel_id=1, source_target_pairs={{0,2},{1,3},{2,0},{3,1},{8,10},{9,11},{10,8},{11,9},{16,18},{17,19... | collective-permute-start | bytes 1572872 | tf_op jit(solution)/shard_map/ppermute | solution.py:355
  40.8 0.0 collective-permute-done
  40.8 1.5 %collective-permute-start.2 = (bf16[1024,256]{1,0:T(8,128)(2,1)S(1)}, bf16[1024,256]{1,0:T(8,128)(2,1)}, u32[]{:S(2)}, u32[]{:S(2)}) collective-permute-start(bf16[1024,256]{1,0:T(8,128)(2,1)S(1)} %collective-permute-done), channel_id=1, source_target_pairs={{4,6},{5,7},{6,4},{7,5},{12,14},{13,15},{14,12},{15,13},{20,22},{2... | collective-permute-start | bytes 1572872 | tf_op jit(solution)/shard_map/ppermute | solution.py:376
  42.3 2.4 %collective-permute-start.5 = (bf16[768,256]{1,0:T(8,128)(2,1)S(1)}, bf16[768,256]{1,0:T(8,128)(2,1)}, u32[]{:S(2)}, u32[]{:S(2)}) collective-permute-start(bf16[768,256]{1,0:T(8,128)(2,1)S(1)} %get-tuple-element.201), channel_id=1, source_target_pairs={{0,2},{1,3},{2,0},{3,1},{8,10},{9,11},{10,8},{11,9},{16,18},{17,19... | collective-permute-start | bytes 1179656 | tf_op jit(solution)/shard_map/ppermute | solution.py:355
  44.7 2.0 %collective-permute-start.6 = (bf16[768,256]{1,0:T(8,128)(2,1)S(1)}, bf16[768,256]{1,0:T(8,128)(2,1)}, u32[]{:S(2)}, u32[]{:S(2)}) collective-permute-start(bf16[768,256]{1,0:T(8,128)(2,1)S(1)} %get-tuple-element.201), channel_id=1, source_target_pairs={{0,6},{1,7},{2,4},{3,5},{8,14},{9,15},{10,12},{11,13},{16,22},{17,... | collective-permute-start | bytes 1179656 | tf_op jit(solution)/shard_map/ppermute | solution.py:355
  46.8 0.0 collective-permute-done.4
  46.8 0.1 select_bitcast_fusion.3
  46.9 0.1 select_bitcast_fusion.1
  47.0 7.2 %collective-permute-done.1 = bf16[1024,256]{1,0:T(8,128)(2,1)S(1)} collective-permute-done((bf16[1024,256]{1,0:T(8,128)(2,1)S(1)}, bf16[1024,256]{1,0:T(8,128)(2,1)S(1)}, u32[]{:S(2)}, u32[]{:S(2)}) %collective-permute-start.1) | collective-permute-done | bytes 524320 | tf_op jit(solution)/shard_map/ppermute | solution.py:355
  54.2 0.0 collective-permute-done.2
  54.2 0.1 select_bitcast_fusion
  54.3 0.1 pad_maximum_fusion.raw_a
  54.4 0.1 collective-permute-start.3
  54.5 8.3 %collective-permute-done.5 = bf16[768,256]{1,0:T(8,128)(2,1)} collective-permute-done((bf16[768,256]{1,0:T(8,128)(2,1)S(1)}, bf16[768,256]{1,0:T(8,128)(2,1)}, u32[]{:S(2)}, u32[]{:S(2)}) %collective-permute-start.5) | collective-permute-done | bytes 393248 | tf_op jit(solution)/shard_map/ppermute | solution.py:355
  62.7 3.4 %collective-permute-done.6 = bf16[768,256]{1,0:T(8,128)(2,1)} collective-permute-done((bf16[768,256]{1,0:T(8,128)(2,1)S(1)}, bf16[768,256]{1,0:T(8,128)(2,1)}, u32[]{:S(2)}, u32[]{:S(2)}) %collective-permute-start.6) | collective-permute-done | bytes 393248 | tf_op jit(solution)/shard_map/ppermute | solution.py:355
  66.1 1.0 select_bitcast_fusion.2
  67.2 0.1 pad_maximum_fusion.1.off_a
  67.3 0.1 collective-permute-start.7
  67.3 1.0 shard_map.49.move_ref
  68.4 17.2 %all_gather.7.buf1_ref = bf16[1280,256]{1,0:T(8,128)(2,1)S(1)} all-gather(bf16[320,256]{1,0:T(8,128)(2,1)S(1)} %get-tuple-element.202), channel_id=1, replica_groups=mesh['prow'=4,'pcol'=8] {'prow'}, dimensions={0}, use_global_device_ids=true | all-gather | bytes 819200 | tf_op jit(solution)/shard_map/all_gather | solution.py:381
  85.6 0.0 collective-permute-done.7.off_b
  85.6 0.0 collective-permute-done.3.raw_b
  85.6 0.0 copy-start
  85.6 0.0 copy-start.7
  85.6 10.4 %shard_map.51 = (bf16[1024,512]{1,0:T(8,128)(2,1)S(1)}, bf16[256,512]{1,0:T(8,128)(2,1)S(1)}, bf16[4,96,512]{2,1,0:T(8,128)(2,1)S(1)}) custom-call(s32[8,256]{1,0:T(8,128)S(1)} %get-tuple-element.197.meta_ref, s32[16,256]{1,0:T(8,128)S(1)} %shard_map.49.move_ref, bf16[1024,256]{1,0:T(8,128)(2,1)S(1)} %get-tuple-element.199.top0_ref, ...), custom_call_target="tpu_custom_call" | custom-call | tf_op jit(solution)/shard_map/pallas_call | solution.py:327
  96.1 1.8 %collective-permute-start.10 = (bf16[96,512]{1,0:T(8,128)(2,1)S(1)}, bf16[96,512]{1,0:T(8,128)(2,1)S(1)}, u32[]{:S(2)}, u32[]{:S(2)}) collective-permute-start(bf16[96,512]{1,0:T(8,128)(2,1)S(1)} %get-tuple-element.253), channel_id=1, source_target_pairs={{0,24},{8,0},{16,8},{24,16},{1,25},{9,1},{17,9},{25,17},{2,26},{10... | collective-permute-start | bytes 294920 | tf_op jit(solution)/shard_map/ppermute | solution.py:410
  97.8 0.3 collective-permute-start.8
  98.2 0.8 collective-permute-start.9
  98.9 0.5 slice.347
  100.1 2.4 %collective-permute-done.10 = bf16[96,512]{1,0:T(8,128)(2,1)S(1)} collective-permute-done((bf16[96,512]{1,0:T(8,128)(2,1)S(1)}, bf16[96,512]{1,0:T(8,128)(2,1)S(1)}, u32[]{:S(2)}, u32[]{:S(2)}) %collective-permute-start.10) | collective-permute-done | bytes 98336 | tf_op jit(solution)/shard_map/ppermute | solution.py:410
  102.5 1.8 %collective-permute-done.8 = bf16[96,512]{1,0:T(8,128)(2,1)S(1)} collective-permute-done((bf16[96,512]{1,0:T(8,128)(2,1)S(1)}, bf16[96,512]{1,0:T(8,128)(2,1)S(1)}, u32[]{:S(2)}, u32[]{:S(2)}) %collective-permute-start.8) | collective-permute-done | bytes 98336 | tf_op jit(solution)/shard_map/ppermute | solution.py:410
  104.3 1.9 %collective-permute-done.9 = bf16[96,512]{1,0:T(8,128)(2,1)S(1)} collective-permute-done((bf16[96,512]{1,0:T(8,128)(2,1)S(1)}, bf16[96,512]{1,0:T(8,128)(2,1)S(1)}, u32[]{:S(2)}, u32[]{:S(2)}) %collective-permute-start.9) | collective-permute-done | bytes 98336 | tf_op jit(solution)/shard_map/ppermute | solution.py:410
  106.2 0.0 copy-done
  106.2 0.0 copy-done.7
  106.2 1.3 %conditional.1 = (bf16[4,256,2,256]{3,2,1,0:T(2,128)(2,1)S(1)}) conditional(s32[]{:T(128)} %bitcast.27, (bf16[4,96,512]{2,1,0:T(8,128)(2,1)S(1)}, s32[16,256]{1,0:T(8,128)S(1)}, bf16[1024,512]{1,0:T(8,128)(2,1)S(1)}, bf16[256,512]{1,0:T(8,128)(2,1)S(1)}, bf16[96,512]{1,0:T(8,128)(2,1)S(1)}, /*index=5*/bf16[96,512]{1,0:T(8,128)(2,1)S(1)}, ...), branch_computations={%region_0.1_spmd, %region_1.20_spmd} | conditional | flops 1896640768 | bytes 78463608 | solution.py:423
  106.2 0.9 branch_0_fun.1
  107.2 0.3 reshape.1227
  107.5 0.0 copy-start.1
  107.5 1.0 copy-done.1
  (2 shorter events, 0.0 us)
Async XLA Ops:
  9.9 5.0 %copy-start.6 = (s32[4,256]{1,0:T(4,128)S(1)}, s32[4,256]{1,0:T(4,128)}, u32[]{:S(2)}) copy-start(s32[4,256]{1,0:T(4,128)} %piv_ref.3) | copy-start | bytes 12292
  10.0 30.9 %collective-permute-start = (bf16[1024,256]{1,0:T(8,128)(2,1)S(1)}, bf16[1024,256]{1,0:T(8,128)(2,1)S(1)}, u32[]{:S(2)}, u32[]{:S(2)}) collective-permute-start(bf16[1024,256]{1,0:T(8,128)(2,1)S(1)} %bitcast.138), channel_id=1, source_target_pairs={{0,4},{1,5},{2,6},{3,7},{8,12},{9,13},{10,14},{11,15},{16,20},{17,... | collective-permute-start | bytes 1572872 | tf_op jit(solution)/shard_map/ppermute | solution.py:355
  35.3 11.5 %collective-permute-start.4 = (bf16[768,256]{1,0:T(8,128)(2,1)S(1)}, bf16[768,256]{1,0:T(8,128)(2,1)}, u32[]{:S(2)}, u32[]{:S(2)}) collective-permute-start(bf16[768,256]{1,0:T(8,128)(2,1)S(1)} %get-tuple-element.201), channel_id=1, source_target_pairs={{0,4},{1,5},{2,6},{3,7},{8,12},{9,13},{10,14},{11,15},{16,20},{17,... | collective-permute-start | bytes 1179656 | tf_op jit(solution)/shard_map/ppermute | solution.py:355
  37.4 16.7 %collective-permute-start.1 = (bf16[1024,256]{1,0:T(8,128)(2,1)S(1)}, bf16[1024,256]{1,0:T(8,128)(2,1)S(1)}, u32[]{:S(2)}, u32[]{:S(2)}) collective-permute-start(bf16[1024,256]{1,0:T(8,128)(2,1)S(1)} %bitcast.140), channel_id=1, source_target_pairs={{0,2},{1,3},{2,0},{3,1},{8,10},{9,11},{10,8},{11,9},{16,18},{17,19... | collective-permute-start | bytes 1572872 | tf_op jit(solution)/shard_map/ppermute | solution.py:355
  40.8 13.3 %collective-permute-start.2 = (bf16[1024,256]{1,0:T(8,128)(2,1)S(1)}, bf16[1024,256]{1,0:T(8,128)(2,1)}, u32[]{:S(2)}, u32[]{:S(2)}) collective-permute-start(bf16[1024,256]{1,0:T(8,128)(2,1)S(1)} %collective-permute-done), channel_id=1, source_target_pairs={{4,6},{5,7},{6,4},{7,5},{12,14},{13,15},{14,12},{15,13},{20,22},{2... | collective-permute-start | bytes 1572872 | tf_op jit(solution)/shard_map/ppermute | solution.py:376
  42.3 20.4 %collective-permute-start.5 = (bf16[768,256]{1,0:T(8,128)(2,1)S(1)}, bf16[768,256]{1,0:T(8,128)(2,1)}, u32[]{:S(2)}, u32[]{:S(2)}) collective-permute-start(bf16[768,256]{1,0:T(8,128)(2,1)S(1)} %get-tuple-element.201), channel_id=1, source_target_pairs={{0,2},{1,3},{2,0},{3,1},{8,10},{9,11},{10,8},{11,9},{16,18},{17,19... | collective-permute-start | bytes 1179656 | tf_op jit(solution)/shard_map/ppermute | solution.py:355
  44.7 21.4 %collective-permute-start.6 = (bf16[768,256]{1,0:T(8,128)(2,1)S(1)}, bf16[768,256]{1,0:T(8,128)(2,1)}, u32[]{:S(2)}, u32[]{:S(2)}) collective-permute-start(bf16[768,256]{1,0:T(8,128)(2,1)S(1)} %get-tuple-element.201), channel_id=1, source_target_pairs={{0,6},{1,7},{2,4},{3,5},{8,14},{9,15},{10,12},{11,13},{16,22},{17,... | collective-permute-start | bytes 1179656 | tf_op jit(solution)/shard_map/ppermute | solution.py:355
  54.4 31.2 %collective-permute-start.3 = (bf16[2,1024,256]{2,1,0:T(8,128)(2,1)S(1)}, bf16[2,1024,256]{2,1,0:T(8,128)(2,1)S(1)}, u32[]{:S(2)}, u32[]{:S(2)}) collective-permute-start(bf16[2,1024,256]{2,1,0:T(8,128)(2,1)S(1)} %pad_maximum_fusion.raw_a), channel_id=1, source_target_pairs={{0,1},{1,0},{2,3},{3,2},{4,5},{5,4},{6,7},{7,6},{8,9},{9,8},{10,11... | collective-permute-start | bytes 3145736 | tf_op jit(solution)/shard_map/ppermute | solution.py:358
  67.3 18.3 %collective-permute-start.7 = (bf16[2,768,256]{2,1,0:T(8,128)(2,1)S(1)}, bf16[2,768,256]{2,1,0:T(8,128)(2,1)S(1)}, u32[]{:S(2)}, u32[]{:S(2)}) collective-permute-start(bf16[2,768,256]{2,1,0:T(8,128)(2,1)S(1)} %pad_maximum_fusion.1.off_a), channel_id=1, source_target_pairs={{0,1},{1,0},{2,3},{3,2},{4,5},{5,4},{6,7},{7,6},{8,9},{9,8},{10,11... | collective-permute-start | bytes 2359304 | tf_op jit(solution)/shard_map/ppermute | solution.py:358
  85.6 20.6 %copy-start = (bf16[4,256,2,256]{3,2,1,0:T(2,128)(2,1)S(1)}, bf16[4,256,2,256]{3,2,1,0:T(2,128)(2,1)}, u32[]{:S(2)}) copy-start(bf16[4,256,2,256]{3,2,1,0:T(2,128)(2,1)} %param.32) | copy-start | bytes 3145732
  85.6 20.6 %copy-start.7 = (s32[4,256]{1,0:T(4,128)S(1)}, s32[4,256]{1,0:T(4,128)}, u32[]{:S(2)}) copy-start(s32[4,256]{1,0:T(4,128)} %piv_ref.3) | copy-start | bytes 12292
  96.1 6.4 %collective-permute-start.10 = (bf16[96,512]{1,0:T(8,128)(2,1)S(1)}, bf16[96,512]{1,0:T(8,128)(2,1)S(1)}, u32[]{:S(2)}, u32[]{:S(2)}) collective-permute-start(bf16[96,512]{1,0:T(8,128)(2,1)S(1)} %get-tuple-element.253), channel_id=1, source_target_pairs={{0,24},{8,0},{16,8},{24,16},{1,25},{9,1},{17,9},{25,17},{2,26},{10... | collective-permute-start | bytes 294920 | tf_op jit(solution)/shard_map/ppermute | solution.py:410
  97.8 6.4 %collective-permute-start.8 = (bf16[96,512]{1,0:T(8,128)(2,1)S(1)}, bf16[96,512]{1,0:T(8,128)(2,1)S(1)}, u32[]{:S(2)}, u32[]{:S(2)}) collective-permute-start(bf16[96,512]{1,0:T(8,128)(2,1)S(1)} %get-tuple-element.255), channel_id=1, source_target_pairs={{0,8},{8,16},{16,24},{24,0},{1,9},{9,17},{17,25},{25,1},{2,10},{10... | collective-permute-start | bytes 294920 | tf_op jit(solution)/shard_map/ppermute | solution.py:410
  98.2 8.0 %collective-permute-start.9 = (bf16[96,512]{1,0:T(8,128)(2,1)S(1)}, bf16[96,512]{1,0:T(8,128)(2,1)S(1)}, u32[]{:S(2)}, u32[]{:S(2)}) collective-permute-start(bf16[96,512]{1,0:T(8,128)(2,1)S(1)} %get-tuple-element.254), channel_id=1, source_target_pairs={{0,16},{8,24},{16,0},{24,8},{1,17},{9,25},{17,1},{25,9},{2,18},{10... | collective-permute-start | bytes 294920 | tf_op jit(solution)/shard_map/ppermute | solution.py:410
  107.5 1.0 copy-start.1

commit v2 on v1

--- a/solution.py
+++ b/solution.py
@@ -15,9 +15,20 @@
 MOVE_SLOTS = 128
 
 
+def ring_sum(value, axis):
+    size = lax.axis_size(axis)
+
+    def turn(_, carry):
+        total, passing = carry
+        passing = lax.ppermute(passing, axis, [(i, (i + 1) % size) for i in range(size)])
+        return total + passing, passing
+
+    return lax.fori_loop(1, size, turn, (value, value))[0]
+
+
 def spread(value, axis, source):
     kept = jnp.where(lax.axis_index(axis) == source, value, 0).astype(value.dtype)
-    return lax.psum(kept, axis)
+    return ring_sum(kept, axis)
 
 
 def stepwise(matrix, pivots, lower_inverse, upper_inverse):
@@ -52,7 +63,7 @@
         picked = jnp.where(is_mine[:, None], picked, jnp.zeros_like(picked))
         diag_rows = matrix_loc[diag_local : diag_local + block_size]
         own_diag = jnp.where(my_row == diag_root, diag_rows, jnp.zeros_like(diag_rows))
-        new_rows, old_diag = lax.psum(picked, "prow"), lax.psum(own_diag, "prow")
+        new_rows, old_diag = ring_sum(picked, "prow"), ring_sum(own_diag, "prow")
         moved_rows = is_mine & (chosen != targets)
         matrix_loc = matrix_loc.at[jnp.where(moved_rows, chosen_local, local_rows)].set(
             old_diag, mode="drop"
@@ -122,7 +133,7 @@
     return [counts[i * k : (i + 1) * k] for i in range(len(rows))]
 
 
-def pick_kernel(cfg, piv_ref, m0_ref, m1_ref, meta_ref, pack0_ref, pack1_ref):
+def pick_kernel(cfg, piv_ref, mat_ref, meta_ref, pack0_ref, pack1_ref):
     nb, steps, n_row, cap, local_rows = cfg
     my_row = lax.axis_index("prow")
     piv = [piv_ref[t : t + 1, :] for t in range(steps)]
@@ -156,8 +167,8 @@
         total = total + jnp.where(slot == key, places[t] + 1, 0)
     source = jnp.sum(total, axis=1, keepdims=True) - 1
     chosen = one_hot(source == iota((cap, local_rows), 1))
-    pack0_ref[...] = dot(chosen, m0_ref[...]).astype(BF16)
-    pack1_ref[...] = dot(chosen, m1_ref[...]).astype(BF16)
+    pack0_ref[...] = dot(chosen, mat_ref[0]).astype(BF16)
+    pack1_ref[...] = dot(chosen, mat_ref[1]).astype(BF16)
 
 
 def move_kernel(cfg, piv_ref, meta_ref, move_ref):
@@ -210,23 +221,21 @@
 
 
 def factor_kernel(
-    cfg, meta_ref, move_ref, top0_ref, buf1_ref, m0_ref, m1_ref, raw_a, raw_b, off_a, off_b,
-    linv_ref, uinv_ref, res_ref, top_ref, send_ref, raw, off, l_own, l_top, u_top, upper, first,
+    cfg, meta_ref, move_ref, top0_ref, buf1_ref, mat_ref, raw_0, raw_2, raw_1, raw_3,
+    off_0, off_2, off_1, off_3, linv_ref, uinv_ref, res_ref, top_ref, send_ref, raw, off, l_own, l_top, u_top, upper, first,
     diag, sems,
 ):
     nb, steps, n_row, local_rows = cfg
     my_row = lax.axis_index("prow")
     my_col = lax.axis_index("pcol")
     low = my_col & 3
-    copies = []
-    for i, (src, at, mask) in enumerate(
-        [(off_a, 0, 0), (off_a, 1, 2), (off_b, 0, 1), (off_b, 1, 3)]
-    ):
-        copies.append(pltpu.make_async_copy(src.at[at], off.at[low ^ mask], sems.at[i]))
-    for i, (src, at, mask) in enumerate(
-        [(raw_a, 0, 0), (raw_a, 1, 2), (raw_b, 0, 1), (raw_b, 1, 3)]
-    ):
-        copies.append(pltpu.make_async_copy(src.at[at], raw.at[low ^ mask], sems.at[4 + i]))
+    copies = [
+        pltpu.make_async_copy(src, dst.at[low ^ mask], sems.at[i])
+        for i, (src, dst, mask) in enumerate(
+            [(off_0, off, 0), (off_1, off, 1), (off_2, off, 2), (off_3, off, 3)]
+            + [(raw_0, raw, 0), (raw_1, raw, 1), (raw_2, raw, 2), (raw_3, raw, 3)]
+        )
+    ]
     for c in copies:
         c.start()
     wide = steps * nb
@@ -266,9 +275,9 @@
     for k in range(local_rows // nb):
         rows = slice(k * nb, (k + 1) * nb)
         prod = dot(l_own[rows, :], upper[...])
-        left = (m0_ref[rows, :].astype(F32) - prod[:, :nb]).astype(BF16)
+        left = (mat_ref[0, rows, :].astype(F32) - prod[:, :nb]).astype(BF16)
         res_ref[rows, :nb] = jnp.where(in_panel, l_own[rows, panel], left)
-        res_ref[rows, nb:] = (m1_ref[rows, :].astype(F32) - prod[:, nb:]).astype(BF16)
+        res_ref[rows, nb:] = (mat_ref[1, rows, :].astype(F32) - prod[:, nb:]).astype(BF16)
     block = pl.ds(pl.multiple_of(jnp.minimum(my_row, steps - 1) * nb, nb), nb)
     own_upper = upper[block, :]
     left = jnp.where(my_col == my_row, diag[block, :], own_upper[:, :nb])
@@ -348,8 +357,8 @@
     my_col = lax.axis_index("pcol")
     local_rows = row_blocks * nb
     cap = -(-(steps * nb // n_row + 64) // 16) * 16
-    m0 = matrix[:, :, 0, :].reshape(local_rows, nb)
-    m1 = matrix[:, :, 1, :].reshape(local_rows, nb)
+    mat = jnp.transpose(matrix, (2, 0, 1, 3)).reshape(col_blocks, local_rows, nb)
+    m0 = mat[0]
 
     def from_panels(value, mask):
         return lax.ppermute(value, "pcol", [(i, i ^ mask) for i in range(steps)])
@@ -365,34 +374,42 @@
     meta, pack0, pack1 = call(
         functools.partial(pick_kernel, (nb, steps, n_row, cap, local_rows)),
         (shape(8, nb, dtype=I32), shape(cap, nb), shape(cap, nb)),
-        (pivots, m0, m1),
+        (pivots, mat),
     )
     buf0 = lax.all_gather(pack0, "prow", tiled=True)
+    buf0, raw_x, raw_far = lax.optimization_barrier((buf0, raw_x, raw_far))
     top0, off = call(
         functools.partial(order_kernel, (nb, steps)),
         (shape(steps * nb, nb), shape((steps - 1) * nb, nb)),
         (meta, buf0),
     )
-    raw_far_x = lax.ppermute(raw_far, "pcol", [(i, i ^ 2) for i in range(steps, n_col)])
+    pack1, off = lax.optimization_barrier((pack1, off))
     off_x = from_panels(off, 2)
     off_far = functools.reduce(jnp.add, [from_panels(off, mask) for mask in fours])
     off_far_x = functools.reduce(jnp.add, [from_panels(off, mask + 2) for mask in fours])
-    pack1, _ = lax.optimization_barrier((pack1, off))
+    raw_far_x = lax.ppermute(raw_far, "pcol", [(i, i ^ 2) for i in range(steps, n_col)])
     buf1 = lax.all_gather(pack1, "prow", tiled=True)
     move = call(
         functools.partial(move_kernel, (nb, steps, n_row, cap)),
         shape(16, nb, dtype=I32),
         (pivots, meta),
     )
-    raw_a = jnp.stack([jnp.where(on_panel, m0, raw_far), jnp.where(on_panel, raw_x, raw_far_x)])
-    raw_b = swap_cores(raw_a)
-    off_a = jnp.stack([jnp.where(on_panel, off, off_far), jnp.where(on_panel, off_x, off_far_x)])
-    off_b = swap_cores(off_a)
+    buf1, off_far, raw_far_x = lax.optimization_barrier((buf1, off_far, raw_far_x))
+    raw_0 = jnp.where(on_panel, m0, raw_far)
+    raw_2 = jnp.where(on_panel, raw_x, raw_far_x)
+    off_0 = jnp.where(on_panel, off, off_far)
+    raw_1, raw_3, off_1 = swap_cores(raw_0), swap_cores(raw_2), swap_cores(off_0)
+    buf1, off_x, off_far_x = lax.optimization_barrier((buf1, off_x, off_far_x))
+    off_2 = jnp.where(on_panel, off_x, off_far_x)
+    off_3 = swap_cores(off_2)
     top_rows = steps * nb
     res, top, send = call(
         functools.partial(factor_kernel, (nb, steps, n_row, local_rows)),
         (shape(local_rows, 2 * nb), shape(nb, 2 * nb), shape(n_row, MOVE_ROWS, 2 * nb)),
-        (meta, move, top0, buf1, m0, m1, raw_a, raw_b, off_a, off_b, lower_inverse, upper_inverse),
+        (
+            meta, move, top0, buf1, mat, raw_0, raw_2, raw_1, raw_3, off_0, off_2, off_1, off_3,
+            lower_inverse, upper_inverse,
+        ),
         scratch=(
             pltpu.VMEM((steps, local_rows, nb), BF16),
             pltpu.VMEM((steps, top_rows - nb, nb), BF16),
@@ -404,7 +421,7 @@
             pltpu.VMEM((top_rows, nb), BF16),
             pltpu.SemaphoreType.DMA((8,)),
         ),
-        any_at=(6, 7, 8, 9),
+        any_at=range(5, 13),
     )
     recv = [send[0]] + [
         lax.ppermute(send[k], "prow", [(i, (i + k) % n_row) for i in range(n_row)])

time: 116 us -> 80.9 us (0.70)
  waiting for transfers between devices: 25 us -> 7.2 us
  between operations: 14.2 us -> 0.86 us
  local copies, waits for them, and re-layouts: 5.3 us -> 3.22 us
  other arithmetic: 1.44 us -> 0.26 us
    ppermute x5, waiting for transfers between devices: 18.9 us -> 0.01 us  [from_panels(): return lax.ppermute(value, 'pcol', [(i, i ^ mask) for i in range(steps)])]
    slice x1, local copies, waits for them, and re-layouts: 3.3 us -> 0.04 us  [local(): m0 = mat[0]]
    ppermute x5, starting transfers between devices: 14.9 us -> 12.7 us  [from_panels(): return lax.ppermute(value, 'pcol', [(i, i ^ mask) for i in range(steps)])]
    another operation x6 -> x0, other arithmetic: 1.44 us -> none  [the longest x3 1.17 us: local(): jnp.stack([jnp.where(on_panel, off, off_far), jnp.where(on_panel, off_x,...]
    ppermute x2 -> x4, waiting for transfers between devices: 0.01 us -> 1.2 us  [swap_cores(): return lax.ppermute(value, 'pcol', [(i, i ^ 1) for i in range(n_col)])]
    unnamed x10 -> x13, local copies, waits for them, and re-layouts: 1.17 us -> 2.35 us
  transfers between devices with their start and end apart: 11 -> 13, of which waited for: 6 -> 3; matrix products, arithmetic and copies ran while one was open for 2% -> 1% of each run, Pallas kernels for 3% -> 4%
where the time goes in v2:
time: 80.9 us; the launch traced here: 80.5 us
  blocking collectives  35.6 us (44%)
  starting transfers between devices  18.8 us (23%)
  Pallas kernels  14.5 us (18%)
  waiting for transfers between devices  7.2 us (9%)
  local copies, waits for them, and re-layouts  3.22 us (4%)
  between operations  0.86 us (1%)
    all_gather x1, blocking collectives, local(): buf0 = lax.all_gather(pack0, 'prow', tiled=True)  18.1 us
    all_gather x1, blocking collectives, local(): buf1 = lax.all_gather(pack1, 'prow', tiled=True)  17.5 us
    pallas_call x5, Pallas kernels, call(): pl.pallas_call(kernel, out_shape=outs, in_specs=[anywhere if i in any_at...  14.5 us
    ppermute x5, starting transfers between devices, from_panels(): return lax.ppermute(value, 'pcol', [(i, i ^ mask) for i in range(steps)])  12.7 us
    ppermute x3, waiting for transfers between devices, local(): lax.ppermute(send[k], 'prow', [(i, (i + k) % n_row) for i in range(n_row)])  5.98 us
    ppermute x3, starting transfers between devices, local(): lax.ppermute(send[k], 'prow', [(i, (i + k) % n_row) for i in range(n_row)])  3.88 us
    unnamed x13, local copies, waits for them, and re-layouts  2.35 us
  transfers between devices with their start and end apart: 13, of which 3 were waited for; matrix products, arithmetic and copies ran while one was open for 1% of the time, Pallas kernels for 4%

profile of v2, /device:TPU:0, one launch (start us, length us, event | category | flops | bytes accessed | tf_op | source)
XLA Modules:
  0.0 80.5 jit_solution(12160393715718931600)
XLA Ops:
  0.0 1.4 %copy.25 = bf16[4,256,2,256]{3,1,0,2:T(8,128)(2,1)S(1)} copy(bf16[4,256,2,256]{3,2,1,0:T(2,128)(2,1)} %param.56) | data formatting | bytes 2097152 | tf_op args[0]
  1.4 0.0 copy-start.9
  1.4 4.8 %collective-permute-start.12 = (bf16[1024,256]{1,0:T(8,128)(2,1)S(1)}, bf16[1024,256]{1,0:T(8,128)(2,1)S(1)}, u32[]{:S(2)}, u32[]{:S(2)}) collective-permute-start(bf16[1024,256]{1,0:T(8,128)(2,1)S(1)} %bitcast.142), channel_id=1, source_target_pairs={{0,2},{1,3},{2,0},{3,1},{8,10},{9,11},{10,8},{11,9},{16,18},{17,19... | collective-permute-start | bytes 1572872 | tf_op jit(solution)/shard_map/ppermute | solution.py:364
  6.3 2.1 %collective-permute-start.13 = (bf16[1024,256]{1,0:T(8,128)(2,1)S(1)}, bf16[1024,256]{1,0:T(8,128)(2,1)}, u32[]{:S(2)}, u32[]{:S(2)}) collective-permute-start(bf16[1024,256]{1,0:T(8,128)(2,1)S(1)} %bitcast.143), channel_id=1, source_target_pairs={{0,4},{1,5},{2,6},{3,7},{8,12},{9,13},{10,14},{11,15},{16,20},{17,... | collective-permute-start | bytes 1572872 | tf_op jit(solution)/shard_map/ppermute | solution.py:364
  8.4 0.0 copy-done.9
  8.4 1.2 %shard_map.48 = (s32[8,256]{1,0:T(8,128)S(1)}, bf16[320,256]{1,0:T(8,128)(2,1)S(1)}, bf16[320,256]{1,0:T(8,128)(2,1)S(1)}) custom-call(s32[4,256]{1,0:T(4,128)S(1)} %copy-done.9, bf16[2,1024,256]{2,1,0:T(8,128)(2,1)S(1)} %bitcast.135), custom_call_target="tpu_custom_call" | custom-call | tf_op jit(solution)/shard_map/pallas_call | solution.py:336
  9.6 18.1 %all_gather.6.buf_ref = bf16[1280,256]{1,0:T(8,128)(2,1)S(1)} all-gather(bf16[320,256]{1,0:T(8,128)(2,1)S(1)} %get-tuple-element.412), channel_id=1, replica_groups=mesh['prow'=4,'pcol'=8] {'prow'}, dimensions={0}, use_global_device_ids=true | all-gather | bytes 819200 | tf_op jit(solution)/shard_map/all_gather | solution.py:379
  27.7 0.0 collective-permute-done.12
  27.7 0.0 copy-start.7
  27.7 0.0 collective-permute-done.13
  27.7 1.5 %collective-permute-start.15 = (bf16[1024,256]{1,0:T(8,128)(2,1)}, bf16[1024,256]{1,0:T(8,128)(2,1)}, u32[]{:S(2)}, u32[]{:S(2)}) collective-permute-start(bf16[1024,256]{1,0:T(8,128)(2,1)} %collective-permute-done.13), channel_id=1, source_target_pairs={{4,6},{5,7},{6,4},{7,5},{12,14},{13,15},{14,12},{15,13},{20,22},{2... | collective-permute-start | bytes 1572872 | tf_op jit(solution)/shard_map/ppermute | solution.py:390
  29.2 0.0 copy-done.7
  29.2 1.1 %shard_map.50 = (bf16[1024,256]{1,0:T(8,128)(2,1)S(1)}, bf16[768,256]{1,0:T(8,128)(2,1)S(1)}) custom-call(s32[8,256]{1,0:T(8,128)S(1)} %get-tuple-element.411.meta_ref, bf16[1280,256]{1,0:T(8,128)(2,1)S(1)} %all_gather.6.buf_ref), custom_call_target="tpu_custom_call" | custom-call | tf_op jit(solution)/shard_map/pallas_call | solution.py:336
  30.3 2.0 %collective-permute-start.14 = (bf16[768,256]{1,0:T(8,128)(2,1)S(1)}, bf16[768,256]{1,0:T(8,128)(2,1)S(1)}, u32[]{:S(2)}, u32[]{:S(2)}) collective-permute-start(bf16[768,256]{1,0:T(8,128)(2,1)S(1)} %get-tuple-element.418), channel_id=1, source_target_pairs={{0,4},{1,5},{2,6},{3,7},{8,12},{9,13},{10,14},{11,15},{16,20},{17,... | collective-permute-start | bytes 1179656 | tf_op jit(solution)/shard_map/ppermute | solution.py:364
  32.2 2.4 %collective-permute-start.16 = (bf16[768,256]{1,0:T(8,128)(2,1)S(1)}, bf16[768,256]{1,0:T(8,128)(2,1)S(1)}, u32[]{:S(2)}, u32[]{:S(2)}) collective-permute-start(bf16[768,256]{1,0:T(8,128)(2,1)S(1)} %get-tuple-element.418), channel_id=1, source_target_pairs={{0,2},{1,3},{2,0},{3,1},{8,10},{9,11},{10,8},{11,9},{16,18},{17,19... | collective-permute-start | bytes 1179656 | tf_op jit(solution)/shard_map/ppermute | solution.py:364
  34.7 1.3 %collective-permute-start.17 = (bf16[768,256]{1,0:T(8,128)(2,1)S(1)}, bf16[768,256]{1,0:T(8,128)(2,1)S(1)}, u32[]{:S(2)}, u32[]{:S(2)}) collective-permute-start(bf16[768,256]{1,0:T(8,128)(2,1)S(1)} %get-tuple-element.418), channel_id=1, source_target_pairs={{0,6},{1,7},{2,4},{3,5},{8,14},{9,15},{10,12},{11,13},{16,22},{17,... | collective-permute-start | bytes 1179656 | tf_op jit(solution)/shard_map/ppermute | solution.py:364
  36.0 0.1 broadcast_select_fusion.5.raw_0
  36.1 0.0 copy-start.8
  36.1 0.1 collective-permute-start.18
  36.2 17.5 %all_gather.7.buf1_ref = bf16[1280,256]{1,0:T(8,128)(2,1)S(1)} all-gather(bf16[320,256]{1,0:T(8,128)(2,1)S(1)} %get-tuple-element.417), channel_id=1, replica_groups=mesh['prow'=4,'pcol'=8] {'prow'}, dimensions={0}, use_global_device_ids=true | all-gather | bytes 819200 | tf_op jit(solution)/shard_map/all_gather | solution.py:391
  53.7 0.0 collective-permute-done.14
  53.7 0.0 collective-permute-done.15
  53.7 0.0 collective-permute-done.16
  53.8 0.0 collective-permute-done.17
  53.8 0.0 copy-start.1
  53.8 0.1 collective-permute-start.21
  53.9 0.0 copy-done.8
  53.9 0.1 broadcast_select_fusion.4.raw_2
  54.0 0.5 collective-permute-start.19
  54.6 0.1 collective-permute-start.20
  54.7 1.0 %shard_map.49.move_ref = s32[16,256]{1,0:T(8,128)S(1)} custom-call(s32[4,256]{1,0:T(4,128)S(1)} %copy-done.9, s32[8,256]{1,0:T(8,128)S(1)} %get-tuple-element.411.meta_ref), custom_call_target="tpu_custom_call" | custom-call | tf_op jit(solution)/shard_map/pallas_call | solution.py:336
  55.7 0.0 collective-permute-done.18.raw_1
  55.7 0.0 collective-permute-done.21.off_3
  55.7 1.2 %collective-permute-done.20.off_1 = bf16[768,256]{1,0:T(8,128)(2,1)S(1)} collective-permute-done((bf16[768,256]{1,0:T(8,128)(2,1)S(1)}, bf16[768,256]{1,0:T(8,128)(2,1)S(1)}, u32[]{:S(2)}, u32[]{:S(2)}) %collective-permute-start.20) | collective-permute-done | bytes 393248 | tf_op jit(solution)/shard_map/ppermute | solution.py:367
  56.9 0.0 collective-permute-done.19.raw_3
  56.9 0.0 copy-done.1
  56.9 0.0 copy-start
  56.9 10.3 %shard_map.51 = (bf16[1024,512]{1,0:T(8,128)(2,1)S(1)}, bf16[256,512]{1,0:T(8,128)(2,1)S(1)}, bf16[4,96,512]{2,1,0:T(8,128)(2,1)S(1)}) custom-call(s32[8,256]{1,0:T(8,128)S(1)} %get-tuple-element.411.meta_ref, s32[16,256]{1,0:T(8,128)S(1)} %shard_map.49.move_ref, bf16[1024,256]{1,0:T(8,128)(2,1)S(1)} %get-tuple-element.414.top0_ref, ...), custom_call_target="tpu_custom_call" | custom-call | tf_op jit(solution)/shard_map/pallas_call | solution.py:336
  67.3 0.5 collective-permute-start.22
  67.8 2.6 %collective-permute-start.23 = (bf16[96,512]{1,0:T(8,128)(2,1)S(1)}, bf16[96,512]{1,0:T(8,128)(2,1)S(1)}, u32[]{:S(2)}, u32[]{:S(2)}) collective-permute-start(bf16[96,512]{1,0:T(8,128)(2,1)S(1)} %get-tuple-element.554), channel_id=1, source_target_pairs={{0,16},{8,24},{16,0},{24,8},{1,17},{9,25},{17,1},{25,9},{2,18},{10... | collective-permute-start | bytes 294920 | tf_op jit(solution)/shard_map/ppermute | solution.py:427
  70.4 0.8 collective-permute-start.24
  71.1 0.5 slice.344
  72.3 2.5 %collective-permute-done.22 = bf16[96,512]{1,0:T(8,128)(2,1)S(1)} collective-permute-done((bf16[96,512]{1,0:T(8,128)(2,1)S(1)}, bf16[96,512]{1,0:T(8,128)(2,1)S(1)}, u32[]{:S(2)}, u32[]{:S(2)}) %collective-permute-start.22) | collective-permute-done | bytes 98336 | tf_op jit(solution)/shard_map/ppermute | solution.py:427
  74.9 3.4 %collective-permute-done.23 = bf16[96,512]{1,0:T(8,128)(2,1)S(1)} collective-permute-done((bf16[96,512]{1,0:T(8,128)(2,1)S(1)}, bf16[96,512]{1,0:T(8,128)(2,1)S(1)}, u32[]{:S(2)}, u32[]{:S(2)}) %collective-permute-start.23) | collective-permute-done | bytes 98336 | tf_op jit(solution)/shard_map/ppermute | solution.py:427
  78.3 0.0 collective-permute-done.24
  78.3 0.0 copy-done
  78.3 1.3 %conditional.1 = (bf16[4,256,2,256]{3,2,1,0:T(2,128)(2,1)S(1)}) conditional(s32[]{:T(128)} %bitcast.27, (bf16[4,96,512]{2,1,0:T(8,128)(2,1)S(1)}, s32[16,256]{1,0:T(8,128)S(1)}, bf16[1024,512]{1,0:T(8,128)(2,1)S(1)}, bf16[256,512]{1,0:T(8,128)(2,1)S(1)}, bf16[96,512]{1,0:T(8,128)(2,1)S(1)}, /*index=5*/bf16[96,512]{1,0:T(8,128)(2,1)S(1)}, ...), branch_computations={%region_0.1_spmd, %region_1.32_spmd} | conditional | flops 1896568576 | bytes 101533552 | solution.py:440
  78.3 0.9 %branch_0_fun.1 = bf16[1024,512]{1,0:T(8,128)(2,1)S(1)} custom-call(s32[16,256]{1,0:T(8,128)S(1)} %get-tuple-element.321.move_ref, bf16[1024,512]{1,0:T(8,128)(2,1)S(1)} %get-tuple-element.322.res_ref, bf16[256,512]{1,0:T(8,128)(2,1)S(1)} %get-tuple-element.323.top_ref, bf16[96,512]{1,0:T(8,128)(2,1)S(1)} %slice_bitcast_fusion.refs_0_, ...), custom_call_target="tpu_custom_call" | custom-call | tf_op jit(solution)/shard_map/cond/branch_0_fun/pallas_call | solution.py:336
  79.2 0.3 reshape.1231
  79.6 0.0 copy-start.6
  79.6 1.0 %copy-done.6 = bf16[4,256,2,256]{3,2,1,0:T(2,128)(2,1)} copy-done((bf16[4,256,2,256]{3,2,1,0:T(2,128)(2,1)}, bf16[4,256,2,256]{3,2,1,0:T(2,128)(2,1)S(1)}, u32[]{:S(2)}) %copy-start.6) | copy-done | bytes 1048600
  (5 shorter events, 0.2 us)
Async XLA Ops:
  1.4 7.0 %copy-start.9 = (s32[4,256]{1,0:T(4,128)S(1)}, s32[4,256]{1,0:T(4,128)}, u32[]{:S(2)}) copy-start(s32[4,256]{1,0:T(4,128)} %piv_ref.3) | copy-start | bytes 12292
  1.4 26.3 %collective-permute-start.12 = (bf16[1024,256]{1,0:T(8,128)(2,1)S(1)}, bf16[1024,256]{1,0:T(8,128)(2,1)S(1)}, u32[]{:S(2)}, u32[]{:S(2)}) collective-permute-start(bf16[1024,256]{1,0:T(8,128)(2,1)S(1)} %bitcast.142), channel_id=1, source_target_pairs={{0,2},{1,3},{2,0},{3,1},{8,10},{9,11},{10,8},{11,9},{16,18},{17,19... | collective-permute-start | bytes 1572872 | tf_op jit(solution)/shard_map/ppermute | solution.py:364
  6.3 21.4 %collective-permute-start.13 = (bf16[1024,256]{1,0:T(8,128)(2,1)S(1)}, bf16[1024,256]{1,0:T(8,128)(2,1)}, u32[]{:S(2)}, u32[]{:S(2)}) collective-permute-start(bf16[1024,256]{1,0:T(8,128)(2,1)S(1)} %bitcast.143), channel_id=1, source_target_pairs={{0,4},{1,5},{2,6},{3,7},{8,12},{9,13},{10,14},{11,15},{16,20},{17,... | collective-permute-start | bytes 1572872 | tf_op jit(solution)/shard_map/ppermute | solution.py:364
  27.7 1.5 %copy-start.7 = (bf16[1024,256]{1,0:T(8,128)(2,1)}, bf16[1024,256]{1,0:T(8,128)(2,1)S(1)}, u32[]{:S(2)}) copy-start(bf16[1024,256]{1,0:T(8,128)(2,1)S(1)} %collective-permute-done.12) | copy-start | bytes 1572868
  27.7 26.1 %collective-permute-start.15 = (bf16[1024,256]{1,0:T(8,128)(2,1)}, bf16[1024,256]{1,0:T(8,128)(2,1)}, u32[]{:S(2)}, u32[]{:S(2)}) collective-permute-start(bf16[1024,256]{1,0:T(8,128)(2,1)} %collective-permute-done.13), channel_id=1, source_target_pairs={{4,6},{5,7},{6,4},{7,5},{12,14},{13,15},{14,12},{15,13},{20,22},{2... | collective-permute-start | bytes 1572872 | tf_op jit(solution)/shard_map/ppermute | solution.py:390
  30.3 23.5 %collective-permute-start.14 = (bf16[768,256]{1,0:T(8,128)(2,1)S(1)}, bf16[768,256]{1,0:T(8,128)(2,1)S(1)}, u32[]{:S(2)}, u32[]{:S(2)}) collective-permute-start(bf16[768,256]{1,0:T(8,128)(2,1)S(1)} %get-tuple-element.418), channel_id=1, source_target_pairs={{0,4},{1,5},{2,6},{3,7},{8,12},{9,13},{10,14},{11,15},{16,20},{17,... | collective-permute-start | bytes 1179656 | tf_op jit(solution)/shard_map/ppermute | solution.py:364
  32.2 21.5 %collective-permute-start.16 = (bf16[768,256]{1,0:T(8,128)(2,1)S(1)}, bf16[768,256]{1,0:T(8,128)(2,1)S(1)}, u32[]{:S(2)}, u32[]{:S(2)}) collective-permute-start(bf16[768,256]{1,0:T(8,128)(2,1)S(1)} %get-tuple-element.418), channel_id=1, source_target_pairs={{0,2},{1,3},{2,0},{3,1},{8,10},{9,11},{10,8},{11,9},{16,18},{17,19... | collective-permute-start | bytes 1179656 | tf_op jit(solution)/shard_map/ppermute | solution.py:364
  34.7 19.1 %collective-permute-start.17 = (bf16[768,256]{1,0:T(8,128)(2,1)S(1)}, bf16[768,256]{1,0:T(8,128)(2,1)S(1)}, u32[]{:S(2)}, u32[]{:S(2)}) collective-permute-start(bf16[768,256]{1,0:T(8,128)(2,1)S(1)} %get-tuple-element.418), channel_id=1, source_target_pairs={{0,6},{1,7},{2,4},{3,5},{8,14},{9,15},{10,12},{11,13},{16,22},{17,... | collective-permute-start | bytes 1179656 | tf_op jit(solution)/shard_map/ppermute | solution.py:364
  36.1 17.8 %copy-start.8 = (bf16[1024,256]{1,0:T(8,128)(2,1)S(1)}, bf16[1024,256]{1,0:T(8,128)(2,1)}, u32[]{:S(2)}) copy-start(bf16[1024,256]{1,0:T(8,128)(2,1)} %copy-done.7) | copy-start | bytes 1572868
  36.1 19.6 %collective-permute-start.18 = (bf16[1024,256]{1,0:T(8,128)(2,1)S(1)}, bf16[1024,256]{1,0:T(8,128)(2,1)S(1)}, u32[]{:S(2)}, u32[]{:S(2)}) collective-permute-start(bf16[1024,256]{1,0:T(8,128)(2,1)S(1)} %broadcast_select_fusion.5.raw_0), channel_id=1, source_target_pairs={{0,1},{1,0},{2,3},{3,2},{4,5},{5,4},{6,7},{7,6},{8,9},{9,8},{10,11... | collective-permute-start | bytes 1572872 | tf_op jit(solution)/shard_map/ppermute | solution.py:367
  53.8 3.1 %copy-start.1 = (bf16[4,256,256]{2,1,0:T(8,128)(2,1)S(1)}, bf16[4,256,256]{2,1,0:T(8,128)(2,1)}, u32[]{:S(2)}) copy-start(bf16[4,256,256]{2,1,0:T(8,128)(2,1)} %linv_ref.1) | copy-start | bytes 1572868
  53.8 1.9 %collective-permute-start.21 = (bf16[768,256]{1,0:T(8,128)(2,1)S(1)}, bf16[768,256]{1,0:T(8,128)(2,1)S(1)}, u32[]{:S(2)}, u32[]{:S(2)}) collective-permute-start(bf16[768,256]{1,0:T(8,128)(2,1)S(1)} %broadcast_select_fusion.6.off_2), channel_id=1, source_target_pairs={{0,1},{1,0},{2,3},{3,2},{4,5},{5,4},{6,7},{7,6},{8,9},{9,8},{10,11... | collective-permute-start | bytes 1179656 | tf_op jit(solution)/shard_map/ppermute | solution.py:367
  54.0 2.9 %collective-permute-start.19 = (bf16[1024,256]{1,0:T(8,128)(2,1)S(1)}, bf16[1024,256]{1,0:T(8,128)(2,1)S(1)}, u32[]{:S(2)}, u32[]{:S(2)}) collective-permute-start(bf16[1024,256]{1,0:T(8,128)(2,1)S(1)} %broadcast_select_fusion.4.raw_2), channel_id=1, source_target_pairs={{0,1},{1,0},{2,3},{3,2},{4,5},{5,4},{6,7},{7,6},{8,9},{9,8},{10,11... | collective-permute-start | bytes 1572872 | tf_op jit(solution)/shard_map/ppermute | solution.py:367
  54.6 2.3 %collective-permute-start.20 = (bf16[768,256]{1,0:T(8,128)(2,1)S(1)}, bf16[768,256]{1,0:T(8,128)(2,1)S(1)}, u32[]{:S(2)}, u32[]{:S(2)}) collective-permute-start(bf16[768,256]{1,0:T(8,128)(2,1)S(1)} %broadcast_select_fusion.7.off_0), channel_id=1, source_target_pairs={{0,1},{1,0},{2,3},{3,2},{4,5},{5,4},{6,7},{7,6},{8,9},{9,8},{10,11... | collective-permute-start | bytes 1179656 | tf_op jit(solution)/shard_map/ppermute | solution.py:367
  56.9 21.4 %copy-start = (bf16[4,256,2,256]{3,2,1,0:T(2,128)(2,1)S(1)}, bf16[4,256,2,256]{3,2,1,0:T(2,128)(2,1)}, u32[]{:S(2)}) copy-start(bf16[4,256,2,256]{3,2,1,0:T(2,128)(2,1)} %param.56) | copy-start | bytes 3145732
  67.3 7.6 %collective-permute-start.22 = (bf16[96,512]{1,0:T(8,128)(2,1)S(1)}, bf16[96,512]{1,0:T(8,128)(2,1)S(1)}, u32[]{:S(2)}, u32[]{:S(2)}) collective-permute-start(bf16[96,512]{1,0:T(8,128)(2,1)S(1)} %get-tuple-element.555), channel_id=1, source_target_pairs={{0,8},{8,16},{16,24},{24,0},{1,9},{9,17},{17,25},{25,1},{2,10},{10... | collective-permute-start | bytes 294920 | tf_op jit(solution)/shard_map/ppermute | solution.py:427
  67.8 10.5 %collective-permute-start.23 = (bf16[96,512]{1,0:T(8,128)(2,1)S(1)}, bf16[96,512]{1,0:T(8,128)(2,1)S(1)}, u32[]{:S(2)}, u32[]{:S(2)}) collective-permute-start(bf16[96,512]{1,0:T(8,128)(2,1)S(1)} %get-tuple-element.554), channel_id=1, source_target_pairs={{0,16},{8,24},{16,0},{24,8},{1,17},{9,25},{17,1},{25,9},{2,18},{10... | collective-permute-start | bytes 294920 | tf_op jit(solution)/shard_map/ppermute | solution.py:427
  70.4 7.9 %collective-permute-start.24 = (bf16[96,512]{1,0:T(8,128)(2,1)S(1)}, bf16[96,512]{1,0:T(8,128)(2,1)S(1)}, u32[]{:S(2)}, u32[]{:S(2)}) collective-permute-start(bf16[96,512]{1,0:T(8,128)(2,1)S(1)} %get-tuple-element.553), channel_id=1, source_target_pairs={{0,24},{8,0},{16,8},{24,16},{1,25},{9,1},{17,9},{25,17},{2,26},{10... | collective-permute-start | bytes 294920 | tf_op jit(solution)/shard_map/ppermute | solution.py:427
  79.6 1.0 %copy-start.6 = (bf16[4,256,2,256]{3,2,1,0:T(2,128)(2,1)}, bf16[4,256,2,256]{3,2,1,0:T(2,128)(2,1)S(1)}, u32[]{:S(2)}) copy-start(bf16[4,256,2,256]{3,2,1,0:T(2,128)(2,1)S(1)} %get-tuple-element.955) | copy-start | bytes 3145732

commit v3 on v2

--- a/solution.py
+++ b/solution.py
@@ -11,7 +11,7 @@
 F32 = jnp.float32
 I32 = jnp.int32
 VMEM_BYTES = 44 * 1024 * 1024
-MOVE_ROWS = 96
+MOVE_ROWS = 80
 MOVE_SLOTS = 128
 
 
@@ -157,9 +157,10 @@
         )
         base = base + jnp.sum(jnp.where(member[t], 1.0, 0.0), axis=1, keepdims=True)
     for t in range(steps):
-        meta_ref[t : t + 1, :] = owners[t] * cap + ranks[t]
+        meta_ref[t : t + 1, :] = owners[t]
+        meta_ref[steps + t : steps + t + 1, :] = ranks[t]
     over = jnp.max(base, axis=0, keepdims=True).astype(I32)
-    meta_ref[steps : steps + 1, :] = jnp.broadcast_to(over, (1, nb))
+    meta_ref[2 * steps : 2 * steps + 1, :] = jnp.broadcast_to(over, (1, nb))
     slot = iota((cap, nb), 0)
     total = jnp.zeros((cap, nb), I32)
     for t in range(steps):
@@ -171,7 +172,7 @@
     pack1_ref[...] = dot(chosen, mat_ref[1]).astype(BF16)
 
 
-def move_kernel(cfg, piv_ref, meta_ref, move_ref):
+def find_moves(cfg, piv_ref, meta_ref, move_ref):
     nb, steps, n_row, cap = cfg
     piv = [piv_ref[t : t + 1, :] for t in range(steps)]
     cols = [to_col(piv[t], nb) for t in range(steps)]
@@ -199,101 +200,129 @@
         ).astype(I32)
         most = jnp.maximum(most, jnp.sum(jnp.where(member[t], 1.0, 0.0), axis=1, keepdims=True))
     over = jnp.max(most, axis=0, keepdims=True).astype(I32)
-    bad = (over > MOVE_ROWS) | (meta_ref[steps : steps + 1, :] > cap)
+    bad = (over > MOVE_ROWS) | (meta_ref[2 * steps : 2 * steps + 1, :] > cap)
     move_ref[3 * steps : 3 * steps + 1, :] = jnp.where(bad, 1, 0)
 
 
-def order_rows(meta_ref, buf_ref, t, nb):
-    pos = to_col(meta_ref[t : t + 1, :], nb)
-    hot = one_hot(pos == iota((nb, buf_ref.shape[0]), 1))
+def order_rows(pos, buf_ref):
+    nb = pos.shape[1]
+    hot = one_hot(to_col(pos, nb) == iota((nb, buf_ref.shape[0]), 1))
     return dot(hot, buf_ref[...]).astype(BF16)
 
 
 def order_kernel(cfg, meta_ref, buf_ref, top_ref, off_ref):
-    nb, steps = cfg
+    nb, steps, cap = cfg
     my_col = lax.axis_index("pcol")
     for t in range(steps):
-        top_ref[t * nb : (t + 1) * nb, :] = order_rows(meta_ref, buf_ref, t, nb)
+        pos = meta_ref[t : t + 1, :] * cap + meta_ref[steps + t : steps + t + 1, :]
+        top_ref[t * nb : (t + 1) * nb, :] = order_rows(pos, buf_ref)
     for j in range(steps - 1):
         block = jnp.where(my_col <= j, j + 1, j)
         rows = pl.ds(pl.multiple_of(block * nb, nb), nb)
         off_ref[j * nb : (j + 1) * nb, :] = top_ref[rows, :]
 
 
-def factor_kernel(
-    cfg, meta_ref, move_ref, top0_ref, buf1_ref, mat_ref, raw_0, raw_2, raw_1, raw_3,
-    off_0, off_2, off_1, off_3, linv_ref, uinv_ref, res_ref, top_ref, send_ref, raw, off, l_own, l_top, u_top, upper, first,
-    diag, sems,
-):
-    nb, steps, n_row, local_rows = cfg
-    my_row = lax.axis_index("prow")
-    my_col = lax.axis_index("pcol")
-    low = my_col & 3
+def late_kernel(cfg, piv_ref, meta_ref, buf_ref, move_ref, top_ref):
+    nb, steps, n_row, cap = cfg
+    find_moves(cfg, piv_ref, meta_ref, move_ref)
+    for t in range(steps):
+        pos = meta_ref[t : t + 1, :] * cap + meta_ref[steps + t : steps + t + 1, :]
+        top_ref[t * nb : (t + 1) * nb, :] = order_rows(pos, buf_ref)
+
+
+def fetch(panels, into, sems, first, rows):
+    low = lax.axis_index("pcol") & 3
     copies = [
-        pltpu.make_async_copy(src, dst.at[low ^ mask], sems.at[i])
-        for i, (src, dst, mask) in enumerate(
-            [(off_0, off, 0), (off_1, off, 1), (off_2, off, 2), (off_3, off, 3)]
-            + [(raw_0, raw, 0), (raw_1, raw, 1), (raw_2, raw, 2), (raw_3, raw, 3)]
-        )
+        pltpu.make_async_copy(panel.at[rows], into.at[low ^ mask], sems.at[first + mask])
+        for mask, panel in enumerate(panels)
     ]
     for c in copies:
         c.start()
+    return copies
+
+
+def corner_kernel(
+    cfg, move_ref, top0_ref, top1_ref, mat_ref, raws, offs, linv_ref, uinv_ref,
+    upper, res_ref, top_ref, send_ref, raw, off, left, diag, sems,
+):
+    nb, steps, n_row = cfg
     wide = steps * nb
-    for t in range(steps):
-        first[t * nb : (t + 1) * nb, :nb] = top0_ref[t * nb : (t + 1) * nb, :]
-        first[t * nb : (t + 1) * nb, nb:] = order_rows(meta_ref, buf1_ref, t, nb)
+    my_row = lax.axis_index("prow")
+    my_col = lax.axis_index("pcol")
+    copies = fetch(offs, off, sems, 0, pl.ds(0, wide - nb))
+    copies += fetch(raws, raw, sems, 4, pl.ds(0, nb))
     for c in copies:
         c.wait()
     for t in range(steps):
         here = slice(t * nb, (t + 1) * nb)
         done = slice(0, t * nb)
-        for s in range(t):
-            sel = slice(s * nb, (s + 1) * nb)
-            acc = off[t, sel, :].astype(F32)
-            if s > 0:
-                acc = acc - dot(l_top[sel, : s * nb], u_top[: s * nb, here])
-            u_top[sel, here] = dot(linv_ref[s], acc.astype(BF16)).astype(BF16)
-        if t < steps - 1:
-            acc = off[t, t * nb :, :].astype(F32)
-            if t > 0:
-                acc = acc - dot(l_top[(t + 1) * nb :, done], u_top[done, here])
-            l_top[(t + 1) * nb :, here] = dot(acc.astype(BF16), uinv_ref[t]).astype(BF16)
-        for k in range(local_rows // nb):
-            rows = slice(k * nb, (k + 1) * nb)
-            acc = raw[t, rows, :].astype(F32)
-            if t > 0:
-                acc = acc - dot(l_own[rows, done], u_top[done, here])
-            l_own[rows, here] = dot(acc.astype(BF16), uinv_ref[t]).astype(BF16)
-        acc = first[here, :].astype(F32)
+        parts = [off[j, here, :] for j in range(t + 1, steps)]
+        parts += [top0_ref[here, :], top1_ref[here, :]]
+        column = [off[t, t * nb :, :]] if t < steps - 1 else []
+        column += [raw[t]]
         if t > 0:
-            acc = acc - dot(l_top[here, done], upper[done, :])
-        acc = acc.astype(BF16)
-        diag[here, :] = acc[:, :nb]
-        upper[here, :] = dot(linv_ref[t], acc).astype(BF16)
+            prod = dot(left[here, done], upper[done, (t + 1) * nb :])
+            parts = [
+                (p.astype(F32) - prod[:, i * nb : (i + 1) * nb]).astype(BF16)
+                for i, p in enumerate(parts)
+            ]
+            prod = dot(left[(t + 1) * nb :, done], upper[done, here])
+            at = 0
+            for i, p in enumerate(column):
+                rows = p.shape[0]
+                column[i] = (p.astype(F32) - prod[at : at + rows]).astype(BF16)
+                at += rows
+        diag[here, :] = parts[-2]
+        upper[here, (t + 1) * nb :] = dot(linv_ref[t], jnp.concatenate(parts, axis=1)).astype(BF16)
+        left[(t + 1) * nb :, here] = dot(jnp.concatenate(column, axis=0), uinv_ref[t]).astype(BF16)
     in_panel = my_col < steps
     panel = pl.ds(pl.multiple_of(jnp.minimum(my_col, steps - 1) * nb, nb), nb)
-    for k in range(local_rows // nb):
-        rows = slice(k * nb, (k + 1) * nb)
-        prod = dot(l_own[rows, :], upper[...])
-        left = (mat_ref[0, rows, :].astype(F32) - prod[:, :nb]).astype(BF16)
-        res_ref[rows, :nb] = jnp.where(in_panel, l_own[rows, panel], left)
-        res_ref[rows, nb:] = (mat_ref[1, rows, :].astype(F32) - prod[:, nb:]).astype(BF16)
-    block = pl.ds(pl.multiple_of(jnp.minimum(my_row, steps - 1) * nb, nb), nb)
-    own_upper = upper[block, :]
-    left = jnp.where(my_col == my_row, diag[block, :], own_upper[:, :nb])
-    left = jnp.where(in_panel & (my_col < my_row), l_top[block, panel], left)
-    top_ref[:, :nb] = left
-    top_ref[:, nb:] = own_upper[:, nb:]
+    prod = dot(left[wide:, :], upper[:, wide:])
+    value = (mat_ref[0, :nb, :].astype(F32) - prod[:, :nb]).astype(BF16)
+    res_ref[:, :nb] = jnp.where(in_panel, left[wide:, panel], value)
+    res_ref[:, nb:] = (mat_ref[1, :nb, :].astype(F32) - prod[:, nb:]).astype(BF16)
     here = iota((steps, nb), 0) == my_row
     dest = jnp.sum(jnp.where(here, move_ref[:steps, :] + 1, 0), axis=0, keepdims=True) - 1
     rank = jnp.sum(jnp.where(here, move_ref[steps : 2 * steps, :], 0), axis=0, keepdims=True)
     for k in range(n_row):
         key = jnp.where(dest == lax.rem(my_row + k, n_row), rank, -1)
         hot = one_hot(key == iota((MOVE_ROWS, nb), 0))
-        send_ref[k] = dot(hot, res_ref[:nb, :]).astype(BF16)
-
-
-def place_kernel(cfg, move_ref, res_ref, top_ref, *refs):
+        send_ref[k] = dot(hot, res_ref[...]).astype(BF16)
+    block = pl.ds(pl.multiple_of(jnp.minimum(my_row, steps - 1) * nb, nb), nb)
+    value = jnp.where(my_col == my_row, diag[block, :], upper[block, wide : wide + nb])
+    value = jnp.where(in_panel & (my_col < my_row), left[block, panel], value)
+    top_ref[:, :nb] = value
+    top_ref[:, nb:] = upper[block, wide + nb :]
+
+
+def rows_kernel(
+    cfg, mat_ref, raws, upper, uinv_ref, res_ref, raw, l_own, sems
+):
+    nb, steps, local_rows = cfg
+    my_col = lax.axis_index("pcol")
+    copies = fetch(raws, raw, sems, 0, pl.ds(nb, local_rows - nb))
+    for c in copies:
+        c.wait()
+    tiles = [slice(k * nb, (k + 1) * nb) for k in range(local_rows // nb - 1)]
+    for t in range(steps):
+        here = slice(t * nb, (t + 1) * nb)
+        done = slice(0, t * nb)
+        for rows in tiles:
+            acc = raw[t, rows, :].astype(F32)
+            if t > 0:
+                acc = acc - dot(l_own[rows, done], upper[done, here])
+            l_own[rows, here] = dot(acc.astype(BF16), uinv_ref[t]).astype(BF16)
+    in_panel = my_col < steps
+    panel = pl.ds(pl.multiple_of(jnp.minimum(my_col, steps - 1) * nb, nb), nb)
+    for rows in tiles:
+        prod = dot(l_own[rows, :], upper[:, steps * nb :])
+        source = slice(rows.start + nb, rows.stop + nb)
+        left = (mat_ref[0, source, :].astype(F32) - prod[:, :nb]).astype(BF16)
+        res_ref[rows, :nb] = jnp.where(in_panel, l_own[rows, panel], left)
+        res_ref[rows, nb:] = (mat_ref[1, source, :].astype(F32) - prod[:, nb:]).astype(BF16)
+
+
+def place_kernel(cfg, move_ref, head_ref, res_ref, top_ref, *refs):
     nb, steps, n_row, local_rows = cfg
     recv, out_ref, slots = refs[:n_row], refs[n_row], refs[n_row + 1]
     my_row = lax.axis_index("prow")
@@ -324,22 +353,28 @@
         hit = iota((nb, n_row * MOVE_SLOTS), 0) + k * nb == target
         moved = dot(one_hot(hit), slots[...]).astype(BF16)
         any_hit = jnp.sum(jnp.where(hit, 1.0, 0.0), axis=1, keepdims=True) > 0.5
-        value = jnp.where(any_hit, moved, res_ref[rows, :])
         if k == 0:
+            value = jnp.where(any_hit, moved, head_ref[...])
             value = jnp.where(my_row < steps, top_ref[...], value)
+        else:
+            value = jnp.where(any_hit, moved, res_ref[(k - 1) * nb : k * nb, :])
         out_ref[rows, :] = value
 
 
-def call(kernel, outs, ins, scratch=(), any_at=()):
+def call(kernel, outs, ins, scratch=(), any_at=(), flops=None):
     vmem = pl.BlockSpec(memory_space=pltpu.VMEM)
     anywhere = pl.BlockSpec(memory_space=pl.ANY)
     return pl.pallas_call(
         kernel,
         out_shape=outs,
-        in_specs=[anywhere if i in any_at else vmem for i in range(len(ins))],
+        in_specs=[
+            jax.tree.map(lambda _: anywhere if i in any_at else vmem, x) for i, x in enumerate(ins)
+        ],
         out_specs=jax.tree.map(lambda _: vmem, outs),
         scratch_shapes=list(scratch),
         compiler_params=pltpu.CompilerParams(vmem_limit_bytes=VMEM_BYTES),
+        cost_estimate=flops
+        and pl.CostEstimate(flops=flops, bytes_accessed=1 << 22, transcendentals=0),
     )(*ins)
 
 
@@ -354,7 +389,6 @@
     n_col = lax.axis_size("pcol")
     if steps != 4 or col_blocks != 2 or n_row < steps or n_col < 8 or n_col % 4:
         return stepwise(matrix, pivots, lower_inverse, upper_inverse)
-    my_col = lax.axis_index("pcol")
     local_rows = row_blocks * nb
     cap = -(-(steps * nb // n_row + 64) // 16) * 16
     mat = jnp.transpose(matrix, (2, 0, 1, 3)).reshape(col_blocks, local_rows, nb)
@@ -366,73 +400,83 @@
     def swap_cores(value):
         return lax.ppermute(value, "pcol", [(i, i ^ 1) for i in range(n_col)])
 
-    on_panel = my_col < steps
+    def panel_pair(own, beside, far, far_beside):
+        return jnp.where(on_panel, own, far), jnp.where(on_panel, beside, far_beside)
+
+    on_panel = lax.axis_index("pcol") < steps
     fours = range(4, n_col, 4)
     raw_x = from_panels(m0, 2)
     raw_far = functools.reduce(jnp.add, [from_panels(m0, mask) for mask in fours])
 
     meta, pack0, pack1 = call(
         functools.partial(pick_kernel, (nb, steps, n_row, cap, local_rows)),
-        (shape(8, nb, dtype=I32), shape(cap, nb), shape(cap, nb)),
+        (shape(16, nb, dtype=I32), shape(cap, nb), shape(cap, nb)),
         (pivots, mat),
     )
     buf0 = lax.all_gather(pack0, "prow", tiled=True)
     buf0, raw_x, raw_far = lax.optimization_barrier((buf0, raw_x, raw_far))
     top0, off = call(
-        functools.partial(order_kernel, (nb, steps)),
+        functools.partial(order_kernel, (nb, steps, cap)),
         (shape(steps * nb, nb), shape((steps - 1) * nb, nb)),
         (meta, buf0),
     )
-    pack1, off = lax.optimization_barrier((pack1, off))
+    pack1, off, raw_far = lax.optimization_barrier((pack1, off, raw_far))
     off_x = from_panels(off, 2)
     off_far = functools.reduce(jnp.add, [from_panels(off, mask) for mask in fours])
     off_far_x = functools.reduce(jnp.add, [from_panels(off, mask + 2) for mask in fours])
     raw_far_x = lax.ppermute(raw_far, "pcol", [(i, i ^ 2) for i in range(steps, n_col)])
     buf1 = lax.all_gather(pack1, "prow", tiled=True)
-    move = call(
-        functools.partial(move_kernel, (nb, steps, n_row, cap)),
-        shape(16, nb, dtype=I32),
-        (pivots, meta),
-    )
-    buf1, off_far, raw_far_x = lax.optimization_barrier((buf1, off_far, raw_far_x))
-    raw_0 = jnp.where(on_panel, m0, raw_far)
-    raw_2 = jnp.where(on_panel, raw_x, raw_far_x)
-    off_0 = jnp.where(on_panel, off, off_far)
-    raw_1, raw_3, off_1 = swap_cores(raw_0), swap_cores(raw_2), swap_cores(off_0)
-    buf1, off_x, off_far_x = lax.optimization_barrier((buf1, off_x, off_far_x))
-    off_2 = jnp.where(on_panel, off_x, off_far_x)
-    off_3 = swap_cores(off_2)
+    buf1, off_far, off_x, off_far_x = lax.optimization_barrier((buf1, off_far, off_x, off_far_x))
+    raw_0, raw_2 = panel_pair(m0, raw_x, raw_far, raw_far_x)
+    off_0, off_2 = panel_pair(off, off_x, off_far, off_far_x)
+    raws = (raw_0, swap_cores(raw_0), raw_2, swap_cores(raw_2))
+    offs = (off_0, swap_cores(off_0), off_2, swap_cores(off_2))
+    move, top1 = call(
+        functools.partial(late_kernel, (nb, steps, n_row, cap)),
+        (shape(16, nb, dtype=I32), shape(steps * nb, nb)),
+        (pivots, meta, buf1),
+    )
     top_rows = steps * nb
-    res, top, send = call(
-        functools.partial(factor_kernel, (nb, steps, n_row, local_rows)),
-        (shape(local_rows, 2 * nb), shape(nb, 2 * nb), shape(n_row, MOVE_ROWS, 2 * nb)),
+    upper, head, top, send = call(
+        functools.partial(corner_kernel, (nb, steps, n_row)),
         (
-            meta, move, top0, buf1, mat, raw_0, raw_2, raw_1, raw_3, off_0, off_2, off_1, off_3,
-            lower_inverse, upper_inverse,
+            shape(top_rows, top_rows + 2 * nb), shape(nb, 2 * nb), shape(nb, 2 * nb),
+            shape(n_row, MOVE_ROWS, 2 * nb),
         ),
+        (move, top0, top1, mat, raws, offs, lower_inverse, upper_inverse),
         scratch=(
-            pltpu.VMEM((steps, local_rows, nb), BF16),
+            pltpu.VMEM((steps, nb, nb), BF16),
             pltpu.VMEM((steps, top_rows - nb, nb), BF16),
-            pltpu.VMEM((local_rows, top_rows), BF16),
-            pltpu.VMEM((top_rows, top_rows), BF16),
-            pltpu.VMEM((top_rows, top_rows), BF16),
-            pltpu.VMEM((top_rows, 2 * nb), BF16),
-            pltpu.VMEM((top_rows, 2 * nb), BF16),
+            pltpu.VMEM((top_rows + nb, top_rows), BF16),
             pltpu.VMEM((top_rows, nb), BF16),
             pltpu.SemaphoreType.DMA((8,)),
         ),
-        any_at=range(5, 13),
+        any_at=(4, 5),
     )
     recv = [send[0]] + [
         lax.ppermute(send[k], "prow", [(i, (i + k) % n_row) for i in range(n_row)])
         for k in range(1, n_row)
     ]
 
+    below = local_rows - nb
+    res = call(
+        functools.partial(rows_kernel, (nb, steps, local_rows)),
+        shape(below, 2 * nb),
+        (mat, raws, upper, upper_inverse),
+        scratch=(
+            pltpu.VMEM((steps, below, nb), BF16),
+            pltpu.VMEM((below, top_rows), BF16),
+            pltpu.SemaphoreType.DMA((4,)),
+        ),
+        any_at=(1,),
+        flops=2 * below * top_rows * (top_rows + 2 * nb),
+    )
+
     def finish():
         out = call(
             functools.partial(place_kernel, (nb, steps, n_row, local_rows)),
             shape(local_rows, 2 * nb),
-            (move, res, top, *recv),
+            (move, head, res, top, *recv),
             scratch=(pltpu.VMEM((n_row * MOVE_SLOTS, 2 * nb), BF16),),
         )
         return out.reshape(matrix.shape)

time: 80.9 us -> 74.7 us (0.923)
  waiting for transfers between devices: 7.2 us -> 2.45 us
  starting transfers between devices: 18.8 us -> 17.7 us
    ppermute x3, waiting for transfers between devices: 5.98 us -> 2.43 us  [local(): lax.ppermute(send[k], 'prow', [(i, (i + k) % n_row) for i in range(n_row)])]
    ppermute x4, waiting for transfers between devices: 1.2 us -> 0.01 us  [swap_cores(): return lax.ppermute(value, 'pcol', [(i, i ^ 1) for i in range(n_col)])]
    pallas_call x5 -> x6, Pallas kernels: 14.5 us -> 14.1 us  [call(): pl.pallas_call(kernel, out_shape=outs, in_specs=[jax.tree.map(lambda _: a...]
    unnamed x13 -> x9, local copies, waits for them, and re-layouts: 2.35 us -> 2.35 us
  transfers between devices with their start and end apart: 13 -> 13, of which waited for: 3 -> 1; matrix products, arithmetic and copies ran while one was open for 1% -> 1% of each run, Pallas kernels for 4% -> 9%
where the time goes in v3:
time: 74.7 us; the launch traced here: 74.4 us
  blocking collectives  35.7 us (48%)
  starting transfers between devices  17.7 us (24%)
  Pallas kernels  14.1 us (19%)
  local copies, waits for them, and re-layouts  3.21 us (4%)
  waiting for transfers between devices  2.45 us (3%)
  between operations  0.88 us (1%)
    all_gather x1, blocking collectives, local(): buf0 = lax.all_gather(pack0, 'prow', tiled=True)  18.1 us
    all_gather x1, blocking collectives, local(): buf1 = lax.all_gather(pack1, 'prow', tiled=True)  17.7 us
    pallas_call x6, Pallas kernels, call(): pl.pallas_call(kernel, out_shape=outs, in_specs=[jax.tree.map(lambda _: a...  14.1 us
    ppermute x5, starting transfers between devices, from_panels(): return lax.ppermute(value, 'pcol', [(i, i ^ mask) for i in range(steps)])  12.4 us
    ppermute x3, starting transfers between devices, local(): lax.ppermute(send[k], 'prow', [(i, (i + k) % n_row) for i in range(n_row)])  3.88 us
    ppermute x3, waiting for transfers between devices, local(): lax.ppermute(send[k], 'prow', [(i, (i + k) % n_row) for i in range(n_row)])  2.43 us
    unnamed x9, local copies, waits for them, and re-layouts  2.35 us
  transfers between devices with their start and end apart: 13, of which 1 were waited for; matrix products, arithmetic and copies ran while one was open for 1% of the time, Pallas kernels for 9%

profile of v3, /device:TPU:0, one launch (start us, length us, event | category | flops | bytes accessed | tf_op | source)
XLA Modules:
  0.0 74.4 jit_solution(4497440871132702055)
XLA Ops:
  0.0 0.0 copy-start.3
  0.0 1.4 %copy.25 = bf16[4,256,2,256]{3,1,0,2:T(8,128)(2,1)S(1)} copy(bf16[4,256,2,256]{3,2,1,0:T(2,128)(2,1)} %param.56) | data formatting | bytes 2097152 | tf_op args[0]
  1.4 4.8 %collective-permute-start.12 = (bf16[1024,256]{1,0:T(8,128)(2,1)S(1)}, bf16[1024,256]{1,0:T(8,128)(2,1)S(1)}, u32[]{:S(2)}, u32[]{:S(2)}) collective-permute-start(bf16[1024,256]{1,0:T(8,128)(2,1)S(1)} %bitcast.143), channel_id=1, source_target_pairs={{0,2},{1,3},{2,0},{3,1},{8,10},{9,11},{10,8},{11,9},{16,18},{17,19... | collective-permute-start | bytes 1572872 | tf_op jit(solution)/shard_map/ppermute | solution.py:398
  6.3 2.1 %collective-permute-start.13 = (bf16[1024,256]{1,0:T(8,128)(2,1)S(1)}, bf16[1024,256]{1,0:T(8,128)(2,1)}, u32[]{:S(2)}, u32[]{:S(2)}) collective-permute-start(bf16[1024,256]{1,0:T(8,128)(2,1)S(1)} %bitcast.144), channel_id=1, source_target_pairs={{0,4},{1,5},{2,6},{3,7},{8,12},{9,13},{10,14},{11,15},{16,20},{17,... | collective-permute-start | bytes 1572872 | tf_op jit(solution)/shard_map/ppermute | solution.py:398
  8.4 0.0 copy-done.3
  8.4 1.2 %shard_map.48 = (s32[16,256]{1,0:T(8,128)S(1)}, bf16[320,256]{1,0:T(8,128)(2,1)S(1)}, bf16[320,256]{1,0:T(8,128)(2,1)S(1)}) custom-call(s32[4,256]{1,0:T(4,128)S(1)} %copy-done.3, bf16[2,1024,256]{2,1,0:T(8,128)(2,1)S(1)} %bitcast.135), custom_call_target="tpu_custom_call" | custom-call | tf_op jit(solution)/shard_map/pallas_call | solution.py:367
  9.6 18.1 %all_gather.6.buf_ref = bf16[1280,256]{1,0:T(8,128)(2,1)S(1)} all-gather(bf16[320,256]{1,0:T(8,128)(2,1)S(1)} %get-tuple-element.418), channel_id=1, replica_groups=mesh['prow'=4,'pcol'=8] {'prow'}, dimensions={0}, use_global_device_ids=true | all-gather | bytes 819200 | tf_op jit(solution)/shard_map/all_gather | solution.py:416
  27.7 0.0 collective-permute-done.12
  27.7 0.0 collective-permute-done.13
  27.7 1.1 %shard_map.49 = (bf16[1024,256]{1,0:T(8,128)(2,1)S(1)}, bf16[768,256]{1,0:T(8,128)(2,1)S(1)}) custom-call(s32[16,256]{1,0:T(8,128)S(1)} %get-tuple-element.416.meta_ref, bf16[1280,256]{1,0:T(8,128)(2,1)S(1)} %all_gather.6.buf_ref), custom_call_target="tpu_custom_call" | custom-call | tf_op jit(solution)/shard_map/pallas_call | solution.py:367
  28.8 1.3 %collective-permute-start.14 = (bf16[768,256]{1,0:T(8,128)(2,1)S(1)}, bf16[768,256]{1,0:T(8,128)(2,1)S(1)}, u32[]{:S(2)}, u32[]{:S(2)}) collective-permute-start(bf16[768,256]{1,0:T(8,128)(2,1)S(1)} %get-tuple-element.423), channel_id=1, source_target_pairs={{0,4},{1,5},{2,6},{3,7},{8,12},{9,13},{10,14},{11,15},{16,20},{17,... | collective-permute-start | bytes 1179656 | tf_op jit(solution)/shard_map/ppermute | solution.py:398
  30.1 2.8 %collective-permute-start.15 = (bf16[768,256]{1,0:T(8,128)(2,1)S(1)}, bf16[768,256]{1,0:T(8,128)(2,1)S(1)}, u32[]{:S(2)}, u32[]{:S(2)}) collective-permute-start(bf16[768,256]{1,0:T(8,128)(2,1)S(1)} %get-tuple-element.423), channel_id=1, source_target_pairs={{0,2},{1,3},{2,0},{3,1},{8,10},{9,11},{10,8},{11,9},{16,18},{17,19... | collective-permute-start | bytes 1179656 | tf_op jit(solution)/shard_map/ppermute | solution.py:398
  32.9 1.3 %collective-permute-start.16 = (bf16[768,256]{1,0:T(8,128)(2,1)S(1)}, bf16[768,256]{1,0:T(8,128)(2,1)S(1)}, u32[]{:S(2)}, u32[]{:S(2)}) collective-permute-start(bf16[768,256]{1,0:T(8,128)(2,1)S(1)} %get-tuple-element.423), channel_id=1, source_target_pairs={{0,6},{1,7},{2,4},{3,5},{8,14},{9,15},{10,12},{11,13},{16,22},{17,... | collective-permute-start | bytes 1179656 | tf_op jit(solution)/shard_map/ppermute | solution.py:398
  34.3 0.7 collective-permute-start.18
  35.0 0.1 broadcast_select_fusion.5.raws_0_
  35.1 0.1 collective-permute-start.17
  35.2 17.7 %all_gather.7.buf_ref = bf16[1280,256]{1,0:T(8,128)(2,1)S(1)} all-gather(bf16[320,256]{1,0:T(8,128)(2,1)S(1)} %get-tuple-element.422), channel_id=1, replica_groups=mesh['prow'=4,'pcol'=8] {'prow'}, dimensions={0}, use_global_device_ids=true | all-gather | bytes 819200 | tf_op jit(solution)/shard_map/all_gather | solution.py:428
  52.8 0.0 copy-start.1
  52.8 0.0 collective-permute-done.14
  52.8 0.0 collective-permute-done.15
  52.8 0.0 collective-permute-done.16
  52.9 0.1 collective-permute-start.21
  53.0 0.0 collective-permute-done.18
  53.0 0.1 broadcast_select_fusion.4.raws_2_
  53.0 0.5 collective-permute-start.19
  53.6 0.1 collective-permute-start.20
  53.7 1.8 %shard_map.50 = (s32[16,256]{1,0:T(8,128)S(1)}, bf16[1024,256]{1,0:T(8,128)(2,1)S(1)}) custom-call(s32[4,256]{1,0:T(4,128)S(1)} %copy-done.3, s32[16,256]{1,0:T(8,128)S(1)} %get-tuple-element.416.meta_ref, bf16[1280,256]{1,0:T(8,128)(2,1)S(1)} %all_gather.7.buf_ref), custom_call_target="tpu_custom_call" | custom-call | tf_op jit(solution)/shard_map/pallas_call | solution.py:367
  55.5 0.5 slice.316
  56.7 0.0 collective-permute-done.17.raws_1_
  56.7 0.0 collective-permute-done.21.offs_3_
  56.7 0.0 collective-permute-done.20.offs_1_
  56.7 0.0 collective-permute-done.19.raws_3_
  56.7 0.0 copy-done.1
  56.7 5.2 %shard_map.51 = (bf16[1024,1536]{1,0:T(8,128)(2,1)S(1)}, bf16[256,512]{1,0:T(8,128)(2,1)S(1)}, bf16[256,512]{1,0:T(8,128)(2,1)S(1)}, bf16[4,80,512]{2,1,0:T(8,128)(2,1)S(1)}) custom-call(s32[16,256]{1,0:T(8,128)S(1)} %get-tuple-element.425.move_ref, bf16[1024,256]{1,0:T(8,128)(2,1)S(1)} %get-tuple-element.426.top0_ref, ...), custom_call_target="tpu_custom_call" | custom-call | tf_op jit(solution)/shard_map/pallas_call | solution.py:367
  61.9 0.5 collective-permute-start.22
  62.4 2.6 %collective-permute-start.23 = (bf16[80,512]{1,0:T(8,128)(2,1)S(1)}, bf16[80,512]{1,0:T(8,128)(2,1)S(1)}, u32[]{:S(2)}, u32[]{:S(2)}) collective-permute-start(bf16[80,512]{1,0:T(8,128)(2,1)S(1)} %get-tuple-element.561), channel_id=1, source_target_pairs={{0,16},{8,24},{16,0},{24,8},{1,17},{9,25},{17,1},{25,9},{2,18},{10... | collective-permute-start | bytes 245768 | tf_op jit(solution)/shard_map/ppermute | solution.py:457
  65.0 0.8 %collective-permute-start.24 = (bf16[80,512]{1,0:T(8,128)(2,1)S(1)}, bf16[80,512]{1,0:T(8,128)(2,1)S(1)}, u32[]{:S(2)}, u32[]{:S(2)}) collective-permute-start(bf16[80,512]{1,0:T(8,128)(2,1)S(1)} %get-tuple-element.560), channel_id=1, source_target_pairs={{0,24},{8,0},{16,8},{24,16},{1,25},{9,1},{17,9},{25,17},{2,26},{10... | collective-permute-start | bytes 245768 | tf_op jit(solution)/shard_map/ppermute | solution.py:457
  65.8 0.0 copy-start
  65.8 3.8 %shard_map.52 = bf16[768,512]{1,0:T(8,128)(2,1)S(1)} custom-call(bf16[2,1024,256]{2,1,0:T(8,128)(2,1)S(1)} %bitcast.137, bf16[1024,256]{1,0:T(8,128)(2,1)S(1)} %broadcast_select_fusion.5.raws_0_, bf16[1024,256]{1,0:T(8,128)(2,1)S(1)} %collective-permute-done.17.raws_1_, bf16[1024,256]{1,0:T(8,128)(2,1)S(1)} %broadcast_select_fusion.4.raws_2_, ...), custom_call_target="tpu_custom_call" | custom-call | flops 2415919104 | bytes 4194304 | tf_op jit(solution)/shard_map/pallas_call | solution.py:367
  69.7 0.0 collective-permute-done.22
  69.7 2.4 %collective-permute-done.23 = bf16[80,512]{1,0:T(8,128)(2,1)S(1)} collective-permute-done((bf16[80,512]{1,0:T(8,128)(2,1)S(1)}, bf16[80,512]{1,0:T(8,128)(2,1)S(1)}, u32[]{:S(2)}, u32[]{:S(2)}) %collective-permute-start.23) | collective-permute-done | bytes 81952 | tf_op jit(solution)/shard_map/ppermute | solution.py:457
  72.1 0.0 collective-permute-done.24
  72.1 0.0 copy-done
  72.1 1.3 %conditional.1 = (bf16[4,256,2,256]{3,2,1,0:T(2,128)(2,1)S(1)}) conditional(s32[]{:T(128)} %bitcast.28, (bf16[4,80,512]{2,1,0:T(8,128)(2,1)S(1)}, s32[16,256]{1,0:T(8,128)S(1)}, bf16[256,512]{1,0:T(8,128)(2,1)S(1)}, bf16[768,512]{1,0:T(8,128)(2,1)S(1)}, bf16[256,512]{1,0:T(8,128)(2,1)S(1)}, /*index=5*/bf16[80,512]{1,0:T(8,128)(2,1)S(1)}, ...), branch_computations={%region_0.1_spmd, %region_1.32_spmd} | conditional | flops 1896568576 | bytes 95241984 | solution.py:484
  72.1 0.9 %branch_0_fun.1 = bf16[1024,512]{1,0:T(8,128)(2,1)S(1)} custom-call(s32[16,256]{1,0:T(8,128)S(1)} %get-tuple-element.323.move_ref, bf16[256,512]{1,0:T(8,128)(2,1)S(1)} %get-tuple-element.324.head_ref, bf16[768,512]{1,0:T(8,128)(2,1)S(1)} %get-tuple-element.325.res_ref, bf16[256,512]{1,0:T(8,128)(2,1)S(1)} %get-tuple-element.326.top_ref, ...), custom_call_target="tpu_custom_call" | custom-call | tf_op jit(solution)/shard_map/cond/branch_0_fun/pallas_call | solution.py:367
  73.1 0.3 reshape.1231
  73.4 0.0 copy-start.2
  73.4 1.0 %copy-done.2 = bf16[4,256,2,256]{3,2,1,0:T(2,128)(2,1)} copy-done((bf16[4,256,2,256]{3,2,1,0:T(2,128)(2,1)}, bf16[4,256,2,256]{3,2,1,0:T(2,128)(2,1)S(1)}, u32[]{:S(2)}) %copy-start.2) | copy-done | bytes 1048600
  (5 shorter events, 0.1 us)
Async XLA Ops:
  0.0 8.4 %copy-start.3 = (s32[4,256]{1,0:T(4,128)S(1)}, s32[4,256]{1,0:T(4,128)}, u32[]{:S(2)}) copy-start(s32[4,256]{1,0:T(4,128)} %piv_ref.3) | copy-start | bytes 12292
  1.4 26.3 %collective-permute-start.12 = (bf16[1024,256]{1,0:T(8,128)(2,1)S(1)}, bf16[1024,256]{1,0:T(8,128)(2,1)S(1)}, u32[]{:S(2)}, u32[]{:S(2)}) collective-permute-start(bf16[1024,256]{1,0:T(8,128)(2,1)S(1)} %bitcast.143), channel_id=1, source_target_pairs={{0,2},{1,3},{2,0},{3,1},{8,10},{9,11},{10,8},{11,9},{16,18},{17,19... | collective-permute-start | bytes 1572872 | tf_op jit(solution)/shard_map/ppermute | solution.py:398
  6.3 21.4 %collective-permute-start.13 = (bf16[1024,256]{1,0:T(8,128)(2,1)S(1)}, bf16[1024,256]{1,0:T(8,128)(2,1)}, u32[]{:S(2)}, u32[]{:S(2)}) collective-permute-start(bf16[1024,256]{1,0:T(8,128)(2,1)S(1)} %bitcast.144), channel_id=1, source_target_pairs={{0,4},{1,5},{2,6},{3,7},{8,12},{9,13},{10,14},{11,15},{16,20},{17,... | collective-permute-start | bytes 1572872 | tf_op jit(solution)/shard_map/ppermute | solution.py:398
  28.8 24.0 %collective-permute-start.14 = (bf16[768,256]{1,0:T(8,128)(2,1)S(1)}, bf16[768,256]{1,0:T(8,128)(2,1)S(1)}, u32[]{:S(2)}, u32[]{:S(2)}) collective-permute-start(bf16[768,256]{1,0:T(8,128)(2,1)S(1)} %get-tuple-element.423), channel_id=1, source_target_pairs={{0,4},{1,5},{2,6},{3,7},{8,12},{9,13},{10,14},{11,15},{16,20},{17,... | collective-permute-start | bytes 1179656 | tf_op jit(solution)/shard_map/ppermute | solution.py:398
  30.1 22.7 %collective-permute-start.15 = (bf16[768,256]{1,0:T(8,128)(2,1)S(1)}, bf16[768,256]{1,0:T(8,128)(2,1)S(1)}, u32[]{:S(2)}, u32[]{:S(2)}) collective-permute-start(bf16[768,256]{1,0:T(8,128)(2,1)S(1)} %get-tuple-element.423), channel_id=1, source_target_pairs={{0,2},{1,3},{2,0},{3,1},{8,10},{9,11},{10,8},{11,9},{16,18},{17,19... | collective-permute-start | bytes 1179656 | tf_op jit(solution)/shard_map/ppermute | solution.py:398
  32.9 19.9 %collective-permute-start.16 = (bf16[768,256]{1,0:T(8,128)(2,1)S(1)}, bf16[768,256]{1,0:T(8,128)(2,1)S(1)}, u32[]{:S(2)}, u32[]{:S(2)}) collective-permute-start(bf16[768,256]{1,0:T(8,128)(2,1)S(1)} %get-tuple-element.423), channel_id=1, source_target_pairs={{0,6},{1,7},{2,4},{3,5},{8,14},{9,15},{10,12},{11,13},{16,22},{17,... | collective-permute-start | bytes 1179656 | tf_op jit(solution)/shard_map/ppermute | solution.py:398
  34.3 18.7 %collective-permute-start.18 = (bf16[1024,256]{1,0:T(8,128)(2,1)}, bf16[1024,256]{1,0:T(8,128)(2,1)S(1)}, u32[]{:S(2)}, u32[]{:S(2)}) collective-permute-start(bf16[1024,256]{1,0:T(8,128)(2,1)} %collective-permute-done.13), channel_id=1, source_target_pairs={{4,6},{5,7},{6,4},{7,5},{12,14},{13,15},{14,12},{15,13},{20,22},{2... | collective-permute-start | bytes 1572872 | tf_op jit(solution)/shard_map/ppermute | solution.py:427
  35.1 21.6 %collective-permute-start.17 = (bf16[1024,256]{1,0:T(8,128)(2,1)S(1)}, bf16[1024,256]{1,0:T(8,128)(2,1)S(1)}, u32[]{:S(2)}, u32[]{:S(2)}) collective-permute-start(bf16[1024,256]{1,0:T(8,128)(2,1)S(1)} %broadcast_select_fusion.5.raws_0_), channel_id=1, source_target_pairs={{0,1},{1,0},{2,3},{3,2},{4,5},{5,4},{6,7},{7,6},{8,9},{9,8},{10,11... | collective-permute-start | bytes 1572872 | tf_op jit(solution)/shard_map/ppermute | solution.py:401
  52.8 3.9 %copy-start.1 = (bf16[4,256,256]{2,1,0:T(8,128)(2,1)S(1)}, bf16[4,256,256]{2,1,0:T(8,128)(2,1)}, u32[]{:S(2)}) copy-start(bf16[4,256,256]{2,1,0:T(8,128)(2,1)} %uinv_ref.3) | copy-start | bytes 1572868
  52.9 3.8 %collective-permute-start.21 = (bf16[768,256]{1,0:T(8,128)(2,1)S(1)}, bf16[768,256]{1,0:T(8,128)(2,1)S(1)}, u32[]{:S(2)}, u32[]{:S(2)}) collective-permute-start(bf16[768,256]{1,0:T(8,128)(2,1)S(1)} %broadcast_select_fusion.6.offs_2_), channel_id=1, source_target_pairs={{0,1},{1,0},{2,3},{3,2},{4,5},{5,4},{6,7},{7,6},{8,9},{9,8},{10,11... | collective-permute-start | bytes 1179656 | tf_op jit(solution)/shard_map/ppermute | solution.py:401
  53.0 3.7 %collective-permute-start.19 = (bf16[1024,256]{1,0:T(8,128)(2,1)S(1)}, bf16[1024,256]{1,0:T(8,128)(2,1)S(1)}, u32[]{:S(2)}, u32[]{:S(2)}) collective-permute-start(bf16[1024,256]{1,0:T(8,128)(2,1)S(1)} %broadcast_select_fusion.4.raws_2_), channel_id=1, source_target_pairs={{0,1},{1,0},{2,3},{3,2},{4,5},{5,4},{6,7},{7,6},{8,9},{9,8},{10,11... | collective-permute-start | bytes 1572872 | tf_op jit(solution)/shard_map/ppermute | solution.py:401
  53.6 3.1 %collective-permute-start.20 = (bf16[768,256]{1,0:T(8,128)(2,1)S(1)}, bf16[768,256]{1,0:T(8,128)(2,1)S(1)}, u32[]{:S(2)}, u32[]{:S(2)}) collective-permute-start(bf16[768,256]{1,0:T(8,128)(2,1)S(1)} %broadcast_select_fusion.7.offs_0_), channel_id=1, source_target_pairs={{0,1},{1,0},{2,3},{3,2},{4,5},{5,4},{6,7},{7,6},{8,9},{9,8},{10,11... | collective-permute-start | bytes 1179656 | tf_op jit(solution)/shard_map/ppermute | solution.py:401
  61.9 7.7 %collective-permute-start.22 = (bf16[80,512]{1,0:T(8,128)(2,1)S(1)}, bf16[80,512]{1,0:T(8,128)(2,1)S(1)}, u32[]{:S(2)}, u32[]{:S(2)}) collective-permute-start(bf16[80,512]{1,0:T(8,128)(2,1)S(1)} %get-tuple-element.562), channel_id=1, source_target_pairs={{0,8},{8,16},{16,24},{24,0},{1,9},{9,17},{17,25},{25,1},{2,10},{10... | collective-permute-start | bytes 245768 | tf_op jit(solution)/shard_map/ppermute | solution.py:457
  62.4 9.7 %collective-permute-start.23 = (bf16[80,512]{1,0:T(8,128)(2,1)S(1)}, bf16[80,512]{1,0:T(8,128)(2,1)S(1)}, u32[]{:S(2)}, u32[]{:S(2)}) collective-permute-start(bf16[80,512]{1,0:T(8,128)(2,1)S(1)} %get-tuple-element.561), channel_id=1, source_target_pairs={{0,16},{8,24},{16,0},{24,8},{1,17},{9,25},{17,1},{25,9},{2,18},{10... | collective-permute-start | bytes 245768 | tf_op jit(solution)/shard_map/ppermute | solution.py:457
  65.0 7.1 %collective-permute-start.24 = (bf16[80,512]{1,0:T(8,128)(2,1)S(1)}, bf16[80,512]{1,0:T(8,128)(2,1)S(1)}, u32[]{:S(2)}, u32[]{:S(2)}) collective-permute-start(bf16[80,512]{1,0:T(8,128)(2,1)S(1)} %get-tuple-element.560), channel_id=1, source_target_pairs={{0,24},{8,0},{16,8},{24,16},{1,25},{9,1},{17,9},{25,17},{2,26},{10... | collective-permute-start | bytes 245768 | tf_op jit(solution)/shard_map/ppermute | solution.py:457
  65.8 6.3 %copy-start = (bf16[4,256,2,256]{3,2,1,0:T(2,128)(2,1)S(1)}, bf16[4,256,2,256]{3,2,1,0:T(2,128)(2,1)}, u32[]{:S(2)}) copy-start(bf16[4,256,2,256]{3,2,1,0:T(2,128)(2,1)} %param.56) | copy-start | bytes 3145732
  73.4 1.0 %copy-start.2 = (bf16[4,256,2,256]{3,2,1,0:T(2,128)(2,1)}, bf16[4,256,2,256]{3,2,1,0:T(2,128)(2,1)S(1)}, u32[]{:S(2)}) copy-start(bf16[4,256,2,256]{3,2,1,0:T(2,128)(2,1)S(1)} %get-tuple-element.962) | copy-start | bytes 3145732

commit v4 on v3

--- a/solution.py
+++ b/solution.py
@@ -10,7 +10,7 @@
 BF16 = jnp.bfloat16
 F32 = jnp.float32
 I32 = jnp.int32
-VMEM_BYTES = 44 * 1024 * 1024
+VMEM_BYTES = 24 * 1024 * 1024
 MOVE_ROWS = 80
 MOVE_SLOTS = 128
 
@@ -172,21 +172,21 @@
     pack1_ref[...] = dot(chosen, mat_ref[1]).astype(BF16)
 
 
+def final_places(x, piv_ref, cols, steps, size):
+    for s in range(steps):
+        base = s * size
+        inside = (x >= base) & (x < base + size)
+        x = jnp.where(inside, look(cols[s], base, x, size), find(cols[s], base, x, size))
+    return x
+
+
 def find_moves(cfg, piv_ref, meta_ref, move_ref):
     nb, steps, n_row, cap = cfg
-    piv = [piv_ref[t : t + 1, :] for t in range(steps)]
-    cols = [to_col(piv[t], nb) for t in range(steps)]
+    cols = [to_col(piv_ref[t : t + 1, :], nb) for t in range(steps)]
     lanes = -(-n_row // 8) * 8
-    dests, member = [], []
-    for t in range(steps):
-        at = iota((1, nb), 1) + t * nb
-        x = at
-        for s in range(t):
-            x = find(cols[s], s * nb, x, nb)
-        x = jnp.where(x == at, piv[t], x)
-        for s in range(t + 1, steps):
-            inside = (x >= s * nb) & (x < (s + 1) * nb)
-            x = jnp.where(inside, look(cols[s], s * nb, x, nb), find(cols[s], s * nb, x, nb))
+    member = []
+    for t in range(steps):
+        x = final_places(iota((1, nb), 1) + t * nb, piv_ref, cols, steps, nb)
         block = x // nb
         dest = jnp.where(x >= steps * nb, block % n_row, -1)
         move_ref[t : t + 1, :] = dest
@@ -201,7 +201,30 @@
         most = jnp.maximum(most, jnp.sum(jnp.where(member[t], 1.0, 0.0), axis=1, keepdims=True))
     over = jnp.max(most, axis=0, keepdims=True).astype(I32)
     bad = (over > MOVE_ROWS) | (meta_ref[2 * steps : 2 * steps + 1, :] > cap)
-    move_ref[3 * steps : 3 * steps + 1, :] = jnp.where(bad, 1, 0)
+    return jnp.where(bad, 1, 0)
+
+
+def find_targets(cfg, move_ref, my_row):
+    nb, steps, n_row = cfg
+    targets = []
+    for k in range(n_row):
+        here = iota((steps, nb), 0) == lax.rem(my_row + n_row - k, n_row)
+        dest = jnp.sum(jnp.where(here, move_ref[:steps, :] + 1, 0), axis=0, keepdims=True) - 1
+        rank = jnp.sum(jnp.where(here, move_ref[steps : 2 * steps, :], 0), axis=0, keepdims=True)
+        place = jnp.sum(
+            jnp.where(here, move_ref[2 * steps : 3 * steps, :], 0), axis=0, keepdims=True
+        )
+        key = jnp.where(dest == my_row, rank, -1)
+        hot = one_hot(key == iota((MOVE_SLOTS, nb), 0))
+        row = iota((8, nb), 0)
+        parts = jnp.where(row == 0, place // 128, jnp.where(row == 1, place % 128, 1))
+        found = lax.dot_general(
+            parts.astype(F32).astype(BF16), hot, (((1,), (1,)), ((), ())),
+            preferred_element_type=F32,
+        )
+        at = found[0:1] * 128.0 + found[1:2]
+        targets.append(jnp.where(found[2:3] > 0.5, at, -1.0).astype(I32))
+    return jnp.concatenate(targets, axis=1)
 
 
 def order_rows(pos, buf_ref):
@@ -222,37 +245,32 @@
         off_ref[j * nb : (j + 1) * nb, :] = top_ref[rows, :]
 
 
-def late_kernel(cfg, piv_ref, meta_ref, buf_ref, move_ref, top_ref):
-    nb, steps, n_row, cap = cfg
-    find_moves(cfg, piv_ref, meta_ref, move_ref)
+def second_kernel(cfg, meta_ref, buf_ref, top_ref):
+    nb, steps, cap = cfg
     for t in range(steps):
         pos = meta_ref[t : t + 1, :] * cap + meta_ref[steps + t : steps + t + 1, :]
         top_ref[t * nb : (t + 1) * nb, :] = order_rows(pos, buf_ref)
 
 
-def fetch(panels, into, sems, first, rows):
+def sort_panels(panels, into, rows):
     low = lax.axis_index("pcol") & 3
-    copies = [
-        pltpu.make_async_copy(panel.at[rows], into.at[low ^ mask], sems.at[first + mask])
-        for mask, panel in enumerate(panels)
-    ]
-    for c in copies:
-        c.start()
-    return copies
+    for mask, panel in enumerate(panels):
+        into[low ^ mask] = panel[rows, :]
 
 
 def corner_kernel(
-    cfg, move_ref, top0_ref, top1_ref, mat_ref, raws, offs, linv_ref, uinv_ref,
-    upper, res_ref, top_ref, send_ref, raw, off, left, diag, sems,
+    cfg, piv_ref, top0_ref, top1_ref, mat_ref, raws, offs, linv_hbm, uinv_ref,
+    upper, res_ref, top_ref, send_ref, raw, off, left, diag, linv_ref, sem,
 ):
     nb, steps, n_row = cfg
     wide = steps * nb
     my_row = lax.axis_index("prow")
     my_col = lax.axis_index("pcol")
-    copies = fetch(offs, off, sems, 0, pl.ds(0, wide - nb))
-    copies += fetch(raws, raw, sems, 4, pl.ds(0, nb))
-    for c in copies:
-        c.wait()
+    load = pltpu.make_async_copy(linv_hbm, linv_ref, sem)
+    load.start()
+    sort_panels(offs, off, slice(0, wide - nb))
+    sort_panels(raws, raw, slice(0, nb))
+    load.wait()
     for t in range(steps):
         here = slice(t * nb, (t + 1) * nb)
         done = slice(0, t * nb)
@@ -281,9 +299,12 @@
     value = (mat_ref[0, :nb, :].astype(F32) - prod[:, :nb]).astype(BF16)
     res_ref[:, :nb] = jnp.where(in_panel, left[wide:, panel], value)
     res_ref[:, nb:] = (mat_ref[1, :nb, :].astype(F32) - prod[:, nb:]).astype(BF16)
-    here = iota((steps, nb), 0) == my_row
-    dest = jnp.sum(jnp.where(here, move_ref[:steps, :] + 1, 0), axis=0, keepdims=True) - 1
-    rank = jnp.sum(jnp.where(here, move_ref[steps : 2 * steps, :], 0), axis=0, keepdims=True)
+    cols = [to_col(piv_ref[t : t + 1, :], nb) for t in range(steps)]
+    x = final_places(iota((1, nb), 1) + my_row * nb, piv_ref, cols, steps, nb)
+    dest = jnp.where((x >= wide) & (my_row < steps), x // nb % n_row, -1)
+    member = iota((-(-n_row // 8) * 8, nb), 0) == dest
+    rank = jnp.sum(jnp.where(member, before([member], nb)[0], 0.0), axis=0, keepdims=True)
+    rank = rank.astype(I32)
     for k in range(n_row):
         key = jnp.where(dest == lax.rem(my_row + k, n_row), rank, -1)
         hot = one_hot(key == iota((MOVE_ROWS, nb), 0))
@@ -296,13 +317,15 @@
 
 
 def rows_kernel(
-    cfg, mat_ref, raws, upper, uinv_ref, res_ref, raw, l_own, sems
+    cfg, piv_ref, meta_ref, mat_ref, raws, upper, uinv_ref, res_ref, target_ref,
+    flag_ref, raw, l_own, move_ref,
 ):
-    nb, steps, local_rows = cfg
+    nb, steps, n_row, cap, local_rows = cfg
     my_col = lax.axis_index("pcol")
-    copies = fetch(raws, raw, sems, 0, pl.ds(nb, local_rows - nb))
-    for c in copies:
-        c.wait()
+    sort_panels(raws, raw, slice(nb, local_rows))
+    bad = find_moves((nb, steps, n_row, cap), piv_ref, meta_ref, move_ref)
+    target_ref[...] = find_targets((nb, steps, n_row), move_ref, lax.axis_index("prow"))
+    flag_ref[0] = jnp.max(bad)
     tiles = [slice(k * nb, (k + 1) * nb) for k in range(local_rows // nb - 1)]
     for t in range(steps):
         here = slice(t * nb, (t + 1) * nb)
@@ -322,32 +345,14 @@
         res_ref[rows, nb:] = (mat_ref[1, source, :].astype(F32) - prod[:, nb:]).astype(BF16)
 
 
-def place_kernel(cfg, move_ref, head_ref, res_ref, top_ref, *refs):
+def place_kernel(cfg, target_ref, head_ref, res_ref, top_ref, *refs):
     nb, steps, n_row, local_rows = cfg
     recv, out_ref, slots = refs[:n_row], refs[n_row], refs[n_row + 1]
     my_row = lax.axis_index("prow")
     slots[...] = jnp.zeros_like(slots)
-    targets = []
     for k in range(n_row):
         slots[k * MOVE_SLOTS : k * MOVE_SLOTS + MOVE_ROWS, :] = recv[k][...]
-        source = lax.rem(my_row + n_row - k, n_row)
-        here = iota((steps, nb), 0) == source
-        dest = jnp.sum(jnp.where(here, move_ref[:steps, :] + 1, 0), axis=0, keepdims=True) - 1
-        rank = jnp.sum(jnp.where(here, move_ref[steps : 2 * steps, :], 0), axis=0, keepdims=True)
-        place = jnp.sum(
-            jnp.where(here, move_ref[2 * steps : 3 * steps, :], 0), axis=0, keepdims=True
-        )
-        key = jnp.where(dest == my_row, rank, -1)
-        hot = one_hot(key == iota((MOVE_SLOTS, nb), 0))
-        row = iota((8, nb), 0)
-        parts = jnp.where(row == 0, place // 128, jnp.where(row == 1, place % 128, 1))
-        found = lax.dot_general(
-            parts.astype(F32).astype(BF16), hot, (((1,), (1,)), ((), ())),
-            preferred_element_type=F32,
-        )
-        at = found[0:1] * 128.0 + found[1:2]
-        targets.append(jnp.where(found[2:3] > 0.5, at, -1.0).astype(I32))
-    target = jnp.concatenate(targets, axis=1)
+    target = target_ref[...]
     for k in range(local_rows // nb):
         rows = slice(k * nb, (k + 1) * nb)
         hit = iota((nb, n_row * MOVE_SLOTS), 0) + k * nb == target
@@ -364,13 +369,14 @@
 def call(kernel, outs, ins, scratch=(), any_at=(), flops=None):
     vmem = pl.BlockSpec(memory_space=pltpu.VMEM)
     anywhere = pl.BlockSpec(memory_space=pl.ANY)
+    scalars = pl.BlockSpec(memory_space=pltpu.SMEM)
     return pl.pallas_call(
         kernel,
         out_shape=outs,
         in_specs=[
             jax.tree.map(lambda _: anywhere if i in any_at else vmem, x) for i, x in enumerate(ins)
         ],
-        out_specs=jax.tree.map(lambda _: vmem, outs),
+        out_specs=jax.tree.map(lambda x: scalars if x.shape == (1,) else vmem, outs),
         scratch_shapes=list(scratch),
         compiler_params=pltpu.CompilerParams(vmem_limit_bytes=VMEM_BYTES),
         cost_estimate=flops
@@ -431,10 +437,8 @@
     off_0, off_2 = panel_pair(off, off_x, off_far, off_far_x)
     raws = (raw_0, swap_cores(raw_0), raw_2, swap_cores(raw_2))
     offs = (off_0, swap_cores(off_0), off_2, swap_cores(off_2))
-    move, top1 = call(
-        functools.partial(late_kernel, (nb, steps, n_row, cap)),
-        (shape(16, nb, dtype=I32), shape(steps * nb, nb)),
-        (pivots, meta, buf1),
+    top1 = call(
+        functools.partial(second_kernel, (nb, steps, cap)), shape(steps * nb, nb), (meta, buf1)
     )
     top_rows = steps * nb
     upper, head, top, send = call(
@@ -443,15 +447,16 @@
             shape(top_rows, top_rows + 2 * nb), shape(nb, 2 * nb), shape(nb, 2 * nb),
             shape(n_row, MOVE_ROWS, 2 * nb),
         ),
-        (move, top0, top1, mat, raws, offs, lower_inverse, upper_inverse),
+        (pivots, top0, top1, mat, raws, offs, lower_inverse, upper_inverse),
         scratch=(
             pltpu.VMEM((steps, nb, nb), BF16),
             pltpu.VMEM((steps, top_rows - nb, nb), BF16),
             pltpu.VMEM((top_rows + nb, top_rows), BF16),
             pltpu.VMEM((top_rows, nb), BF16),
-            pltpu.SemaphoreType.DMA((8,)),
+            pltpu.VMEM((steps, nb, nb), BF16),
+            pltpu.SemaphoreType.DMA,
         ),
-        any_at=(4, 5),
+        any_at=(6,),
     )
     recv = [send[0]] + [
         lax.ppermute(send[k], "prow", [(i, (i + k) % n_row) for i in range(n_row)])
@@ -459,16 +464,17 @@
     ]
 
     below = local_rows - nb
-    res = call(
-        functools.partial(rows_kernel, (nb, steps, local_rows)),
-        shape(below, 2 * nb),
-        (mat, raws, upper, upper_inverse),
+    res, target, crowded = call(
+        functools.partial(rows_kernel, (nb, steps, n_row, cap, local_rows)),
+        (
+            shape(below, 2 * nb), shape(1, n_row * MOVE_SLOTS, dtype=I32), shape(1, dtype=I32),
+        ),
+        (pivots, meta, mat, raws, upper, upper_inverse),
         scratch=(
             pltpu.VMEM((steps, below, nb), BF16),
             pltpu.VMEM((below, top_rows), BF16),
-            pltpu.SemaphoreType.DMA((4,)),
+            pltpu.VMEM((16, nb), I32),
         ),
-        any_at=(1,),
         flops=2 * below * top_rows * (top_rows + 2 * nb),
     )
 
@@ -476,13 +482,13 @@
         out = call(
             functools.partial(place_kernel, (nb, steps, n_row, local_rows)),
             shape(local_rows, 2 * nb),
-            (move, head, res, top, *recv),
+            (target, head, res, top, *recv),
             scratch=(pltpu.VMEM((n_row * MOVE_SLOTS, 2 * nb), BF16),),
         )
         return out.reshape(matrix.shape)
 
     return lax.cond(
-        move[3 * steps, 0] > 0,
+        crowded[0] > 0,
         lambda: stepwise(matrix, pivots, lower_inverse, upper_inverse),
         finish,
     )

time: 74.7 us -> 71.4 us (0.956)
  Pallas kernels: 14.1 us -> 12.3 us
    pallas_call x6, Pallas kernels: 14.1 us -> 12.3 us  [call(): pl.pallas_call(kernel, out_shape=outs, in_specs=[jax.tree.map(lambda _: a...]
    ppermute x3, waiting for transfers between devices: 2.43 us -> 0.93 us  [local(): lax.ppermute(send[k], 'prow', [(i, (i + k) % n_row) for i in range(n_row)])]
    ppermute x4, waiting for transfers between devices: 0.01 us -> 1.29 us  [swap_cores(): return lax.ppermute(value, 'pcol', [(i, i ^ 1) for i in range(n_col)])]
  transfers between devices with their start and end apart: 13 -> 13, of which waited for: 1 -> 2; matrix products, arithmetic and copies ran while one was open for 1% -> 0% of each run, Pallas kernels for 9% -> 9%
where the time goes in v4:
time: 71.4 us; the launch traced here: 71.1 us
  blocking collectives  35.7 us (50%)
  starting transfers between devices  17 us (24%)
  Pallas kernels  12.3 us (17%)
  local copies, waits for them, and re-layouts  2.7 us (4%)
  waiting for transfers between devices  2.23 us (3%)
  between operations  0.88 us (1%)
    all_gather x1, blocking collectives, local(): buf0 = lax.all_gather(pack0, 'prow', tiled=True)  18.1 us
    all_gather x1, blocking collectives, local(): buf1 = lax.all_gather(pack1, 'prow', tiled=True)  17.6 us
    pallas_call x6, Pallas kernels, call(): pl.pallas_call(kernel, out_shape=outs, in_specs=[jax.tree.map(lambda _: a...  12.3 us
    ppermute x5, starting transfers between devices, from_panels(): return lax.ppermute(value, 'pcol', [(i, i ^ mask) for i in range(steps)])  11.7 us
    ppermute x3, starting transfers between devices, local(): lax.ppermute(send[k], 'prow', [(i, (i + k) % n_row) for i in range(n_row)])  3.88 us
    unnamed x9, local copies, waits for them, and re-layouts  2.35 us
  transfers between devices with their start and end apart: 13, of which 2 were waited for; matrix products, arithmetic and copies ran while one was open for 0% of the time, Pallas kernels for 9%

profile of v4, /device:TPU:0, one launch (start us, length us, event | category | flops | bytes accessed | tf_op | source)
XLA Modules:
  0.0 71.1 jit_solution(12171310106074062082)
XLA Ops:
  0.0 0.0 copy-start.5
  0.0 1.4 %copy.25 = bf16[4,256,2,256]{3,1,0,2:T(8,128)(2,1)S(1)} copy(bf16[4,256,2,256]{3,2,1,0:T(2,128)(2,1)} %param.56) | data formatting | bytes 2097152 | tf_op args[0]
  1.4 4.8 %collective-permute-start.12 = (bf16[1024,256]{1,0:T(8,128)(2,1)S(1)}, bf16[1024,256]{1,0:T(8,128)(2,1)S(1)}, u32[]{:S(2)}, u32[]{:S(2)}) collective-permute-start(bf16[1024,256]{1,0:T(8,128)(2,1)S(1)} %bitcast.143), channel_id=1, source_target_pairs={{0,2},{1,3},{2,0},{3,1},{8,10},{9,11},{10,8},{11,9},{16,18},{17,19... | collective-permute-start | bytes 1572872 | tf_op jit(solution)/shard_map/ppermute | solution.py:404
  6.3 1.3 %collective-permute-start.13 = (bf16[1024,256]{1,0:T(8,128)(2,1)S(1)}, bf16[1024,256]{1,0:T(8,128)(2,1)S(1)}, u32[]{:S(2)}, u32[]{:S(2)}) collective-permute-start(bf16[1024,256]{1,0:T(8,128)(2,1)S(1)} %bitcast.144), channel_id=1, source_target_pairs={{0,4},{1,5},{2,6},{3,7},{8,12},{9,13},{10,14},{11,15},{16,20},{17,... | collective-permute-start | bytes 1572872 | tf_op jit(solution)/shard_map/ppermute | solution.py:404
  7.6 0.0 copy-done.5
  7.6 1.3 %shard_map.48 = (s32[16,256]{1,0:T(8,128)S(1)}, bf16[320,256]{1,0:T(8,128)(2,1)S(1)}, bf16[320,256]{1,0:T(8,128)(2,1)S(1)}) custom-call(s32[4,256]{1,0:T(4,128)S(1)} %copy-done.5, bf16[2,1024,256]{2,1,0:T(8,128)(2,1)S(1)} %bitcast.135), custom_call_target="tpu_custom_call" | custom-call | tf_op jit(solution)/shard_map/pallas_call | solution.py:373
  8.9 18.1 %all_gather.6.buf_ref = bf16[1280,256]{1,0:T(8,128)(2,1)S(1)} all-gather(bf16[320,256]{1,0:T(8,128)(2,1)S(1)} %get-tuple-element.419), channel_id=1, replica_groups=mesh['prow'=4,'pcol'=8] {'prow'}, dimensions={0}, use_global_device_ids=true | all-gather | bytes 819200 | tf_op jit(solution)/shard_map/all_gather | solution.py:422
  27.0 0.0 collective-permute-done.12
  27.0 0.0 collective-permute-done.13
  27.0 1.1 %shard_map.49 = (bf16[1024,256]{1,0:T(8,128)(2,1)S(1)}, bf16[768,256]{1,0:T(8,128)(2,1)S(1)}) custom-call(s32[16,256]{1,0:T(8,128)S(1)} %get-tuple-element.417.meta_ref, bf16[1280,256]{1,0:T(8,128)(2,1)S(1)} %all_gather.6.buf_ref), custom_call_target="tpu_custom_call" | custom-call | tf_op jit(solution)/shard_map/pallas_call | solution.py:373
  28.0 1.3 %collective-permute-start.17 = (bf16[768,256]{1,0:T(8,128)(2,1)S(1)}, bf16[768,256]{1,0:T(8,128)(2,1)S(1)}, u32[]{:S(2)}, u32[]{:S(2)}) collective-permute-start(bf16[768,256]{1,0:T(8,128)(2,1)S(1)} %get-tuple-element.427), channel_id=1, source_target_pairs={{0,4},{1,5},{2,6},{3,7},{8,12},{9,13},{10,14},{11,15},{16,20},{17,... | collective-permute-start | bytes 1179656 | tf_op jit(solution)/shard_map/ppermute | solution.py:404
  29.4 2.9 %collective-permute-start.18 = (bf16[768,256]{1,0:T(8,128)(2,1)S(1)}, bf16[768,256]{1,0:T(8,128)(2,1)S(1)}, u32[]{:S(2)}, u32[]{:S(2)}) collective-permute-start(bf16[768,256]{1,0:T(8,128)(2,1)S(1)} %get-tuple-element.427), channel_id=1, source_target_pairs={{0,2},{1,3},{2,0},{3,1},{8,10},{9,11},{10,8},{11,9},{16,18},{17,19... | collective-permute-start | bytes 1179656 | tf_op jit(solution)/shard_map/ppermute | solution.py:404
  32.3 1.3 %collective-permute-start.19 = (bf16[768,256]{1,0:T(8,128)(2,1)S(1)}, bf16[768,256]{1,0:T(8,128)(2,1)S(1)}, u32[]{:S(2)}, u32[]{:S(2)}) collective-permute-start(bf16[768,256]{1,0:T(8,128)(2,1)S(1)} %get-tuple-element.427), channel_id=1, source_target_pairs={{0,6},{1,7},{2,4},{3,5},{8,14},{9,15},{10,12},{11,13},{16,22},{17,... | collective-permute-start | bytes 1179656 | tf_op jit(solution)/shard_map/ppermute | solution.py:404
  33.6 0.7 collective-permute-start.15
  34.3 0.1 broadcast_select_fusion.5.raws_0_
  34.4 0.1 collective-permute-start.14
  34.5 17.6 %all_gather.7.buf_ref = bf16[1280,256]{1,0:T(8,128)(2,1)S(1)} all-gather(bf16[320,256]{1,0:T(8,128)(2,1)S(1)} %get-tuple-element.426), channel_id=1, replica_groups=mesh['prow'=4,'pcol'=8] {'prow'}, dimensions={0}, use_global_device_ids=true | all-gather | bytes 819200 | tf_op jit(solution)/shard_map/all_gather | solution.py:434
  52.1 0.0 collective-permute-done.17
  52.1 0.0 collective-permute-done.18
  52.1 0.0 collective-permute-done.19
  52.1 0.0 copy-start.1
  52.1 0.1 collective-permute-start.21
  52.2 0.0 collective-permute-done.15
  52.2 0.1 broadcast_select_fusion.4.raws_2_
  52.3 0.5 collective-permute-start.16
  52.9 0.1 collective-permute-start.20
  53.0 1.0 %shard_map.50.top1_ref = bf16[1024,256]{1,0:T(8,128)(2,1)S(1)} custom-call(s32[16,256]{1,0:T(8,128)S(1)} %get-tuple-element.417.meta_ref, bf16[1280,256]{1,0:T(8,128)(2,1)S(1)} %all_gather.7.buf_ref), custom_call_target="tpu_custom_call" | custom-call | tf_op jit(solution)/shard_map/pallas_call | solution.py:373
  53.9 0.0 collective-permute-done.14.raws_1_
  54.0 0.0 collective-permute-done.21.offs_3_
  54.0 1.3 %collective-permute-done.20.offs_1_ = bf16[768,256]{1,0:T(8,128)(2,1)S(1)} collective-permute-done((bf16[768,256]{1,0:T(8,128)(2,1)S(1)}, bf16[768,256]{1,0:T(8,128)(2,1)S(1)}, u32[]{:S(2)}, u32[]{:S(2)}) %collective-permute-start.20) | collective-permute-done | bytes 393248 | tf_op jit(solution)/shard_map/ppermute | solution.py:407
  55.2 0.0 collective-permute-done.16.raws_3_
  55.2 0.0 copy-done.1
  55.2 3.8 %shard_map.51 = (bf16[1024,1536]{1,0:T(8,128)(2,1)S(1)}, bf16[256,512]{1,0:T(8,128)(2,1)S(1)}, bf16[256,512]{1,0:T(8,128)(2,1)S(1)}, bf16[4,80,512]{2,1,0:T(8,128)(2,1)S(1)}) custom-call(s32[4,256]{1,0:T(4,128)S(1)} %copy-done.5, bf16[1024,256]{1,0:T(8,128)(2,1)S(1)} %get-tuple-element.425.top0_ref, bf16[1024,256]{1,0:T(8,128)(2,1)S(1)} %shard_map.50.top1_ref, ...), custom_call_target="tpu_custom_call" | custom-call | tf_op jit(solution)/shard_map/pallas_call | solution.py:373
  59.1 0.5 collective-permute-start.22
  59.6 2.6 %collective-permute-start.23 = (bf16[80,512]{1,0:T(8,128)(2,1)S(1)}, bf16[80,512]{1,0:T(8,128)(2,1)S(1)}, u32[]{:S(2)}, u32[]{:S(2)}) collective-permute-start(bf16[80,512]{1,0:T(8,128)(2,1)S(1)} %get-tuple-element.563), channel_id=1, source_target_pairs={{0,16},{8,24},{16,0},{24,8},{1,17},{9,25},{17,1},{25,9},{2,18},{10... | collective-permute-start | bytes 245768 | tf_op jit(solution)/shard_map/ppermute | solution.py:462
  62.2 0.8 %collective-permute-start.24 = (bf16[80,512]{1,0:T(8,128)(2,1)S(1)}, bf16[80,512]{1,0:T(8,128)(2,1)S(1)}, u32[]{:S(2)}, u32[]{:S(2)}) collective-permute-start(bf16[80,512]{1,0:T(8,128)(2,1)S(1)} %get-tuple-element.562), channel_id=1, source_target_pairs={{0,24},{8,0},{16,8},{24,16},{1,25},{9,1},{17,9},{25,17},{2,26},{10... | collective-permute-start | bytes 245768 | tf_op jit(solution)/shard_map/ppermute | solution.py:462
  63.0 0.0 copy-start
  63.0 4.5 %shard_map.52 = (bf16[768,512]{1,0:T(8,128)(2,1)S(1)}, s32[1,512]{1,0:T(1,128)S(1)}, s32[1]{0:T(128)}) custom-call(s32[4,256]{1,0:T(4,128)S(1)} %copy-done.5, s32[16,256]{1,0:T(8,128)S(1)} %get-tuple-element.417.meta_ref, bf16[2,1024,256]{2,1,0:T(8,128)(2,1)S(1)} %bitcast.137, bf16[1024,256]{1,0:T(8,128)(2,1)S(1)} %broadcast_select_fusion.5.raws_0_, ...), custom_call_target="tpu_custom_call" | custom-call | flops 2415919104 | bytes 4194304 | tf_op jit(solution)/shard_map/pallas_call | solution.py:373
  68.1 0.0 collective-permute-done.22
  68.1 0.9 %collective-permute-done.23 = bf16[80,512]{1,0:T(8,128)(2,1)S(1)} collective-permute-done((bf16[80,512]{1,0:T(8,128)(2,1)S(1)}, bf16[80,512]{1,0:T(8,128)(2,1)S(1)}, u32[]{:S(2)}, u32[]{:S(2)}) %collective-permute-start.23) | collective-permute-done | bytes 81952 | tf_op jit(solution)/shard_map/ppermute | solution.py:462
  69.1 0.0 collective-permute-done.24
  69.1 0.0 copy-done
  69.1 1.1 %conditional.1 = (bf16[4,256,2,256]{3,2,1,0:T(2,128)(2,1)S(1)}) conditional(s32[]{:T(128)} %bitcast.29, (bf16[4,80,512]{2,1,0:T(8,128)(2,1)S(1)}, s32[1,512]{1,0:T(1,128)S(1)}, bf16[256,512]{1,0:T(8,128)(2,1)S(1)}, bf16[768,512]{1,0:T(8,128)(2,1)S(1)}, bf16[256,512]{1,0:T(8,128)(2,1)S(1)}, /*index=5*/bf16[80,512]{1,0:T(8,128)(2,1)S(1)}, ...), branch_computations={%region_0.1_spmd, %region_1.32_spmd} | conditional | flops 1896568576 | bytes 99436336 | solution.py:490
  69.1 0.8 %branch_0_fun.1 = bf16[1024,512]{1,0:T(8,128)(2,1)S(1)} custom-call(s32[1,512]{1,0:T(1,128)S(1)} %get-tuple-element.323.target_ref, bf16[256,512]{1,0:T(8,128)(2,1)S(1)} %get-tuple-element.324.head_ref, bf16[768,512]{1,0:T(8,128)(2,1)S(1)} %get-tuple-element.325.res_ref, bf16[256,512]{1,0:T(8,128)(2,1)S(1)} %get-tuple-element.326.top_ref, ...), custom_call_target="tpu_custom_call" | custom-call | tf_op jit(solution)/shard_map/cond/branch_0_fun/pallas_call | solution.py:373
  69.8 0.3 reshape.1231
  70.1 0.0 copy-start.4
  70.2 1.0 %copy-done.4 = bf16[4,256,2,256]{3,2,1,0:T(2,128)(2,1)} copy-done((bf16[4,256,2,256]{3,2,1,0:T(2,128)(2,1)}, bf16[4,256,2,256]{3,2,1,0:T(2,128)(2,1)S(1)}, u32[]{:S(2)}) %copy-start.4) | copy-done | bytes 1048600
  (5 shorter events, 0.1 us)
Async XLA Ops:
  0.0 7.6 %copy-start.5 = (s32[4,256]{1,0:T(4,128)S(1)}, s32[4,256]{1,0:T(4,128)}, u32[]{:S(2)}) copy-start(s32[4,256]{1,0:T(4,128)} %piv_ref.5) | copy-start | bytes 12292
  1.4 25.5 %collective-permute-start.12 = (bf16[1024,256]{1,0:T(8,128)(2,1)S(1)}, bf16[1024,256]{1,0:T(8,128)(2,1)S(1)}, u32[]{:S(2)}, u32[]{:S(2)}) collective-permute-start(bf16[1024,256]{1,0:T(8,128)(2,1)S(1)} %bitcast.143), channel_id=1, source_target_pairs={{0,2},{1,3},{2,0},{3,1},{8,10},{9,11},{10,8},{11,9},{16,18},{17,19... | collective-permute-start | bytes 1572872 | tf_op jit(solution)/shard_map/ppermute | solution.py:404
  6.3 20.7 %collective-permute-start.13 = (bf16[1024,256]{1,0:T(8,128)(2,1)S(1)}, bf16[1024,256]{1,0:T(8,128)(2,1)S(1)}, u32[]{:S(2)}, u32[]{:S(2)}) collective-permute-start(bf16[1024,256]{1,0:T(8,128)(2,1)S(1)} %bitcast.144), channel_id=1, source_target_pairs={{0,4},{1,5},{2,6},{3,7},{8,12},{9,13},{10,14},{11,15},{16,20},{17,... | collective-permute-start | bytes 1572872 | tf_op jit(solution)/shard_map/ppermute | solution.py:404
  28.0 24.0 %collective-permute-start.17 = (bf16[768,256]{1,0:T(8,128)(2,1)S(1)}, bf16[768,256]{1,0:T(8,128)(2,1)S(1)}, u32[]{:S(2)}, u32[]{:S(2)}) collective-permute-start(bf16[768,256]{1,0:T(8,128)(2,1)S(1)} %get-tuple-element.427), channel_id=1, source_target_pairs={{0,4},{1,5},{2,6},{3,7},{8,12},{9,13},{10,14},{11,15},{16,20},{17,... | collective-permute-start | bytes 1179656 | tf_op jit(solution)/shard_map/ppermute | solution.py:404
  29.4 22.7 %collective-permute-start.18 = (bf16[768,256]{1,0:T(8,128)(2,1)S(1)}, bf16[768,256]{1,0:T(8,128)(2,1)S(1)}, u32[]{:S(2)}, u32[]{:S(2)}) collective-permute-start(bf16[768,256]{1,0:T(8,128)(2,1)S(1)} %get-tuple-element.427), channel_id=1, source_target_pairs={{0,2},{1,3},{2,0},{3,1},{8,10},{9,11},{10,8},{11,9},{16,18},{17,19... | collective-permute-start | bytes 1179656 | tf_op jit(solution)/shard_map/ppermute | solution.py:404
  32.3 19.8 %collective-permute-start.19 = (bf16[768,256]{1,0:T(8,128)(2,1)S(1)}, bf16[768,256]{1,0:T(8,128)(2,1)S(1)}, u32[]{:S(2)}, u32[]{:S(2)}) collective-permute-start(bf16[768,256]{1,0:T(8,128)(2,1)S(1)} %get-tuple-element.427), channel_id=1, source_target_pairs={{0,6},{1,7},{2,4},{3,5},{8,14},{9,15},{10,12},{11,13},{16,22},{17,... | collective-permute-start | bytes 1179656 | tf_op jit(solution)/shard_map/ppermute | solution.py:404
  33.6 18.6 %collective-permute-start.15 = (bf16[1024,256]{1,0:T(8,128)(2,1)S(1)}, bf16[1024,256]{1,0:T(8,128)(2,1)S(1)}, u32[]{:S(2)}, u32[]{:S(2)}) collective-permute-start(bf16[1024,256]{1,0:T(8,128)(2,1)S(1)} %collective-permute-done.13), channel_id=1, source_target_pairs={{4,6},{5,7},{6,4},{7,5},{12,14},{13,15},{14,12},{15,13},{20,22},{2... | collective-permute-start | bytes 1572872 | tf_op jit(solution)/shard_map/ppermute | solution.py:433
  34.4 19.6 %collective-permute-start.14 = (bf16[1024,256]{1,0:T(8,128)(2,1)S(1)}, bf16[1024,256]{1,0:T(8,128)(2,1)S(1)}, u32[]{:S(2)}, u32[]{:S(2)}) collective-permute-start(bf16[1024,256]{1,0:T(8,128)(2,1)S(1)} %broadcast_select_fusion.5.raws_0_), channel_id=1, source_target_pairs={{0,1},{1,0},{2,3},{3,2},{4,5},{5,4},{6,7},{7,6},{8,9},{9,8},{10,11... | collective-permute-start | bytes 1572872 | tf_op jit(solution)/shard_map/ppermute | solution.py:407
  52.1 3.1 %copy-start.1 = (bf16[4,256,256]{2,1,0:T(8,128)(2,1)S(1)}, bf16[4,256,256]{2,1,0:T(8,128)(2,1)}, u32[]{:S(2)}) copy-start(bf16[4,256,256]{2,1,0:T(8,128)(2,1)} %uinv_ref.3) | copy-start | bytes 1572868
  52.1 1.8 %collective-permute-start.21 = (bf16[768,256]{1,0:T(8,128)(2,1)S(1)}, bf16[768,256]{1,0:T(8,128)(2,1)S(1)}, u32[]{:S(2)}, u32[]{:S(2)}) collective-permute-start(bf16[768,256]{1,0:T(8,128)(2,1)S(1)} %broadcast_select_fusion.6.offs_2_), channel_id=1, source_target_pairs={{0,1},{1,0},{2,3},{3,2},{4,5},{5,4},{6,7},{7,6},{8,9},{9,8},{10,11... | collective-permute-start | bytes 1179656 | tf_op jit(solution)/shard_map/ppermute | solution.py:407
  52.3 2.9 %collective-permute-start.16 = (bf16[1024,256]{1,0:T(8,128)(2,1)S(1)}, bf16[1024,256]{1,0:T(8,128)(2,1)S(1)}, u32[]{:S(2)}, u32[]{:S(2)}) collective-permute-start(bf16[1024,256]{1,0:T(8,128)(2,1)S(1)} %broadcast_select_fusion.4.raws_2_), channel_id=1, source_target_pairs={{0,1},{1,0},{2,3},{3,2},{4,5},{5,4},{6,7},{7,6},{8,9},{9,8},{10,11... | collective-permute-start | bytes 1572872 | tf_op jit(solution)/shard_map/ppermute | solution.py:407
  52.9 2.4 %collective-permute-start.20 = (bf16[768,256]{1,0:T(8,128)(2,1)S(1)}, bf16[768,256]{1,0:T(8,128)(2,1)S(1)}, u32[]{:S(2)}, u32[]{:S(2)}) collective-permute-start(bf16[768,256]{1,0:T(8,128)(2,1)S(1)} %broadcast_select_fusion.7.offs_0_), channel_id=1, source_target_pairs={{0,1},{1,0},{2,3},{3,2},{4,5},{5,4},{6,7},{7,6},{8,9},{9,8},{10,11... | collective-permute-start | bytes 1179656 | tf_op jit(solution)/shard_map/ppermute | solution.py:407
  59.1 9.0 %collective-permute-start.22 = (bf16[80,512]{1,0:T(8,128)(2,1)S(1)}, bf16[80,512]{1,0:T(8,128)(2,1)S(1)}, u32[]{:S(2)}, u32[]{:S(2)}) collective-permute-start(bf16[80,512]{1,0:T(8,128)(2,1)S(1)} %get-tuple-element.564), channel_id=1, source_target_pairs={{0,8},{8,16},{16,24},{24,0},{1,9},{9,17},{17,25},{25,1},{2,10},{10... | collective-permute-start | bytes 245768 | tf_op jit(solution)/shard_map/ppermute | solution.py:462
  59.6 9.5 %collective-permute-start.23 = (bf16[80,512]{1,0:T(8,128)(2,1)S(1)}, bf16[80,512]{1,0:T(8,128)(2,1)S(1)}, u32[]{:S(2)}, u32[]{:S(2)}) collective-permute-start(bf16[80,512]{1,0:T(8,128)(2,1)S(1)} %get-tuple-element.563), channel_id=1, source_target_pairs={{0,16},{8,24},{16,0},{24,8},{1,17},{9,25},{17,1},{25,9},{2,18},{10... | collective-permute-start | bytes 245768 | tf_op jit(solution)/shard_map/ppermute | solution.py:462
  62.2 6.9 %collective-permute-start.24 = (bf16[80,512]{1,0:T(8,128)(2,1)S(1)}, bf16[80,512]{1,0:T(8,128)(2,1)S(1)}, u32[]{:S(2)}, u32[]{:S(2)}) collective-permute-start(bf16[80,512]{1,0:T(8,128)(2,1)S(1)} %get-tuple-element.562), channel_id=1, source_target_pairs={{0,24},{8,0},{16,8},{24,16},{1,25},{9,1},{17,9},{25,17},{2,26},{10... | collective-permute-start | bytes 245768 | tf_op jit(solution)/shard_map/ppermute | solution.py:462
  63.0 6.1 %copy-start = (bf16[4,256,2,256]{3,2,1,0:T(2,128)(2,1)S(1)}, bf16[4,256,2,256]{3,2,1,0:T(2,128)(2,1)}, u32[]{:S(2)}) copy-start(bf16[4,256,2,256]{3,2,1,0:T(2,128)(2,1)} %param.56) | copy-start | bytes 3145732
  70.1 1.0 %copy-start.4 = (bf16[4,256,2,256]{3,2,1,0:T(2,128)(2,1)}, bf16[4,256,2,256]{3,2,1,0:T(2,128)(2,1)S(1)}, u32[]{:S(2)}) copy-start(bf16[4,256,2,256]{3,2,1,0:T(2,128)(2,1)S(1)} %get-tuple-element.964) | copy-start | bytes 3145732

commit v5 on v4

--- a/solution.py
+++ b/solution.py
@@ -233,12 +233,17 @@
     return dot(hot, buf_ref[...]).astype(BF16)
 
 
-def order_kernel(cfg, meta_ref, buf_ref, top_ref, off_ref):
-    nb, steps, cap = cfg
+def order_kernel(cfg, meta_ref, parts, top_ref, off_ref, buf):
+    nb, steps, n_row, cap = cfg
+    my_row = lax.axis_index("prow")
     my_col = lax.axis_index("pcol")
-    for t in range(steps):
-        pos = meta_ref[t : t + 1, :] * cap + meta_ref[steps + t : steps + t + 1, :]
-        top_ref[t * nb : (t + 1) * nb, :] = order_rows(pos, buf_ref)
+    for k in range(n_row):
+        buf[k * cap : (k + 1) * cap, :] = parts[k][...]
+    for t in range(steps):
+        turn = my_row - meta_ref[t : t + 1, :]
+        turn = jnp.where(turn < 0, turn + n_row, turn)
+        pos = turn * cap + meta_ref[steps + t : steps + t + 1, :]
+        top_ref[t * nb : (t + 1) * nb, :] = order_rows(pos, buf)
     for j in range(steps - 1):
         block = jnp.where(my_col <= j, j + 1, j)
         rows = pl.ds(pl.multiple_of(block * nb, nb), nb)
@@ -305,10 +310,13 @@
     member = iota((-(-n_row // 8) * 8, nb), 0) == dest
     rank = jnp.sum(jnp.where(member, before([member], nb)[0], 0.0), axis=0, keepdims=True)
     rank = rank.astype(I32)
+    hot = []
     for k in range(n_row):
         key = jnp.where(dest == lax.rem(my_row + k, n_row), rank, -1)
-        hot = one_hot(key == iota((MOVE_ROWS, nb), 0))
-        send_ref[k] = dot(hot, res_ref[...]).astype(BF16)
+        hot.append(one_hot(key == iota((MOVE_ROWS, nb), 0)))
+    moved = dot(jnp.concatenate(hot, axis=0), res_ref[...]).astype(BF16)
+    for k in range(n_row):
+        send_ref[k] = moved[k * MOVE_ROWS : (k + 1) * MOVE_ROWS]
     block = pl.ds(pl.multiple_of(jnp.minimum(my_row, steps - 1) * nb, nb), nb)
     value = jnp.where(my_col == my_row, diag[block, :], upper[block, wide : wide + nb])
     value = jnp.where(in_panel & (my_col < my_row), left[block, panel], value)
@@ -411,26 +419,30 @@
 
     on_panel = lax.axis_index("pcol") < steps
     fours = range(4, n_col, 4)
-    raw_x = from_panels(m0, 2)
-    raw_far = functools.reduce(jnp.add, [from_panels(m0, mask) for mask in fours])
-
     meta, pack0, pack1 = call(
         functools.partial(pick_kernel, (nb, steps, n_row, cap, local_rows)),
         (shape(16, nb, dtype=I32), shape(cap, nb), shape(cap, nb)),
         (pivots, mat),
     )
-    buf0 = lax.all_gather(pack0, "prow", tiled=True)
-    buf0, raw_x, raw_far = lax.optimization_barrier((buf0, raw_x, raw_far))
+    late0, pack0 = lax.optimization_barrier((m0, pack0))
+    raw_x = from_panels(m0, 2)
+    raw_far = functools.reduce(jnp.add, [from_panels(late0, mask) for mask in fours])
+    parts = [pack0] + [
+        lax.ppermute(pack0, "prow", [(i, (i + k) % n_row) for i in range(n_row)])
+        for k in range(1, n_row)
+    ]
+    parts[1], raw_x = lax.optimization_barrier((parts[1], raw_x))
+    raw_far_x = lax.ppermute(raw_far, "pcol", [(i, i ^ 2) for i in range(steps, n_col)])
     top0, off = call(
-        functools.partial(order_kernel, (nb, steps, cap)),
+        functools.partial(order_kernel, (nb, steps, n_row, cap)),
         (shape(steps * nb, nb), shape((steps - 1) * nb, nb)),
-        (meta, buf0),
-    )
-    pack1, off, raw_far = lax.optimization_barrier((pack1, off, raw_far))
+        (meta, tuple(parts)),
+        scratch=(pltpu.VMEM((n_row * cap, nb), BF16),),
+    )
+    pack1, off = lax.optimization_barrier((pack1, off))
     off_x = from_panels(off, 2)
     off_far = functools.reduce(jnp.add, [from_panels(off, mask) for mask in fours])
     off_far_x = functools.reduce(jnp.add, [from_panels(off, mask + 2) for mask in fours])
-    raw_far_x = lax.ppermute(raw_far, "pcol", [(i, i ^ 2) for i in range(steps, n_col)])
     buf1 = lax.all_gather(pack1, "prow", tiled=True)
     buf1, off_far, off_x, off_far_x = lax.optimization_barrier((buf1, off_far, off_x, off_far_x))
     raw_0, raw_2 = panel_pair(m0, raw_x, raw_far, raw_far_x)

time: 71.4 us -> 70.4 us (0.986)
  blocking collectives: 35.7 us -> 19.8 us
  waiting for transfers between devices: 2.23 us -> 11.4 us
  starting transfers between devices: 17 us -> 22.8 us
    all_gather x1 -> x0, blocking collectives: 18.1 us -> none  [local(): buf0 = lax.all_gather(pack0, 'prow', tiled=True)]
    ppermute x0 -> x3, waiting for transfers between devices: none -> 8.88 us  [local(): lax.ppermute(pack0, 'prow', [(i, (i + k) % n_row) for i in range(n_row)])]
    ppermute x0 -> x3, starting transfers between devices: none -> 5.56 us  [local(): lax.ppermute(pack0, 'prow', [(i, (i + k) % n_row) for i in range(n_row)])]
    all_gather x1, blocking collectives: 17.6 us -> 19.8 us  [local(): buf1 = lax.all_gather(pack1, 'prow', tiled=True)]
  transfers between devices with their start and end apart: 13 -> 16, of which waited for: 2 -> 5; matrix products, arithmetic and copies ran while one was open for 0% -> 0% of each run, Pallas kernels for 9% -> 11%
where the time goes in v5:
time: 70.4 us; the launch traced here: 70 us
  starting transfers between devices  22.8 us (32%)
  blocking collectives  19.8 us (28%)
  Pallas kernels  12.3 us (17%)
  waiting for transfers between devices  11.4 us (16%)
  local copies, waits for them, and re-layouts  2.7 us (4%)
  between operations  0.88 us (1%)
    all_gather x1, blocking collectives, local(): buf1 = lax.all_gather(pack1, 'prow', tiled=True)  19.8 us
    pallas_call x6, Pallas kernels, call(): pl.pallas_call(kernel, out_shape=outs, in_specs=[jax.tree.map(lambda _: a...  12.3 us
    ppermute x5, starting transfers between devices, from_panels(): return lax.ppermute(value, 'pcol', [(i, i ^ mask) for i in range(steps)])  11.9 us
    ppermute x3, waiting for transfers between devices, local(): lax.ppermute(pack0, 'prow', [(i, (i + k) % n_row) for i in range(n_row)])  8.88 us
    ppermute x3, starting transfers between devices, local(): lax.ppermute(pack0, 'prow', [(i, (i + k) % n_row) for i in range(n_row)])  5.56 us
    ppermute x3, starting transfers between devices, local(): lax.ppermute(send[k], 'prow', [(i, (i + k) % n_row) for i in range(n_row)])  3.88 us
    unnamed x9, local copies, waits for them, and re-layouts  2.35 us
  transfers between devices with their start and end apart: 16, of which 5 were waited for; matrix products, arithmetic and copies ran while one was open for 0% of the time, Pallas kernels for 11%

profile of v5, /device:TPU:0, one launch (start us, length us, event | category | flops | bytes accessed | tf_op | source)
XLA Modules:
  0.0 70.0 jit_solution(4638690844077428222)
XLA Ops:
  0.0 0.0 copy-start.5
  0.0 1.4 %copy.25 = bf16[4,256,2,256]{3,1,0,2:T(8,128)(2,1)S(1)} copy(bf16[4,256,2,256]{3,2,1,0:T(2,128)(2,1)} %param.56) | data formatting | bytes 2097152 | tf_op args[0]
  1.4 4.8 %collective-permute-start.15 = (bf16[1024,256]{1,0:T(8,128)(2,1)S(1)}, bf16[1024,256]{1,0:T(8,128)(2,1)S(1)}, u32[]{:S(2)}, u32[]{:S(2)}) collective-permute-start(bf16[1024,256]{1,0:T(8,128)(2,1)S(1)} %bitcast.143), channel_id=1, source_target_pairs={{0,2},{1,3},{2,0},{3,1},{8,10},{9,11},{10,8},{11,9},{16,18},{17,19... | collective-permute-start | bytes 1572872 | tf_op jit(solution)/shard_map/ppermute | solution.py:412
  6.3 0.0 copy-done.5
  6.3 1.3 %shard_map.48 = (s32[16,256]{1,0:T(8,128)S(1)}, bf16[320,256]{1,0:T(8,128)(2,1)S(1)}, bf16[320,256]{1,0:T(8,128)(2,1)S(1)}) custom-call(s32[4,256]{1,0:T(4,128)S(1)} %copy-done.5, bf16[2,1024,256]{2,1,0:T(8,128)(2,1)S(1)} %bitcast.135), custom_call_target="tpu_custom_call" | custom-call | tf_op jit(solution)/shard_map/pallas_call | solution.py:381
  7.6 1.3 %collective-permute-start.12 = (bf16[1024,256]{1,0:T(8,128)(2,1)S(1)}, bf16[1024,256]{1,0:T(8,128)(2,1)S(1)}, u32[]{:S(2)}, u32[]{:S(2)}) collective-permute-start(bf16[1024,256]{1,0:T(8,128)(2,1)S(1)} %bitcast.144), channel_id=1, source_target_pairs={{0,4},{1,5},{2,6},{3,7},{8,12},{9,13},{10,14},{11,15},{16,20},{17,... | collective-permute-start | bytes 1572872 | tf_op jit(solution)/shard_map/ppermute | solution.py:412
  8.9 1.6 %collective-permute-start.14 = (bf16[320,256]{1,0:T(8,128)(2,1)S(1)}, bf16[320,256]{1,0:T(8,128)(2,1)S(1)}, u32[]{:S(2)}, u32[]{:S(2)}) collective-permute-start(bf16[320,256]{1,0:T(8,128)(2,1)S(1)} %get-tuple-element.420.parts_0_), channel_id=1, source_target_pairs={{0,8},{8,16},{16,24},{24,0},{1,9},{9,17},{17,25},{25,1},{2,10},{10... | collective-permute-start | bytes 491528 | tf_op jit(solution)/shard_map/ppermute | solution.py:431
  10.5 2.6 %collective-permute-start.18 = (bf16[320,256]{1,0:T(8,128)(2,1)S(1)}, bf16[320,256]{1,0:T(8,128)(2,1)S(1)}, u32[]{:S(2)}, u32[]{:S(2)}) collective-permute-start(bf16[320,256]{1,0:T(8,128)(2,1)S(1)} %get-tuple-element.420.parts_0_), channel_id=1, source_target_pairs={{0,16},{8,24},{16,0},{24,8},{1,17},{9,25},{17,1},{25,9},{2,18},{10... | collective-permute-start | bytes 491528 | tf_op jit(solution)/shard_map/ppermute | solution.py:431
  13.1 1.3 %collective-permute-start.19 = (bf16[320,256]{1,0:T(8,128)(2,1)S(1)}, bf16[320,256]{1,0:T(8,128)(2,1)S(1)}, u32[]{:S(2)}, u32[]{:S(2)}) collective-permute-start(bf16[320,256]{1,0:T(8,128)(2,1)S(1)} %get-tuple-element.420.parts_0_), channel_id=1, source_target_pairs={{0,24},{8,0},{16,8},{24,16},{1,25},{9,1},{17,9},{25,17},{2,26},{10... | collective-permute-start | bytes 491528 | tf_op jit(solution)/shard_map/ppermute | solution.py:431
  14.4 3.5 %collective-permute-done.14.parts_1_ = bf16[320,256]{1,0:T(8,128)(2,1)S(1)} collective-permute-done((bf16[320,256]{1,0:T(8,128)(2,1)S(1)}, bf16[320,256]{1,0:T(8,128)(2,1)S(1)}, u32[]{:S(2)}, u32[]{:S(2)}) %collective-permute-start.14) | collective-permute-done | bytes 163872 | tf_op jit(solution)/shard_map/ppermute | solution.py:431
  18.0 0.2 collective-permute-done.15
  18.2 5.4 %collective-permute-done.18.parts_2_ = bf16[320,256]{1,0:T(8,128)(2,1)S(1)} collective-permute-done((bf16[320,256]{1,0:T(8,128)(2,1)S(1)}, bf16[320,256]{1,0:T(8,128)(2,1)S(1)}, u32[]{:S(2)}, u32[]{:S(2)}) %collective-permute-start.18) | collective-permute-done | bytes 163872 | tf_op jit(solution)/shard_map/ppermute | solution.py:431
  23.6 0.0 collective-permute-done.19.parts_3_
  23.6 1.1 %shard_map.49 = (bf16[1024,256]{1,0:T(8,128)(2,1)S(1)}, bf16[768,256]{1,0:T(8,128)(2,1)S(1)}) custom-call(s32[16,256]{1,0:T(8,128)S(1)} %get-tuple-element.417.meta_ref, bf16[320,256]{1,0:T(8,128)(2,1)S(1)} %get-tuple-element.420.parts_0_, bf16[320,256]{1,0:T(8,128)(2,1)S(1)} %collective-permute-done.14.parts_1_, ...), custom_call_target="tpu_custom_call" | custom-call | tf_op jit(solution)/shard_map/pallas_call | solution.py:381
  24.7 1.3 %collective-permute-start.20 = (bf16[768,256]{1,0:T(8,128)(2,1)S(1)}, bf16[768,256]{1,0:T(8,128)(2,1)S(1)}, u32[]{:S(2)}, u32[]{:S(2)}) collective-permute-start(bf16[768,256]{1,0:T(8,128)(2,1)S(1)} %get-tuple-element.427), channel_id=1, source_target_pairs={{0,4},{1,5},{2,6},{3,7},{8,12},{9,13},{10,14},{11,15},{16,20},{17,... | collective-permute-start | bytes 1179656 | tf_op jit(solution)/shard_map/ppermute | solution.py:412
  26.0 3.1 %collective-permute-start.21 = (bf16[768,256]{1,0:T(8,128)(2,1)S(1)}, bf16[768,256]{1,0:T(8,128)(2,1)S(1)}, u32[]{:S(2)}, u32[]{:S(2)}) collective-permute-start(bf16[768,256]{1,0:T(8,128)(2,1)S(1)} %get-tuple-element.427), channel_id=1, source_target_pairs={{0,2},{1,3},{2,0},{3,1},{8,10},{9,11},{10,8},{11,9},{16,18},{17,19... | collective-permute-start | bytes 1179656 | tf_op jit(solution)/shard_map/ppermute | solution.py:412
  29.1 1.3 %collective-permute-start.22 = (bf16[768,256]{1,0:T(8,128)(2,1)S(1)}, bf16[768,256]{1,0:T(8,128)(2,1)S(1)}, u32[]{:S(2)}, u32[]{:S(2)}) collective-permute-start(bf16[768,256]{1,0:T(8,128)(2,1)S(1)} %get-tuple-element.427), channel_id=1, source_target_pairs={{0,6},{1,7},{2,4},{3,5},{8,14},{9,15},{10,12},{11,13},{16,22},{17,... | collective-permute-start | bytes 1179656 | tf_op jit(solution)/shard_map/ppermute | solution.py:412
  30.4 0.0 collective-permute-done.12
  30.4 0.7 collective-permute-start.16
  31.1 0.1 broadcast_select_fusion.5.raws_0_
  31.2 0.1 collective-permute-start.13
  31.3 19.8 %all_gather.3.buf_ref = bf16[1280,256]{1,0:T(8,128)(2,1)S(1)} all-gather(bf16[320,256]{1,0:T(8,128)(2,1)S(1)} %get-tuple-element.426), channel_id=1, replica_groups=mesh['prow'=4,'pcol'=8] {'prow'}, dimensions={0}, use_global_device_ids=true | all-gather | bytes 819200 | tf_op jit(solution)/shard_map/all_gather | solution.py:446
  51.1 0.0 collective-permute-done.20
  51.1 0.0 collective-permute-done.21
  51.1 0.0 collective-permute-done.22
  51.1 0.0 copy-start.1
  51.1 0.1 collective-permute-start.24
  51.2 0.0 collective-permute-done.16
  51.2 0.1 broadcast_select_fusion.4.raws_2_
  51.3 0.5 collective-permute-start.17
  51.9 0.1 collective-permute-start.23
  52.0 1.0 %shard_map.50.top1_ref = bf16[1024,256]{1,0:T(8,128)(2,1)S(1)} custom-call(s32[16,256]{1,0:T(8,128)S(1)} %get-tuple-element.417.meta_ref, bf16[1280,256]{1,0:T(8,128)(2,1)S(1)} %all_gather.3.buf_ref), custom_call_target="tpu_custom_call" | custom-call | tf_op jit(solution)/shard_map/pallas_call | solution.py:381
  52.9 0.0 collective-permute-done.13.raws_1_
  52.9 0.0 collective-permute-done.24.offs_3_
  53.0 1.3 %collective-permute-done.23.offs_1_ = bf16[768,256]{1,0:T(8,128)(2,1)S(1)} collective-permute-done((bf16[768,256]{1,0:T(8,128)(2,1)S(1)}, bf16[768,256]{1,0:T(8,128)(2,1)S(1)}, u32[]{:S(2)}, u32[]{:S(2)}) %collective-permute-start.23) | collective-permute-done | bytes 393248 | tf_op jit(solution)/shard_map/ppermute | solution.py:415
  54.2 0.0 collective-permute-done.17.raws_3_
  54.2 0.0 copy-done.1
  54.2 3.7 %shard_map.51 = (bf16[1024,1536]{1,0:T(8,128)(2,1)S(1)}, bf16[256,512]{1,0:T(8,128)(2,1)S(1)}, bf16[256,512]{1,0:T(8,128)(2,1)S(1)}, bf16[4,80,512]{2,1,0:T(8,128)(2,1)S(1)}) custom-call(s32[4,256]{1,0:T(4,128)S(1)} %copy-done.5, bf16[1024,256]{1,0:T(8,128)(2,1)S(1)} %get-tuple-element.423.top0_ref, bf16[1024,256]{1,0:T(8,128)(2,1)S(1)} %shard_map.50.top1_ref, ...), custom_call_target="tpu_custom_call" | custom-call | tf_op jit(solution)/shard_map/pallas_call | solution.py:381
  58.0 0.5 collective-permute-start.25
  58.5 2.6 %collective-permute-start.26 = (bf16[80,512]{1,0:T(8,128)(2,1)S(1)}, bf16[80,512]{1,0:T(8,128)(2,1)S(1)}, u32[]{:S(2)}, u32[]{:S(2)}) collective-permute-start(bf16[80,512]{1,0:T(8,128)(2,1)S(1)} %get-tuple-element.563), channel_id=1, source_target_pairs={{0,16},{8,24},{16,0},{24,8},{1,17},{9,25},{17,1},{25,9},{2,18},{10... | collective-permute-start | bytes 245768 | tf_op jit(solution)/shard_map/ppermute | solution.py:474
  61.1 0.8 %collective-permute-start.27 = (bf16[80,512]{1,0:T(8,128)(2,1)S(1)}, bf16[80,512]{1,0:T(8,128)(2,1)S(1)}, u32[]{:S(2)}, u32[]{:S(2)}) collective-permute-start(bf16[80,512]{1,0:T(8,128)(2,1)S(1)} %get-tuple-element.562), channel_id=1, source_target_pairs={{0,24},{8,0},{16,8},{24,16},{1,25},{9,1},{17,9},{25,17},{2,26},{10... | collective-permute-start | bytes 245768 | tf_op jit(solution)/shard_map/ppermute | solution.py:474
  61.9 0.0 copy-start
  61.9 4.5 %shard_map.52 = (bf16[768,512]{1,0:T(8,128)(2,1)S(1)}, s32[1,512]{1,0:T(1,128)S(1)}, s32[1]{0:T(128)}) custom-call(s32[4,256]{1,0:T(4,128)S(1)} %copy-done.5, s32[16,256]{1,0:T(8,128)S(1)} %get-tuple-element.417.meta_ref, bf16[2,1024,256]{2,1,0:T(8,128)(2,1)S(1)} %bitcast.137, bf16[1024,256]{1,0:T(8,128)(2,1)S(1)} %broadcast_select_fusion.5.raws_0_, ...), custom_call_target="tpu_custom_call" | custom-call | flops 2415919104 | bytes 4194304 | tf_op jit(solution)/shard_map/pallas_call | solution.py:381
  67.0 0.0 collective-permute-done.25
  67.1 0.9 %collective-permute-done.26 = bf16[80,512]{1,0:T(8,128)(2,1)S(1)} collective-permute-done((bf16[80,512]{1,0:T(8,128)(2,1)S(1)}, bf16[80,512]{1,0:T(8,128)(2,1)S(1)}, u32[]{:S(2)}, u32[]{:S(2)}) %collective-permute-start.26) | collective-permute-done | bytes 81952 | tf_op jit(solution)/shard_map/ppermute | solution.py:474
  68.0 0.0 collective-permute-done.27
  68.0 0.0 copy-done
  68.0 1.1 %conditional.1 = (bf16[4,256,2,256]{3,2,1,0:T(2,128)(2,1)S(1)}) conditional(s32[]{:T(128)} %bitcast.29, (bf16[4,80,512]{2,1,0:T(8,128)(2,1)S(1)}, s32[1,512]{1,0:T(1,128)S(1)}, bf16[256,512]{1,0:T(8,128)(2,1)S(1)}, bf16[768,512]{1,0:T(8,128)(2,1)S(1)}, bf16[256,512]{1,0:T(8,128)(2,1)S(1)}, /*index=5*/bf16[80,512]{1,0:T(8,128)(2,1)S(1)}, ...), branch_computations={%region_0.1_spmd, %region_1.32_spmd} | conditional | flops 1896568576 | bytes 99436336 | solution.py:502
  68.0 0.8 %branch_0_fun.1 = bf16[1024,512]{1,0:T(8,128)(2,1)S(1)} custom-call(s32[1,512]{1,0:T(1,128)S(1)} %get-tuple-element.323.target_ref, bf16[256,512]{1,0:T(8,128)(2,1)S(1)} %get-tuple-element.324.head_ref, bf16[768,512]{1,0:T(8,128)(2,1)S(1)} %get-tuple-element.325.res_ref, bf16[256,512]{1,0:T(8,128)(2,1)S(1)} %get-tuple-element.326.top_ref, ...), custom_call_target="tpu_custom_call" | custom-call | tf_op jit(solution)/shard_map/cond/branch_0_fun/pallas_call | solution.py:381
  68.8 0.3 reshape.1231
  69.1 0.0 copy-start.4
  69.1 1.0 %copy-done.4 = bf16[4,256,2,256]{3,2,1,0:T(2,128)(2,1)} copy-done((bf16[4,256,2,256]{3,2,1,0:T(2,128)(2,1)}, bf16[4,256,2,256]{3,2,1,0:T(2,128)(2,1)S(1)}, u32[]{:S(2)}) %copy-start.4) | copy-done | bytes 1048600
  (5 shorter events, 0.1 us)
Async XLA Ops:
  0.0 6.3 %copy-start.5 = (s32[4,256]{1,0:T(4,128)S(1)}, s32[4,256]{1,0:T(4,128)}, u32[]{:S(2)}) copy-start(s32[4,256]{1,0:T(4,128)} %piv_ref.5) | copy-start | bytes 12292
  1.4 16.8 %collective-permute-start.15 = (bf16[1024,256]{1,0:T(8,128)(2,1)S(1)}, bf16[1024,256]{1,0:T(8,128)(2,1)S(1)}, u32[]{:S(2)}, u32[]{:S(2)}) collective-permute-start(bf16[1024,256]{1,0:T(8,128)(2,1)S(1)} %bitcast.143), channel_id=1, source_target_pairs={{0,2},{1,3},{2,0},{3,1},{8,10},{9,11},{10,8},{11,9},{16,18},{17,19... | collective-permute-start | bytes 1572872 | tf_op jit(solution)/shard_map/ppermute | solution.py:412
  7.6 22.8 %collective-permute-start.12 = (bf16[1024,256]{1,0:T(8,128)(2,1)S(1)}, bf16[1024,256]{1,0:T(8,128)(2,1)S(1)}, u32[]{:S(2)}, u32[]{:S(2)}) collective-permute-start(bf16[1024,256]{1,0:T(8,128)(2,1)S(1)} %bitcast.144), channel_id=1, source_target_pairs={{0,4},{1,5},{2,6},{3,7},{8,12},{9,13},{10,14},{11,15},{16,20},{17,... | collective-permute-start | bytes 1572872 | tf_op jit(solution)/shard_map/ppermute | solution.py:412
  8.9 9.1 %collective-permute-start.14 = (bf16[320,256]{1,0:T(8,128)(2,1)S(1)}, bf16[320,256]{1,0:T(8,128)(2,1)S(1)}, u32[]{:S(2)}, u32[]{:S(2)}) collective-permute-start(bf16[320,256]{1,0:T(8,128)(2,1)S(1)} %get-tuple-element.420.parts_0_), channel_id=1, source_target_pairs={{0,8},{8,16},{16,24},{24,0},{1,9},{9,17},{17,25},{25,1},{2,10},{10... | collective-permute-start | bytes 491528 | tf_op jit(solution)/shard_map/ppermute | solution.py:431
  10.5 13.1 %collective-permute-start.18 = (bf16[320,256]{1,0:T(8,128)(2,1)S(1)}, bf16[320,256]{1,0:T(8,128)(2,1)S(1)}, u32[]{:S(2)}, u32[]{:S(2)}) collective-permute-start(bf16[320,256]{1,0:T(8,128)(2,1)S(1)} %get-tuple-element.420.parts_0_), channel_id=1, source_target_pairs={{0,16},{8,24},{16,0},{24,8},{1,17},{9,25},{17,1},{25,9},{2,18},{10... | collective-permute-start | bytes 491528 | tf_op jit(solution)/shard_map/ppermute | solution.py:431
  13.1 10.5 %collective-permute-start.19 = (bf16[320,256]{1,0:T(8,128)(2,1)S(1)}, bf16[320,256]{1,0:T(8,128)(2,1)S(1)}, u32[]{:S(2)}, u32[]{:S(2)}) collective-permute-start(bf16[320,256]{1,0:T(8,128)(2,1)S(1)} %get-tuple-element.420.parts_0_), channel_id=1, source_target_pairs={{0,24},{8,0},{16,8},{24,16},{1,25},{9,1},{17,9},{25,17},{2,26},{10... | collective-permute-start | bytes 491528 | tf_op jit(solution)/shard_map/ppermute | solution.py:431
  24.7 26.4 %collective-permute-start.20 = (bf16[768,256]{1,0:T(8,128)(2,1)S(1)}, bf16[768,256]{1,0:T(8,128)(2,1)S(1)}, u32[]{:S(2)}, u32[]{:S(2)}) collective-permute-start(bf16[768,256]{1,0:T(8,128)(2,1)S(1)} %get-tuple-element.427), channel_id=1, source_target_pairs={{0,4},{1,5},{2,6},{3,7},{8,12},{9,13},{10,14},{11,15},{16,20},{17,... | collective-permute-start | bytes 1179656 | tf_op jit(solution)/shard_map/ppermute | solution.py:412
  26.0 25.1 %collective-permute-start.21 = (bf16[768,256]{1,0:T(8,128)(2,1)S(1)}, bf16[768,256]{1,0:T(8,128)(2,1)S(1)}, u32[]{:S(2)}, u32[]{:S(2)}) collective-permute-start(bf16[768,256]{1,0:T(8,128)(2,1)S(1)} %get-tuple-element.427), channel_id=1, source_target_pairs={{0,2},{1,3},{2,0},{3,1},{8,10},{9,11},{10,8},{11,9},{16,18},{17,19... | collective-permute-start | bytes 1179656 | tf_op jit(solution)/shard_map/ppermute | solution.py:412
  29.1 22.0 %collective-permute-start.22 = (bf16[768,256]{1,0:T(8,128)(2,1)S(1)}, bf16[768,256]{1,0:T(8,128)(2,1)S(1)}, u32[]{:S(2)}, u32[]{:S(2)}) collective-permute-start(bf16[768,256]{1,0:T(8,128)(2,1)S(1)} %get-tuple-element.427), channel_id=1, source_target_pairs={{0,6},{1,7},{2,4},{3,5},{8,14},{9,15},{10,12},{11,13},{16,22},{17,... | collective-permute-start | bytes 1179656 | tf_op jit(solution)/shard_map/ppermute | solution.py:412
  30.4 20.8 %collective-permute-start.16 = (bf16[1024,256]{1,0:T(8,128)(2,1)S(1)}, bf16[1024,256]{1,0:T(8,128)(2,1)S(1)}, u32[]{:S(2)}, u32[]{:S(2)}) collective-permute-start(bf16[1024,256]{1,0:T(8,128)(2,1)S(1)} %collective-permute-done.12), channel_id=1, source_target_pairs={{4,6},{5,7},{6,4},{7,5},{12,14},{13,15},{14,12},{15,13},{20,22},{2... | collective-permute-start | bytes 1572872 | tf_op jit(solution)/shard_map/ppermute | solution.py:435
  31.2 21.7 %collective-permute-start.13 = (bf16[1024,256]{1,0:T(8,128)(2,1)S(1)}, bf16[1024,256]{1,0:T(8,128)(2,1)S(1)}, u32[]{:S(2)}, u32[]{:S(2)}) collective-permute-start(bf16[1024,256]{1,0:T(8,128)(2,1)S(1)} %broadcast_select_fusion.5.raws_0_), channel_id=1, source_target_pairs={{0,1},{1,0},{2,3},{3,2},{4,5},{5,4},{6,7},{7,6},{8,9},{9,8},{10,11... | collective-permute-start | bytes 1572872 | tf_op jit(solution)/shard_map/ppermute | solution.py:415
  51.1 3.1 %copy-start.1 = (bf16[4,256,256]{2,1,0:T(8,128)(2,1)S(1)}, bf16[4,256,256]{2,1,0:T(8,128)(2,1)}, u32[]{:S(2)}) copy-start(bf16[4,256,256]{2,1,0:T(8,128)(2,1)} %uinv_ref.3) | copy-start | bytes 1572868
  51.1 1.8 %collective-permute-start.24 = (bf16[768,256]{1,0:T(8,128)(2,1)S(1)}, bf16[768,256]{1,0:T(8,128)(2,1)S(1)}, u32[]{:S(2)}, u32[]{:S(2)}) collective-permute-start(bf16[768,256]{1,0:T(8,128)(2,1)S(1)} %broadcast_select_fusion.6.offs_2_), channel_id=1, source_target_pairs={{0,1},{1,0},{2,3},{3,2},{4,5},{5,4},{6,7},{7,6},{8,9},{9,8},{10,11... | collective-permute-start | bytes 1179656 | tf_op jit(solution)/shard_map/ppermute | solution.py:415
  51.3 2.9 %collective-permute-start.17 = (bf16[1024,256]{1,0:T(8,128)(2,1)S(1)}, bf16[1024,256]{1,0:T(8,128)(2,1)S(1)}, u32[]{:S(2)}, u32[]{:S(2)}) collective-permute-start(bf16[1024,256]{1,0:T(8,128)(2,1)S(1)} %broadcast_select_fusion.4.raws_2_), channel_id=1, source_target_pairs={{0,1},{1,0},{2,3},{3,2},{4,5},{5,4},{6,7},{7,6},{8,9},{9,8},{10,11... | collective-permute-start | bytes 1572872 | tf_op jit(solution)/shard_map/ppermute | solution.py:415
  51.9 2.4 %collective-permute-start.23 = (bf16[768,256]{1,0:T(8,128)(2,1)S(1)}, bf16[768,256]{1,0:T(8,128)(2,1)S(1)}, u32[]{:S(2)}, u32[]{:S(2)}) collective-permute-start(bf16[768,256]{1,0:T(8,128)(2,1)S(1)} %broadcast_select_fusion.7.offs_0_), channel_id=1, source_target_pairs={{0,1},{1,0},{2,3},{3,2},{4,5},{5,4},{6,7},{7,6},{8,9},{9,8},{10,11... | collective-permute-start | bytes 1179656 | tf_op jit(solution)/shard_map/ppermute | solution.py:415
  58.0 9.0 %collective-permute-start.25 = (bf16[80,512]{1,0:T(8,128)(2,1)S(1)}, bf16[80,512]{1,0:T(8,128)(2,1)S(1)}, u32[]{:S(2)}, u32[]{:S(2)}) collective-permute-start(bf16[80,512]{1,0:T(8,128)(2,1)S(1)} %get-tuple-element.564), channel_id=1, source_target_pairs={{0,8},{8,16},{16,24},{24,0},{1,9},{9,17},{17,25},{25,1},{2,10},{10... | collective-permute-start | bytes 245768 | tf_op jit(solution)/shard_map/ppermute | solution.py:474
  58.5 9.5 %collective-permute-start.26 = (bf16[80,512]{1,0:T(8,128)(2,1)S(1)}, bf16[80,512]{1,0:T(8,128)(2,1)S(1)}, u32[]{:S(2)}, u32[]{:S(2)}) collective-permute-start(bf16[80,512]{1,0:T(8,128)(2,1)S(1)} %get-tuple-element.563), channel_id=1, source_target_pairs={{0,16},{8,24},{16,0},{24,8},{1,17},{9,25},{17,1},{25,9},{2,18},{10... | collective-permute-start | bytes 245768 | tf_op jit(solution)/shard_map/ppermute | solution.py:474
  61.1 6.9 %collective-permute-start.27 = (bf16[80,512]{1,0:T(8,128)(2,1)S(1)}, bf16[80,512]{1,0:T(8,128)(2,1)S(1)}, u32[]{:S(2)}, u32[]{:S(2)}) collective-permute-start(bf16[80,512]{1,0:T(8,128)(2,1)S(1)} %get-tuple-element.562), channel_id=1, source_target_pairs={{0,24},{8,0},{16,8},{24,16},{1,25},{9,1},{17,9},{25,17},{2,26},{10... | collective-permute-start | bytes 245768 | tf_op jit(solution)/shard_map/ppermute | solution.py:474
  61.9 6.1 %copy-start = (bf16[4,256,2,256]{3,2,1,0:T(2,128)(2,1)S(1)}, bf16[4,256,2,256]{3,2,1,0:T(2,128)(2,1)}, u32[]{:S(2)}) copy-start(bf16[4,256,2,256]{3,2,1,0:T(2,128)(2,1)} %param.56) | copy-start | bytes 3145732
  69.1 1.0 %copy-start.4 = (bf16[4,256,2,256]{3,2,1,0:T(2,128)(2,1)}, bf16[4,256,2,256]{3,2,1,0:T(2,128)(2,1)S(1)}, u32[]{:S(2)}) copy-start(bf16[4,256,2,256]{3,2,1,0:T(2,128)(2,1)S(1)} %get-tuple-element.970) | copy-start | bytes 3145732

commit v6 on v5

--- a/solution.py
+++ b/solution.py
@@ -11,7 +11,7 @@
 F32 = jnp.float32
 I32 = jnp.int32
 VMEM_BYTES = 24 * 1024 * 1024
-MOVE_ROWS = 80
+MOVE_ROWS = 64
 MOVE_SLOTS = 128
 
 
@@ -404,7 +404,7 @@
     if steps != 4 or col_blocks != 2 or n_row < steps or n_col < 8 or n_col % 4:
         return stepwise(matrix, pivots, lower_inverse, upper_inverse)
     local_rows = row_blocks * nb
-    cap = -(-(steps * nb // n_row + 64) // 16) * 16
+    cap = -(-(steps * nb // n_row + 48) // 16) * 16
     mat = jnp.transpose(matrix, (2, 0, 1, 3)).reshape(col_blocks, local_rows, nb)
     m0 = mat[0]
 
@@ -440,11 +440,11 @@
         scratch=(pltpu.VMEM((n_row * cap, nb), BF16),),
     )
     pack1, off = lax.optimization_barrier((pack1, off))
+    off_far = functools.reduce(jnp.add, [from_panels(off, mask) for mask in fours])
     off_x = from_panels(off, 2)
-    off_far = functools.reduce(jnp.add, [from_panels(off, mask) for mask in fours])
     off_far_x = functools.reduce(jnp.add, [from_panels(off, mask + 2) for mask in fours])
     buf1 = lax.all_gather(pack1, "prow", tiled=True)
-    buf1, off_far, off_x, off_far_x = lax.optimization_barrier((buf1, off_far, off_x, off_far_x))
+    buf1, off_x, off_far_x, off_far = lax.optimization_barrier((buf1, off_x, off_far_x, off_far))
     raw_0, raw_2 = panel_pair(m0, raw_x, raw_far, raw_far_x)
     off_0, off_2 = panel_pair(off, off_x, off_far, off_far_x)
     raws = (raw_0, swap_cores(raw_0), raw_2, swap_cores(raw_2))

time: 70.4 us -> 68.3 us (0.970)
  waiting for transfers between devices: 11.4 us -> 9.89 us
    ppermute x3, waiting for transfers between devices: 0.93 us -> 0.01 us  [local(): lax.ppermute(send[k], 'prow', [(i, (i + k) % n_row) for i in range(n_row)])]
    ppermute x3, waiting for transfers between devices: 8.88 us -> 8.17 us  [local(): lax.ppermute(pack0, 'prow', [(i, (i + k) % n_row) for i in range(n_row)])]
  transfers between devices with their start and end apart: 16 -> 16, of which waited for: 5 -> 4; matrix products, arithmetic and copies ran while one was open for 0% -> 0% of each run, Pallas kernels for 11% -> 11%
where the time goes in v6:
time: 68.3 us; the launch traced here: 68 us
  starting transfers between devices  22.5 us (33%)
  blocking collectives  19.3 us (28%)
  Pallas kernels  12.3 us (18%)
  waiting for transfers between devices  9.89 us (14%)
  local copies, waits for them, and re-layouts  2.7 us (4%)
  between operations  0.89 us (1%)
    all_gather x1, blocking collectives, local(): buf1 = lax.all_gather(pack1, 'prow', tiled=True)  19.3 us
    pallas_call x6, Pallas kernels, call(): pl.pallas_call(kernel, out_shape=outs, in_specs=[jax.tree.map(lambda _: a...  12.3 us
    ppermute x5, starting transfers between devices, from_panels(): return lax.ppermute(value, 'pcol', [(i, i ^ mask) for i in range(steps)])  11.6 us
    ppermute x3, waiting for transfers between devices, local(): lax.ppermute(pack0, 'prow', [(i, (i + k) % n_row) for i in range(n_row)])  8.17 us
    ppermute x3, starting transfers between devices, local(): lax.ppermute(pack0, 'prow', [(i, (i + k) % n_row) for i in range(n_row)])  5.57 us
    ppermute x3, starting transfers between devices, local(): lax.ppermute(send[k], 'prow', [(i, (i + k) % n_row) for i in range(n_row)])  3.88 us
    unnamed x9, local copies, waits for them, and re-layouts  2.35 us
  transfers between devices with their start and end apart: 16, of which 4 were waited for; matrix products, arithmetic and copies ran while one was open for 0% of the time, Pallas kernels for 11%

profile of v6, /device:TPU:0, one launch (start us, length us, event | category | flops | bytes accessed | tf_op | source)
XLA Modules:
  0.0 68.0 jit_solution(8042506934800398443)
XLA Ops:
  0.0 0.0 copy-start.5
  0.0 1.4 %copy.25 = bf16[4,256,2,256]{3,1,0,2:T(8,128)(2,1)S(1)} copy(bf16[4,256,2,256]{3,2,1,0:T(2,128)(2,1)} %param.56) | data formatting | bytes 2097152 | tf_op args[0]
  1.4 4.8 %collective-permute-start.15 = (bf16[1024,256]{1,0:T(8,128)(2,1)S(1)}, bf16[1024,256]{1,0:T(8,128)(2,1)S(1)}, u32[]{:S(2)}, u32[]{:S(2)}) collective-permute-start(bf16[1024,256]{1,0:T(8,128)(2,1)S(1)} %bitcast.143), channel_id=1, source_target_pairs={{0,2},{1,3},{2,0},{3,1},{8,10},{9,11},{10,8},{11,9},{16,18},{17,19... | collective-permute-start | bytes 1572872 | tf_op jit(solution)/shard_map/ppermute | solution.py:412
  6.3 0.0 copy-done.5
  6.3 1.2 %shard_map.48 = (s32[16,256]{1,0:T(8,128)S(1)}, bf16[304,256]{1,0:T(8,128)(2,1)S(1)}, bf16[304,256]{1,0:T(8,128)(2,1)S(1)}) custom-call(s32[4,256]{1,0:T(4,128)S(1)} %copy-done.5, bf16[2,1024,256]{2,1,0:T(8,128)(2,1)S(1)} %bitcast.135), custom_call_target="tpu_custom_call" | custom-call | tf_op jit(solution)/shard_map/pallas_call | solution.py:381
  7.5 1.3 %collective-permute-start.12 = (bf16[1024,256]{1,0:T(8,128)(2,1)S(1)}, bf16[1024,256]{1,0:T(8,128)(2,1)S(1)}, u32[]{:S(2)}, u32[]{:S(2)}) collective-permute-start(bf16[1024,256]{1,0:T(8,128)(2,1)S(1)} %bitcast.144), channel_id=1, source_target_pairs={{0,4},{1,5},{2,6},{3,7},{8,12},{9,13},{10,14},{11,15},{16,20},{17,... | collective-permute-start | bytes 1572872 | tf_op jit(solution)/shard_map/ppermute | solution.py:412
  8.9 1.6 %collective-permute-start.14 = (bf16[304,256]{1,0:T(8,128)(2,1)S(1)}, bf16[304,256]{1,0:T(8,128)(2,1)S(1)}, u32[]{:S(2)}, u32[]{:S(2)}) collective-permute-start(bf16[304,256]{1,0:T(8,128)(2,1)S(1)} %get-tuple-element.420.parts_0_), channel_id=1, source_target_pairs={{0,8},{8,16},{16,24},{24,0},{1,9},{9,17},{17,25},{25,1},{2,10},{10... | collective-permute-start | bytes 466952 | tf_op jit(solution)/shard_map/ppermute | solution.py:431
  10.5 2.6 %collective-permute-start.18 = (bf16[304,256]{1,0:T(8,128)(2,1)S(1)}, bf16[304,256]{1,0:T(8,128)(2,1)S(1)}, u32[]{:S(2)}, u32[]{:S(2)}) collective-permute-start(bf16[304,256]{1,0:T(8,128)(2,1)S(1)} %get-tuple-element.420.parts_0_), channel_id=1, source_target_pairs={{0,16},{8,24},{16,0},{24,8},{1,17},{9,25},{17,1},{25,9},{2,18},{10... | collective-permute-start | bytes 466952 | tf_op jit(solution)/shard_map/ppermute | solution.py:431
  13.1 1.3 %collective-permute-start.19 = (bf16[304,256]{1,0:T(8,128)(2,1)S(1)}, bf16[304,256]{1,0:T(8,128)(2,1)S(1)}, u32[]{:S(2)}, u32[]{:S(2)}) collective-permute-start(bf16[304,256]{1,0:T(8,128)(2,1)S(1)} %get-tuple-element.420.parts_0_), channel_id=1, source_target_pairs={{0,24},{8,0},{16,8},{24,16},{1,25},{9,1},{17,9},{25,17},{2,26},{10... | collective-permute-start | bytes 466952 | tf_op jit(solution)/shard_map/ppermute | solution.py:431
  14.4 3.3 %collective-permute-done.14.parts_1_ = bf16[304,256]{1,0:T(8,128)(2,1)S(1)} collective-permute-done((bf16[304,256]{1,0:T(8,128)(2,1)S(1)}, bf16[304,256]{1,0:T(8,128)(2,1)S(1)}, u32[]{:S(2)}, u32[]{:S(2)}) %collective-permute-start.14) | collective-permute-done | bytes 155680 | tf_op jit(solution)/shard_map/ppermute | solution.py:431
  17.8 0.4 collective-permute-done.15
  18.2 4.8 %collective-permute-done.18.parts_2_ = bf16[304,256]{1,0:T(8,128)(2,1)S(1)} collective-permute-done((bf16[304,256]{1,0:T(8,128)(2,1)S(1)}, bf16[304,256]{1,0:T(8,128)(2,1)S(1)}, u32[]{:S(2)}, u32[]{:S(2)}) %collective-permute-start.18) | collective-permute-done | bytes 155680 | tf_op jit(solution)/shard_map/ppermute | solution.py:431
  23.0 0.0 collective-permute-done.19.parts_3_
  23.0 1.1 %shard_map.49 = (bf16[1024,256]{1,0:T(8,128)(2,1)S(1)}, bf16[768,256]{1,0:T(8,128)(2,1)S(1)}) custom-call(s32[16,256]{1,0:T(8,128)S(1)} %get-tuple-element.417.meta_ref, bf16[304,256]{1,0:T(8,128)(2,1)S(1)} %get-tuple-element.420.parts_0_, bf16[304,256]{1,0:T(8,128)(2,1)S(1)} %collective-permute-done.14.parts_1_, ...), custom_call_target="tpu_custom_call" | custom-call | tf_op jit(solution)/shard_map/pallas_call | solution.py:381
  24.1 2.8 %collective-permute-start.20 = (bf16[768,256]{1,0:T(8,128)(2,1)S(1)}, bf16[768,256]{1,0:T(8,128)(2,1)S(1)}, u32[]{:S(2)}, u32[]{:S(2)}) collective-permute-start(bf16[768,256]{1,0:T(8,128)(2,1)S(1)} %get-tuple-element.427), channel_id=1, source_target_pairs={{0,2},{1,3},{2,0},{3,1},{8,10},{9,11},{10,8},{11,9},{16,18},{17,19... | collective-permute-start | bytes 1179656 | tf_op jit(solution)/shard_map/ppermute | solution.py:412
  27.0 1.3 %collective-permute-start.21 = (bf16[768,256]{1,0:T(8,128)(2,1)S(1)}, bf16[768,256]{1,0:T(8,128)(2,1)S(1)}, u32[]{:S(2)}, u32[]{:S(2)}) collective-permute-start(bf16[768,256]{1,0:T(8,128)(2,1)S(1)} %get-tuple-element.427), channel_id=1, source_target_pairs={{0,6},{1,7},{2,4},{3,5},{8,14},{9,15},{10,12},{11,13},{16,22},{17,... | collective-permute-start | bytes 1179656 | tf_op jit(solution)/shard_map/ppermute | solution.py:412
  28.3 1.3 %collective-permute-start.22 = (bf16[768,256]{1,0:T(8,128)(2,1)S(1)}, bf16[768,256]{1,0:T(8,128)(2,1)S(1)}, u32[]{:S(2)}, u32[]{:S(2)}) collective-permute-start(bf16[768,256]{1,0:T(8,128)(2,1)S(1)} %get-tuple-element.427), channel_id=1, source_target_pairs={{0,4},{1,5},{2,6},{3,7},{8,12},{9,13},{10,14},{11,15},{16,20},{17,... | collective-permute-start | bytes 1179656 | tf_op jit(solution)/shard_map/ppermute | solution.py:412
  29.6 0.0 collective-permute-done.12
  29.6 0.7 %collective-permute-start.16 = (bf16[1024,256]{1,0:T(8,128)(2,1)S(1)}, bf16[1024,256]{1,0:T(8,128)(2,1)S(1)}, u32[]{:S(2)}, u32[]{:S(2)}) collective-permute-start(bf16[1024,256]{1,0:T(8,128)(2,1)S(1)} %collective-permute-done.12), channel_id=1, source_target_pairs={{4,6},{5,7},{6,4},{7,5},{12,14},{13,15},{14,12},{15,13},{20,22},{2... | collective-permute-start | bytes 1572872 | tf_op jit(solution)/shard_map/ppermute | solution.py:435
  30.3 0.1 broadcast_select_fusion.5.raws_0_
  30.4 0.1 collective-permute-start.13
  30.5 19.3 %all_gather.3.buf_ref = bf16[1216,256]{1,0:T(8,128)(2,1)S(1)} all-gather(bf16[304,256]{1,0:T(8,128)(2,1)S(1)} %get-tuple-element.426), channel_id=1, replica_groups=mesh['prow'=4,'pcol'=8] {'prow'}, dimensions={0}, use_global_device_ids=true | all-gather | bytes 778240 | tf_op jit(solution)/shard_map/all_gather | solution.py:446
  49.8 0.0 collective-permute-done.20
  49.8 0.0 collective-permute-done.21
  49.8 0.0 collective-permute-done.22
  49.8 0.0 copy-start.1
  49.8 0.1 collective-permute-start.24
  49.9 0.0 collective-permute-done.16
  49.9 0.1 broadcast_select_fusion.4.raws_2_
  50.0 0.6 collective-permute-start.17
  50.6 0.1 broadcast_select_fusion.7.offs_0_
  50.6 0.1 collective-permute-start.23
  50.7 1.0 %shard_map.50.top1_ref = bf16[1024,256]{1,0:T(8,128)(2,1)S(1)} custom-call(s32[16,256]{1,0:T(8,128)S(1)} %get-tuple-element.417.meta_ref, bf16[1216,256]{1,0:T(8,128)(2,1)S(1)} %all_gather.3.buf_ref), custom_call_target="tpu_custom_call" | custom-call | tf_op jit(solution)/shard_map/pallas_call | solution.py:381
  51.7 0.0 collective-permute-done.13.raws_1_
  51.7 0.0 collective-permute-done.24.offs_3_
  51.7 1.3 %collective-permute-done.23.offs_1_ = bf16[768,256]{1,0:T(8,128)(2,1)S(1)} collective-permute-done((bf16[768,256]{1,0:T(8,128)(2,1)S(1)}, bf16[768,256]{1,0:T(8,128)(2,1)S(1)}, u32[]{:S(2)}, u32[]{:S(2)}) %collective-permute-start.23) | collective-permute-done | bytes 393248 | tf_op jit(solution)/shard_map/ppermute | solution.py:415
  52.9 0.0 collective-permute-done.17.raws_3_
  52.9 0.0 copy-done.1
  52.9 3.7 %shard_map.51 = (bf16[1024,1536]{1,0:T(8,128)(2,1)S(1)}, bf16[256,512]{1,0:T(8,128)(2,1)S(1)}, bf16[256,512]{1,0:T(8,128)(2,1)S(1)}, bf16[4,64,512]{2,1,0:T(8,128)(2,1)S(1)}) custom-call(s32[4,256]{1,0:T(4,128)S(1)} %copy-done.5, bf16[1024,256]{1,0:T(8,128)(2,1)S(1)} %get-tuple-element.423.top0_ref, bf16[1024,256]{1,0:T(8,128)(2,1)S(1)} %shard_map.50.top1_ref, ...), custom_call_target="tpu_custom_call" | custom-call | tf_op jit(solution)/shard_map/pallas_call | solution.py:381
  56.7 0.6 collective-permute-start.25
  57.3 2.5 %collective-permute-start.26 = (bf16[64,512]{1,0:T(8,128)(2,1)S(1)}, bf16[64,512]{1,0:T(8,128)(2,1)S(1)}, u32[]{:S(2)}, u32[]{:S(2)}) collective-permute-start(bf16[64,512]{1,0:T(8,128)(2,1)S(1)} %get-tuple-element.563), channel_id=1, source_target_pairs={{0,16},{8,24},{16,0},{24,8},{1,17},{9,25},{17,1},{25,9},{2,18},{10... | collective-permute-start | bytes 196616 | tf_op jit(solution)/shard_map/ppermute | solution.py:474
  59.8 0.8 %collective-permute-start.27 = (bf16[64,512]{1,0:T(8,128)(2,1)S(1)}, bf16[64,512]{1,0:T(8,128)(2,1)S(1)}, u32[]{:S(2)}, u32[]{:S(2)}) collective-permute-start(bf16[64,512]{1,0:T(8,128)(2,1)S(1)} %get-tuple-element.562), channel_id=1, source_target_pairs={{0,24},{8,0},{16,8},{24,16},{1,25},{9,1},{17,9},{25,17},{2,26},{10... | collective-permute-start | bytes 196616 | tf_op jit(solution)/shard_map/ppermute | solution.py:474
  60.6 0.0 copy-start
  60.6 4.5 %shard_map.52 = (bf16[768,512]{1,0:T(8,128)(2,1)S(1)}, s32[1,512]{1,0:T(1,128)S(1)}, s32[1]{0:T(128)}) custom-call(s32[4,256]{1,0:T(4,128)S(1)} %copy-done.5, s32[16,256]{1,0:T(8,128)S(1)} %get-tuple-element.417.meta_ref, bf16[2,1024,256]{2,1,0:T(8,128)(2,1)S(1)} %bitcast.137, bf16[1024,256]{1,0:T(8,128)(2,1)S(1)} %broadcast_select_fusion.5.raws_0_, ...), custom_call_target="tpu_custom_call" | custom-call | flops 2415919104 | bytes 4194304 | tf_op jit(solution)/shard_map/pallas_call | solution.py:381
  65.7 0.0 collective-permute-done.25
  65.7 0.0 collective-permute-done.26
  65.7 0.0 collective-permute-done.27
  65.8 0.0 copy-done
  65.8 1.3 %conditional.1 = (bf16[4,256,2,256]{3,2,1,0:T(2,128)(2,1)S(1)}) conditional(s32[]{:T(128)} %bitcast.29, (bf16[4,64,512]{2,1,0:T(8,128)(2,1)S(1)}, s32[1,512]{1,0:T(1,128)S(1)}, bf16[256,512]{1,0:T(8,128)(2,1)S(1)}, bf16[768,512]{1,0:T(8,128)(2,1)S(1)}, bf16[256,512]{1,0:T(8,128)(2,1)S(1)}, /*index=5*/bf16[64,512]{1,0:T(8,128)(2,1)S(1)}, ...), branch_computations={%region_0.1_spmd, %region_1.32_spmd} | conditional | flops 1896568576 | bytes 99436336 | solution.py:502
  66.0 0.8 %branch_0_fun.1 = bf16[1024,512]{1,0:T(8,128)(2,1)S(1)} custom-call(s32[1,512]{1,0:T(1,128)S(1)} %get-tuple-element.323.target_ref, bf16[256,512]{1,0:T(8,128)(2,1)S(1)} %get-tuple-element.324.head_ref, bf16[768,512]{1,0:T(8,128)(2,1)S(1)} %get-tuple-element.325.res_ref, bf16[256,512]{1,0:T(8,128)(2,1)S(1)} %get-tuple-element.326.top_ref, ...), custom_call_target="tpu_custom_call" | custom-call | tf_op jit(solution)/shard_map/cond/branch_0_fun/pallas_call | solution.py:381
  66.7 0.3 reshape.1231
  67.0 0.0 copy-start.4
  67.1 1.0 %copy-done.4 = bf16[4,256,2,256]{3,2,1,0:T(2,128)(2,1)} copy-done((bf16[4,256,2,256]{3,2,1,0:T(2,128)(2,1)}, bf16[4,256,2,256]{3,2,1,0:T(2,128)(2,1)S(1)}, u32[]{:S(2)}) %copy-start.4) | copy-done | bytes 1048600
  (4 shorter events, 0.1 us)
Async XLA Ops:
  0.0 6.3 %copy-start.5 = (s32[4,256]{1,0:T(4,128)S(1)}, s32[4,256]{1,0:T(4,128)}, u32[]{:S(2)}) copy-start(s32[4,256]{1,0:T(4,128)} %piv_ref.5) | copy-start | bytes 12292
  1.4 16.8 %collective-permute-start.15 = (bf16[1024,256]{1,0:T(8,128)(2,1)S(1)}, bf16[1024,256]{1,0:T(8,128)(2,1)S(1)}, u32[]{:S(2)}, u32[]{:S(2)}) collective-permute-start(bf16[1024,256]{1,0:T(8,128)(2,1)S(1)} %bitcast.143), channel_id=1, source_target_pairs={{0,2},{1,3},{2,0},{3,1},{8,10},{9,11},{10,8},{11,9},{16,18},{17,19... | collective-permute-start | bytes 1572872 | tf_op jit(solution)/shard_map/ppermute | solution.py:412
  7.5 22.1 %collective-permute-start.12 = (bf16[1024,256]{1,0:T(8,128)(2,1)S(1)}, bf16[1024,256]{1,0:T(8,128)(2,1)S(1)}, u32[]{:S(2)}, u32[]{:S(2)}) collective-permute-start(bf16[1024,256]{1,0:T(8,128)(2,1)S(1)} %bitcast.144), channel_id=1, source_target_pairs={{0,4},{1,5},{2,6},{3,7},{8,12},{9,13},{10,14},{11,15},{16,20},{17,... | collective-permute-start | bytes 1572872 | tf_op jit(solution)/shard_map/ppermute | solution.py:412
  8.9 8.9 %collective-permute-start.14 = (bf16[304,256]{1,0:T(8,128)(2,1)S(1)}, bf16[304,256]{1,0:T(8,128)(2,1)S(1)}, u32[]{:S(2)}, u32[]{:S(2)}) collective-permute-start(bf16[304,256]{1,0:T(8,128)(2,1)S(1)} %get-tuple-element.420.parts_0_), channel_id=1, source_target_pairs={{0,8},{8,16},{16,24},{24,0},{1,9},{9,17},{17,25},{25,1},{2,10},{10... | collective-permute-start | bytes 466952 | tf_op jit(solution)/shard_map/ppermute | solution.py:431
  10.5 12.5 %collective-permute-start.18 = (bf16[304,256]{1,0:T(8,128)(2,1)S(1)}, bf16[304,256]{1,0:T(8,128)(2,1)S(1)}, u32[]{:S(2)}, u32[]{:S(2)}) collective-permute-start(bf16[304,256]{1,0:T(8,128)(2,1)S(1)} %get-tuple-element.420.parts_0_), channel_id=1, source_target_pairs={{0,16},{8,24},{16,0},{24,8},{1,17},{9,25},{17,1},{25,9},{2,18},{10... | collective-permute-start | bytes 466952 | tf_op jit(solution)/shard_map/ppermute | solution.py:431
  13.1 9.9 %collective-permute-start.19 = (bf16[304,256]{1,0:T(8,128)(2,1)S(1)}, bf16[304,256]{1,0:T(8,128)(2,1)S(1)}, u32[]{:S(2)}, u32[]{:S(2)}) collective-permute-start(bf16[304,256]{1,0:T(8,128)(2,1)S(1)} %get-tuple-element.420.parts_0_), channel_id=1, source_target_pairs={{0,24},{8,0},{16,8},{24,16},{1,25},{9,1},{17,9},{25,17},{2,26},{10... | collective-permute-start | bytes 466952 | tf_op jit(solution)/shard_map/ppermute | solution.py:431
  24.1 25.6 %collective-permute-start.20 = (bf16[768,256]{1,0:T(8,128)(2,1)S(1)}, bf16[768,256]{1,0:T(8,128)(2,1)S(1)}, u32[]{:S(2)}, u32[]{:S(2)}) collective-permute-start(bf16[768,256]{1,0:T(8,128)(2,1)S(1)} %get-tuple-element.427), channel_id=1, source_target_pairs={{0,2},{1,3},{2,0},{3,1},{8,10},{9,11},{10,8},{11,9},{16,18},{17,19... | collective-permute-start | bytes 1179656 | tf_op jit(solution)/shard_map/ppermute | solution.py:412
  27.0 22.8 %collective-permute-start.21 = (bf16[768,256]{1,0:T(8,128)(2,1)S(1)}, bf16[768,256]{1,0:T(8,128)(2,1)S(1)}, u32[]{:S(2)}, u32[]{:S(2)}) collective-permute-start(bf16[768,256]{1,0:T(8,128)(2,1)S(1)} %get-tuple-element.427), channel_id=1, source_target_pairs={{0,6},{1,7},{2,4},{3,5},{8,14},{9,15},{10,12},{11,13},{16,22},{17,... | collective-permute-start | bytes 1179656 | tf_op jit(solution)/shard_map/ppermute | solution.py:412
  28.3 21.5 %collective-permute-start.22 = (bf16[768,256]{1,0:T(8,128)(2,1)S(1)}, bf16[768,256]{1,0:T(8,128)(2,1)S(1)}, u32[]{:S(2)}, u32[]{:S(2)}) collective-permute-start(bf16[768,256]{1,0:T(8,128)(2,1)S(1)} %get-tuple-element.427), channel_id=1, source_target_pairs={{0,4},{1,5},{2,6},{3,7},{8,12},{9,13},{10,14},{11,15},{16,20},{17,... | collective-permute-start | bytes 1179656 | tf_op jit(solution)/shard_map/ppermute | solution.py:412
  29.6 20.3 %collective-permute-start.16 = (bf16[1024,256]{1,0:T(8,128)(2,1)S(1)}, bf16[1024,256]{1,0:T(8,128)(2,1)S(1)}, u32[]{:S(2)}, u32[]{:S(2)}) collective-permute-start(bf16[1024,256]{1,0:T(8,128)(2,1)S(1)} %collective-permute-done.12), channel_id=1, source_target_pairs={{4,6},{5,7},{6,4},{7,5},{12,14},{13,15},{14,12},{15,13},{20,22},{2... | collective-permute-start | bytes 1572872 | tf_op jit(solution)/shard_map/ppermute | solution.py:435
  30.4 21.2 %collective-permute-start.13 = (bf16[1024,256]{1,0:T(8,128)(2,1)S(1)}, bf16[1024,256]{1,0:T(8,128)(2,1)S(1)}, u32[]{:S(2)}, u32[]{:S(2)}) collective-permute-start(bf16[1024,256]{1,0:T(8,128)(2,1)S(1)} %broadcast_select_fusion.5.raws_0_), channel_id=1, source_target_pairs={{0,1},{1,0},{2,3},{3,2},{4,5},{5,4},{6,7},{7,6},{8,9},{9,8},{10,11... | collective-permute-start | bytes 1572872 | tf_op jit(solution)/shard_map/ppermute | solution.py:415
  49.8 3.1 %copy-start.1 = (bf16[4,256,256]{2,1,0:T(8,128)(2,1)S(1)}, bf16[4,256,256]{2,1,0:T(8,128)(2,1)}, u32[]{:S(2)}) copy-start(bf16[4,256,256]{2,1,0:T(8,128)(2,1)} %uinv_ref.3) | copy-start | bytes 1572868
  49.8 1.8 %collective-permute-start.24 = (bf16[768,256]{1,0:T(8,128)(2,1)S(1)}, bf16[768,256]{1,0:T(8,128)(2,1)S(1)}, u32[]{:S(2)}, u32[]{:S(2)}) collective-permute-start(bf16[768,256]{1,0:T(8,128)(2,1)S(1)} %broadcast_select_fusion.6.offs_2_), channel_id=1, source_target_pairs={{0,1},{1,0},{2,3},{3,2},{4,5},{5,4},{6,7},{7,6},{8,9},{9,8},{10,11... | collective-permute-start | bytes 1179656 | tf_op jit(solution)/shard_map/ppermute | solution.py:415
  50.0 2.9 %collective-permute-start.17 = (bf16[1024,256]{1,0:T(8,128)(2,1)S(1)}, bf16[1024,256]{1,0:T(8,128)(2,1)S(1)}, u32[]{:S(2)}, u32[]{:S(2)}) collective-permute-start(bf16[1024,256]{1,0:T(8,128)(2,1)S(1)} %broadcast_select_fusion.4.raws_2_), channel_id=1, source_target_pairs={{0,1},{1,0},{2,3},{3,2},{4,5},{5,4},{6,7},{7,6},{8,9},{9,8},{10,11... | collective-permute-start | bytes 1572872 | tf_op jit(solution)/shard_map/ppermute | solution.py:415
  50.6 2.3 %collective-permute-start.23 = (bf16[768,256]{1,0:T(8,128)(2,1)S(1)}, bf16[768,256]{1,0:T(8,128)(2,1)S(1)}, u32[]{:S(2)}, u32[]{:S(2)}) collective-permute-start(bf16[768,256]{1,0:T(8,128)(2,1)S(1)} %broadcast_select_fusion.7.offs_0_), channel_id=1, source_target_pairs={{0,1},{1,0},{2,3},{3,2},{4,5},{5,4},{6,7},{7,6},{8,9},{9,8},{10,11... | collective-permute-start | bytes 1179656 | tf_op jit(solution)/shard_map/ppermute | solution.py:415
  56.7 9.0 %collective-permute-start.25 = (bf16[64,512]{1,0:T(8,128)(2,1)S(1)}, bf16[64,512]{1,0:T(8,128)(2,1)S(1)}, u32[]{:S(2)}, u32[]{:S(2)}) collective-permute-start(bf16[64,512]{1,0:T(8,128)(2,1)S(1)} %get-tuple-element.564), channel_id=1, source_target_pairs={{0,8},{8,16},{16,24},{24,0},{1,9},{9,17},{17,25},{25,1},{2,10},{10... | collective-permute-start | bytes 196616 | tf_op jit(solution)/shard_map/ppermute | solution.py:474
  57.3 8.4 %collective-permute-start.26 = (bf16[64,512]{1,0:T(8,128)(2,1)S(1)}, bf16[64,512]{1,0:T(8,128)(2,1)S(1)}, u32[]{:S(2)}, u32[]{:S(2)}) collective-permute-start(bf16[64,512]{1,0:T(8,128)(2,1)S(1)} %get-tuple-element.563), channel_id=1, source_target_pairs={{0,16},{8,24},{16,0},{24,8},{1,17},{9,25},{17,1},{25,9},{2,18},{10... | collective-permute-start | bytes 196616 | tf_op jit(solution)/shard_map/ppermute | solution.py:474
  59.8 6.0 %collective-permute-start.27 = (bf16[64,512]{1,0:T(8,128)(2,1)S(1)}, bf16[64,512]{1,0:T(8,128)(2,1)S(1)}, u32[]{:S(2)}, u32[]{:S(2)}) collective-permute-start(bf16[64,512]{1,0:T(8,128)(2,1)S(1)} %get-tuple-element.562), channel_id=1, source_target_pairs={{0,24},{8,0},{16,8},{24,16},{1,25},{9,1},{17,9},{25,17},{2,26},{10... | collective-permute-start | bytes 196616 | tf_op jit(solution)/shard_map/ppermute | solution.py:474
  60.6 5.2 %copy-start = (bf16[4,256,2,256]{3,2,1,0:T(2,128)(2,1)S(1)}, bf16[4,256,2,256]{3,2,1,0:T(2,128)(2,1)}, u32[]{:S(2)}) copy-start(bf16[4,256,2,256]{3,2,1,0:T(2,128)(2,1)} %param.56) | copy-start | bytes 3145732
  67.0 1.0 %copy-start.4 = (bf16[4,256,2,256]{3,2,1,0:T(2,128)(2,1)}, bf16[4,256,2,256]{3,2,1,0:T(2,128)(2,1)S(1)}, u32[]{:S(2)}) copy-start(bf16[4,256,2,256]{3,2,1,0:T(2,128)(2,1)S(1)} %get-tuple-element.970) | copy-start | bytes 3145732

commit v7 on v6

--- a/solution.py
+++ b/solution.py
@@ -172,8 +172,8 @@
     pack1_ref[...] = dot(chosen, mat_ref[1]).astype(BF16)
 
 
-def final_places(x, piv_ref, cols, steps, size):
-    for s in range(steps):
+def final_places(x, cols, steps, size):
+    for s in steps:
         base = s * size
         inside = (x >= base) & (x < base + size)
         x = jnp.where(inside, look(cols[s], base, x, size), find(cols[s], base, x, size))
@@ -186,7 +186,12 @@
     lanes = -(-n_row // 8) * 8
     member = []
     for t in range(steps):
-        x = final_places(iota((1, nb), 1) + t * nb, piv_ref, cols, steps, nb)
+        at = iota((1, nb), 1) + t * nb
+        x = at
+        for s in range(t):
+            x = find(cols[s], s * nb, x, nb)
+        x = jnp.where(x == at, piv_ref[t : t + 1, :], x)
+        x = final_places(x, cols, range(t + 1, steps), nb)
         block = x // nb
         dest = jnp.where(x >= steps * nb, block % n_row, -1)
         move_ref[t : t + 1, :] = dest
@@ -305,7 +310,7 @@
     res_ref[:, :nb] = jnp.where(in_panel, left[wide:, panel], value)
     res_ref[:, nb:] = (mat_ref[1, :nb, :].astype(F32) - prod[:, nb:]).astype(BF16)
     cols = [to_col(piv_ref[t : t + 1, :], nb) for t in range(steps)]
-    x = final_places(iota((1, nb), 1) + my_row * nb, piv_ref, cols, steps, nb)
+    x = final_places(iota((1, nb), 1) + my_row * nb, cols, range(steps), nb)
     dest = jnp.where((x >= wide) & (my_row < steps), x // nb % n_row, -1)
     member = iota((-(-n_row // 8) * 8, nb), 0) == dest
     rank = jnp.sum(jnp.where(member, before([member], nb)[0], 0.0), axis=0, keepdims=True)
@@ -334,7 +339,7 @@
     bad = find_moves((nb, steps, n_row, cap), piv_ref, meta_ref, move_ref)
     target_ref[...] = find_targets((nb, steps, n_row), move_ref, lax.axis_index("prow"))
     flag_ref[0] = jnp.max(bad)
-    tiles = [slice(k * nb, (k + 1) * nb) for k in range(local_rows // nb - 1)]
+    tiles = [slice(0, local_rows - nb)]
     for t in range(steps):
         here = slice(t * nb, (t + 1) * nb)
         done = slice(0, t * nb)

time: 68.3 us -> 68.1 us (level)
  transfers between devices with their start and end apart: 16 -> 16, of which waited for: 4 -> 5; matrix products, arithmetic and copies ran while one was open for 0% -> 0% of each run, Pallas kernels for 11% -> 11%
where the time goes in v7:
time: 68.1 us; the launch traced here: 67.8 us
  starting transfers between devices  22.5 us (33%)
  blocking collectives  19.3 us (28%)
  Pallas kernels  12 us (18%)
  waiting for transfers between devices  9.97 us (15%)
  local copies, waits for them, and re-layouts  2.7 us (4%)
  between operations  0.86 us (1%)
    all_gather x1, blocking collectives, local(): buf1 = lax.all_gather(pack1, 'prow', tiled=True)  19.3 us
    pallas_call x6, Pallas kernels, call(): pl.pallas_call(kernel, out_shape=outs, in_specs=[jax.tree.map(lambda _: a...  12 us
    ppermute x5, starting transfers between devices, from_panels(): return lax.ppermute(value, 'pcol', [(i, i ^ mask) for i in range(steps)])  11.6 us
    ppermute x3, waiting for transfers between devices, local(): lax.ppermute(pack0, 'prow', [(i, (i + k) % n_row) for i in range(n_row)])  8.17 us
    ppermute x3, starting transfers between devices, local(): lax.ppermute(pack0, 'prow', [(i, (i + k) % n_row) for i in range(n_row)])  5.57 us
    ppermute x3, starting transfers between devices, local(): lax.ppermute(send[k], 'prow', [(i, (i + k) % n_row) for i in range(n_row)])  3.88 us
    unnamed x9, local copies, waits for them, and re-layouts  2.35 us
  transfers between devices with their start and end apart: 16, of which 5 were waited for; matrix products, arithmetic and copies ran while one was open for 0% of the time, Pallas kernels for 11%

profile of v7, /device:TPU:0, one launch (start us, length us, event | category | flops | bytes accessed | tf_op | source)
XLA Modules:
  0.0 67.8 jit_solution(16354518378080617086)
XLA Ops:
  0.0 0.0 copy-start.5
  0.0 1.4 %copy.25 = bf16[4,256,2,256]{3,1,0,2:T(8,128)(2,1)S(1)} copy(bf16[4,256,2,256]{3,2,1,0:T(2,128)(2,1)} %param.56) | data formatting | bytes 2097152 | tf_op args[0]
  1.4 4.8 %collective-permute-start.15 = (bf16[1024,256]{1,0:T(8,128)(2,1)S(1)}, bf16[1024,256]{1,0:T(8,128)(2,1)S(1)}, u32[]{:S(2)}, u32[]{:S(2)}) collective-permute-start(bf16[1024,256]{1,0:T(8,128)(2,1)S(1)} %bitcast.143), channel_id=1, source_target_pairs={{0,2},{1,3},{2,0},{3,1},{8,10},{9,11},{10,8},{11,9},{16,18},{17,19... | collective-permute-start | bytes 1572872 | tf_op jit(solution)/shard_map/ppermute | solution.py:417
  6.3 0.0 copy-done.5
  6.3 1.2 %shard_map.48 = (s32[16,256]{1,0:T(8,128)S(1)}, bf16[304,256]{1,0:T(8,128)(2,1)S(1)}, bf16[304,256]{1,0:T(8,128)(2,1)S(1)}) custom-call(s32[4,256]{1,0:T(4,128)S(1)} %copy-done.5, bf16[2,1024,256]{2,1,0:T(8,128)(2,1)S(1)} %bitcast.135), custom_call_target="tpu_custom_call" | custom-call | tf_op jit(solution)/shard_map/pallas_call | solution.py:386
  7.5 1.3 %collective-permute-start.12 = (bf16[1024,256]{1,0:T(8,128)(2,1)S(1)}, bf16[1024,256]{1,0:T(8,128)(2,1)S(1)}, u32[]{:S(2)}, u32[]{:S(2)}) collective-permute-start(bf16[1024,256]{1,0:T(8,128)(2,1)S(1)} %bitcast.144), channel_id=1, source_target_pairs={{0,4},{1,5},{2,6},{3,7},{8,12},{9,13},{10,14},{11,15},{16,20},{17,... | collective-permute-start | bytes 1572872 | tf_op jit(solution)/shard_map/ppermute | solution.py:417
  8.9 1.6 %collective-permute-start.14 = (bf16[304,256]{1,0:T(8,128)(2,1)S(1)}, bf16[304,256]{1,0:T(8,128)(2,1)S(1)}, u32[]{:S(2)}, u32[]{:S(2)}) collective-permute-start(bf16[304,256]{1,0:T(8,128)(2,1)S(1)} %get-tuple-element.420.parts_0_), channel_id=1, source_target_pairs={{0,8},{8,16},{16,24},{24,0},{1,9},{9,17},{17,25},{25,1},{2,10},{10... | collective-permute-start | bytes 466952 | tf_op jit(solution)/shard_map/ppermute | solution.py:436
  10.5 2.6 %collective-permute-start.18 = (bf16[304,256]{1,0:T(8,128)(2,1)S(1)}, bf16[304,256]{1,0:T(8,128)(2,1)S(1)}, u32[]{:S(2)}, u32[]{:S(2)}) collective-permute-start(bf16[304,256]{1,0:T(8,128)(2,1)S(1)} %get-tuple-element.420.parts_0_), channel_id=1, source_target_pairs={{0,16},{8,24},{16,0},{24,8},{1,17},{9,25},{17,1},{25,9},{2,18},{10... | collective-permute-start | bytes 466952 | tf_op jit(solution)/shard_map/ppermute | solution.py:436
  13.1 1.3 %collective-permute-start.19 = (bf16[304,256]{1,0:T(8,128)(2,1)S(1)}, bf16[304,256]{1,0:T(8,128)(2,1)S(1)}, u32[]{:S(2)}, u32[]{:S(2)}) collective-permute-start(bf16[304,256]{1,0:T(8,128)(2,1)S(1)} %get-tuple-element.420.parts_0_), channel_id=1, source_target_pairs={{0,24},{8,0},{16,8},{24,16},{1,25},{9,1},{17,9},{25,17},{2,26},{10... | collective-permute-start | bytes 466952 | tf_op jit(solution)/shard_map/ppermute | solution.py:436
  14.4 3.3 %collective-permute-done.14.parts_1_ = bf16[304,256]{1,0:T(8,128)(2,1)S(1)} collective-permute-done((bf16[304,256]{1,0:T(8,128)(2,1)S(1)}, bf16[304,256]{1,0:T(8,128)(2,1)S(1)}, u32[]{:S(2)}, u32[]{:S(2)}) %collective-permute-start.14) | collective-permute-done | bytes 155680 | tf_op jit(solution)/shard_map/ppermute | solution.py:436
  17.8 0.4 collective-permute-done.15
  18.2 4.8 %collective-permute-done.18.parts_2_ = bf16[304,256]{1,0:T(8,128)(2,1)S(1)} collective-permute-done((bf16[304,256]{1,0:T(8,128)(2,1)S(1)}, bf16[304,256]{1,0:T(8,128)(2,1)S(1)}, u32[]{:S(2)}, u32[]{:S(2)}) %collective-permute-start.18) | collective-permute-done | bytes 155680 | tf_op jit(solution)/shard_map/ppermute | solution.py:436
  23.0 0.0 collective-permute-done.19.parts_3_
  23.0 1.1 %shard_map.49 = (bf16[1024,256]{1,0:T(8,128)(2,1)S(1)}, bf16[768,256]{1,0:T(8,128)(2,1)S(1)}) custom-call(s32[16,256]{1,0:T(8,128)S(1)} %get-tuple-element.417.meta_ref, bf16[304,256]{1,0:T(8,128)(2,1)S(1)} %get-tuple-element.420.parts_0_, bf16[304,256]{1,0:T(8,128)(2,1)S(1)} %collective-permute-done.14.parts_1_, ...), custom_call_target="tpu_custom_call" | custom-call | tf_op jit(solution)/shard_map/pallas_call | solution.py:386
  24.1 2.8 %collective-permute-start.20 = (bf16[768,256]{1,0:T(8,128)(2,1)S(1)}, bf16[768,256]{1,0:T(8,128)(2,1)S(1)}, u32[]{:S(2)}, u32[]{:S(2)}) collective-permute-start(bf16[768,256]{1,0:T(8,128)(2,1)S(1)} %get-tuple-element.427), channel_id=1, source_target_pairs={{0,2},{1,3},{2,0},{3,1},{8,10},{9,11},{10,8},{11,9},{16,18},{17,19... | collective-permute-start | bytes 1179656 | tf_op jit(solution)/shard_map/ppermute | solution.py:417
  27.0 1.3 %collective-permute-start.21 = (bf16[768,256]{1,0:T(8,128)(2,1)S(1)}, bf16[768,256]{1,0:T(8,128)(2,1)S(1)}, u32[]{:S(2)}, u32[]{:S(2)}) collective-permute-start(bf16[768,256]{1,0:T(8,128)(2,1)S(1)} %get-tuple-element.427), channel_id=1, source_target_pairs={{0,6},{1,7},{2,4},{3,5},{8,14},{9,15},{10,12},{11,13},{16,22},{17,... | collective-permute-start | bytes 1179656 | tf_op jit(solution)/shard_map/ppermute | solution.py:417
  28.3 1.3 %collective-permute-start.22 = (bf16[768,256]{1,0:T(8,128)(2,1)S(1)}, bf16[768,256]{1,0:T(8,128)(2,1)S(1)}, u32[]{:S(2)}, u32[]{:S(2)}) collective-permute-start(bf16[768,256]{1,0:T(8,128)(2,1)S(1)} %get-tuple-element.427), channel_id=1, source_target_pairs={{0,4},{1,5},{2,6},{3,7},{8,12},{9,13},{10,14},{11,15},{16,20},{17,... | collective-permute-start | bytes 1179656 | tf_op jit(solution)/shard_map/ppermute | solution.py:417
  29.6 0.0 collective-permute-done.12
  29.6 0.7 %collective-permute-start.16 = (bf16[1024,256]{1,0:T(8,128)(2,1)S(1)}, bf16[1024,256]{1,0:T(8,128)(2,1)S(1)}, u32[]{:S(2)}, u32[]{:S(2)}) collective-permute-start(bf16[1024,256]{1,0:T(8,128)(2,1)S(1)} %collective-permute-done.12), channel_id=1, source_target_pairs={{4,6},{5,7},{6,4},{7,5},{12,14},{13,15},{14,12},{15,13},{20,22},{2... | collective-permute-start | bytes 1572872 | tf_op jit(solution)/shard_map/ppermute | solution.py:440
  30.3 0.1 broadcast_select_fusion.5.raws_0_
  30.4 0.1 collective-permute-start.13
  30.5 19.3 %all_gather.3.buf_ref = bf16[1216,256]{1,0:T(8,128)(2,1)S(1)} all-gather(bf16[304,256]{1,0:T(8,128)(2,1)S(1)} %get-tuple-element.426), channel_id=1, replica_groups=mesh['prow'=4,'pcol'=8] {'prow'}, dimensions={0}, use_global_device_ids=true | all-gather | bytes 778240 | tf_op jit(solution)/shard_map/all_gather | solution.py:451
  49.8 0.0 collective-permute-done.20
  49.8 0.0 collective-permute-done.21
  49.8 0.0 collective-permute-done.22
  49.8 0.0 copy-start.1
  49.8 0.1 collective-permute-start.24
  49.9 0.0 collective-permute-done.16
  49.9 0.1 broadcast_select_fusion.4.raws_2_
  50.0 0.6 collective-permute-start.17
  50.6 0.1 broadcast_select_fusion.7.offs_0_
  50.6 0.1 collective-permute-start.23
  50.7 1.0 %shard_map.50.top1_ref = bf16[1024,256]{1,0:T(8,128)(2,1)S(1)} custom-call(s32[16,256]{1,0:T(8,128)S(1)} %get-tuple-element.417.meta_ref, bf16[1216,256]{1,0:T(8,128)(2,1)S(1)} %all_gather.3.buf_ref), custom_call_target="tpu_custom_call" | custom-call | tf_op jit(solution)/shard_map/pallas_call | solution.py:386
  51.7 0.0 collective-permute-done.13.raws_1_
  51.7 0.0 collective-permute-done.24.offs_3_
  51.7 1.3 %collective-permute-done.23.offs_1_ = bf16[768,256]{1,0:T(8,128)(2,1)S(1)} collective-permute-done((bf16[768,256]{1,0:T(8,128)(2,1)S(1)}, bf16[768,256]{1,0:T(8,128)(2,1)S(1)}, u32[]{:S(2)}, u32[]{:S(2)}) %collective-permute-start.23) | collective-permute-done | bytes 393248 | tf_op jit(solution)/shard_map/ppermute | solution.py:420
  52.9 0.0 collective-permute-done.17.raws_3_
  52.9 0.0 copy-done.1
  52.9 3.7 %shard_map.51 = (bf16[1024,1536]{1,0:T(8,128)(2,1)S(1)}, bf16[256,512]{1,0:T(8,128)(2,1)S(1)}, bf16[256,512]{1,0:T(8,128)(2,1)S(1)}, bf16[4,64,512]{2,1,0:T(8,128)(2,1)S(1)}) custom-call(s32[4,256]{1,0:T(4,128)S(1)} %copy-done.5, bf16[1024,256]{1,0:T(8,128)(2,1)S(1)} %get-tuple-element.423.top0_ref, bf16[1024,256]{1,0:T(8,128)(2,1)S(1)} %shard_map.50.top1_ref, ...), custom_call_target="tpu_custom_call" | custom-call | tf_op jit(solution)/shard_map/pallas_call | solution.py:386
  56.7 0.6 collective-permute-start.25
  57.3 2.5 %collective-permute-start.26 = (bf16[64,512]{1,0:T(8,128)(2,1)S(1)}, bf16[64,512]{1,0:T(8,128)(2,1)S(1)}, u32[]{:S(2)}, u32[]{:S(2)}) collective-permute-start(bf16[64,512]{1,0:T(8,128)(2,1)S(1)} %get-tuple-element.563), channel_id=1, source_target_pairs={{0,16},{8,24},{16,0},{24,8},{1,17},{9,25},{17,1},{25,9},{2,18},{10... | collective-permute-start | bytes 196616 | tf_op jit(solution)/shard_map/ppermute | solution.py:479
  59.8 0.8 %collective-permute-start.27 = (bf16[64,512]{1,0:T(8,128)(2,1)S(1)}, bf16[64,512]{1,0:T(8,128)(2,1)S(1)}, u32[]{:S(2)}, u32[]{:S(2)}) collective-permute-start(bf16[64,512]{1,0:T(8,128)(2,1)S(1)} %get-tuple-element.562), channel_id=1, source_target_pairs={{0,24},{8,0},{16,8},{24,16},{1,25},{9,1},{17,9},{25,17},{2,26},{10... | collective-permute-start | bytes 196616 | tf_op jit(solution)/shard_map/ppermute | solution.py:479
  60.6 0.0 copy-start
  60.6 4.2 %shard_map.52 = (bf16[768,512]{1,0:T(8,128)(2,1)S(1)}, s32[1,512]{1,0:T(1,128)S(1)}, s32[1]{0:T(128)}) custom-call(s32[4,256]{1,0:T(4,128)S(1)} %copy-done.5, s32[16,256]{1,0:T(8,128)S(1)} %get-tuple-element.417.meta_ref, bf16[2,1024,256]{2,1,0:T(8,128)(2,1)S(1)} %bitcast.137, bf16[1024,256]{1,0:T(8,128)(2,1)S(1)} %broadcast_select_fusion.5.raws_0_, ...), custom_call_target="tpu_custom_call" | custom-call | flops 2415919104 | bytes 4194304 | tf_op jit(solution)/shard_map/pallas_call | solution.py:386
  65.5 0.0 collective-permute-done.25
  65.5 0.1 collective-permute-done.26
  65.6 0.0 collective-permute-done.27
  65.6 0.0 copy-done
  65.6 1.2 %conditional.1 = (bf16[4,256,2,256]{3,2,1,0:T(2,128)(2,1)S(1)}) conditional(s32[]{:T(128)} %bitcast.29, (bf16[4,64,512]{2,1,0:T(8,128)(2,1)S(1)}, s32[1,512]{1,0:T(1,128)S(1)}, bf16[256,512]{1,0:T(8,128)(2,1)S(1)}, bf16[768,512]{1,0:T(8,128)(2,1)S(1)}, bf16[256,512]{1,0:T(8,128)(2,1)S(1)}, /*index=5*/bf16[64,512]{1,0:T(8,128)(2,1)S(1)}, ...), branch_computations={%region_0.1_spmd, %region_1.32_spmd} | conditional | flops 1896568576 | bytes 99436336 | solution.py:507
  65.7 0.8 %branch_0_fun.1 = bf16[1024,512]{1,0:T(8,128)(2,1)S(1)} custom-call(s32[1,512]{1,0:T(1,128)S(1)} %get-tuple-element.323.target_ref, bf16[256,512]{1,0:T(8,128)(2,1)S(1)} %get-tuple-element.324.head_ref, bf16[768,512]{1,0:T(8,128)(2,1)S(1)} %get-tuple-element.325.res_ref, bf16[256,512]{1,0:T(8,128)(2,1)S(1)} %get-tuple-element.326.top_ref, ...), custom_call_target="tpu_custom_call" | custom-call | tf_op jit(solution)/shard_map/cond/branch_0_fun/pallas_call | solution.py:386
  66.5 0.3 reshape.1231
  66.8 0.0 copy-start.4
  66.8 1.0 %copy-done.4 = bf16[4,256,2,256]{3,2,1,0:T(2,128)(2,1)} copy-done((bf16[4,256,2,256]{3,2,1,0:T(2,128)(2,1)}, bf16[4,256,2,256]{3,2,1,0:T(2,128)(2,1)S(1)}, u32[]{:S(2)}) %copy-start.4) | copy-done | bytes 1048600
  (4 shorter events, 0.1 us)
Async XLA Ops:
  0.0 6.3 %copy-start.5 = (s32[4,256]{1,0:T(4,128)S(1)}, s32[4,256]{1,0:T(4,128)}, u32[]{:S(2)}) copy-start(s32[4,256]{1,0:T(4,128)} %piv_ref.5) | copy-start | bytes 12292
  1.4 16.8 %collective-permute-start.15 = (bf16[1024,256]{1,0:T(8,128)(2,1)S(1)}, bf16[1024,256]{1,0:T(8,128)(2,1)S(1)}, u32[]{:S(2)}, u32[]{:S(2)}) collective-permute-start(bf16[1024,256]{1,0:T(8,128)(2,1)S(1)} %bitcast.143), channel_id=1, source_target_pairs={{0,2},{1,3},{2,0},{3,1},{8,10},{9,11},{10,8},{11,9},{16,18},{17,19... | collective-permute-start | bytes 1572872 | tf_op jit(solution)/shard_map/ppermute | solution.py:417
  7.5 22.1 %collective-permute-start.12 = (bf16[1024,256]{1,0:T(8,128)(2,1)S(1)}, bf16[1024,256]{1,0:T(8,128)(2,1)S(1)}, u32[]{:S(2)}, u32[]{:S(2)}) collective-permute-start(bf16[1024,256]{1,0:T(8,128)(2,1)S(1)} %bitcast.144), channel_id=1, source_target_pairs={{0,4},{1,5},{2,6},{3,7},{8,12},{9,13},{10,14},{11,15},{16,20},{17,... | collective-permute-start | bytes 1572872 | tf_op jit(solution)/shard_map/ppermute | solution.py:417
  8.9 8.9 %collective-permute-start.14 = (bf16[304,256]{1,0:T(8,128)(2,1)S(1)}, bf16[304,256]{1,0:T(8,128)(2,1)S(1)}, u32[]{:S(2)}, u32[]{:S(2)}) collective-permute-start(bf16[304,256]{1,0:T(8,128)(2,1)S(1)} %get-tuple-element.420.parts_0_), channel_id=1, source_target_pairs={{0,8},{8,16},{16,24},{24,0},{1,9},{9,17},{17,25},{25,1},{2,10},{10... | collective-permute-start | bytes 466952 | tf_op jit(solution)/shard_map/ppermute | solution.py:436
  10.5 12.5 %collective-permute-start.18 = (bf16[304,256]{1,0:T(8,128)(2,1)S(1)}, bf16[304,256]{1,0:T(8,128)(2,1)S(1)}, u32[]{:S(2)}, u32[]{:S(2)}) collective-permute-start(bf16[304,256]{1,0:T(8,128)(2,1)S(1)} %get-tuple-element.420.parts_0_), channel_id=1, source_target_pairs={{0,16},{8,24},{16,0},{24,8},{1,17},{9,25},{17,1},{25,9},{2,18},{10... | collective-permute-start | bytes 466952 | tf_op jit(solution)/shard_map/ppermute | solution.py:436
  13.1 9.9 %collective-permute-start.19 = (bf16[304,256]{1,0:T(8,128)(2,1)S(1)}, bf16[304,256]{1,0:T(8,128)(2,1)S(1)}, u32[]{:S(2)}, u32[]{:S(2)}) collective-permute-start(bf16[304,256]{1,0:T(8,128)(2,1)S(1)} %get-tuple-element.420.parts_0_), channel_id=1, source_target_pairs={{0,24},{8,0},{16,8},{24,16},{1,25},{9,1},{17,9},{25,17},{2,26},{10... | collective-permute-start | bytes 466952 | tf_op jit(solution)/shard_map/ppermute | solution.py:436
  24.1 25.6 %collective-permute-start.20 = (bf16[768,256]{1,0:T(8,128)(2,1)S(1)}, bf16[768,256]{1,0:T(8,128)(2,1)S(1)}, u32[]{:S(2)}, u32[]{:S(2)}) collective-permute-start(bf16[768,256]{1,0:T(8,128)(2,1)S(1)} %get-tuple-element.427), channel_id=1, source_target_pairs={{0,2},{1,3},{2,0},{3,1},{8,10},{9,11},{10,8},{11,9},{16,18},{17,19... | collective-permute-start | bytes 1179656 | tf_op jit(solution)/shard_map/ppermute | solution.py:417
  27.0 22.8 %collective-permute-start.21 = (bf16[768,256]{1,0:T(8,128)(2,1)S(1)}, bf16[768,256]{1,0:T(8,128)(2,1)S(1)}, u32[]{:S(2)}, u32[]{:S(2)}) collective-permute-start(bf16[768,256]{1,0:T(8,128)(2,1)S(1)} %get-tuple-element.427), channel_id=1, source_target_pairs={{0,6},{1,7},{2,4},{3,5},{8,14},{9,15},{10,12},{11,13},{16,22},{17,... | collective-permute-start | bytes 1179656 | tf_op jit(solution)/shard_map/ppermute | solution.py:417
  28.3 21.5 %collective-permute-start.22 = (bf16[768,256]{1,0:T(8,128)(2,1)S(1)}, bf16[768,256]{1,0:T(8,128)(2,1)S(1)}, u32[]{:S(2)}, u32[]{:S(2)}) collective-permute-start(bf16[768,256]{1,0:T(8,128)(2,1)S(1)} %get-tuple-element.427), channel_id=1, source_target_pairs={{0,4},{1,5},{2,6},{3,7},{8,12},{9,13},{10,14},{11,15},{16,20},{17,... | collective-permute-start | bytes 1179656 | tf_op jit(solution)/shard_map/ppermute | solution.py:417
  29.6 20.3 %collective-permute-start.16 = (bf16[1024,256]{1,0:T(8,128)(2,1)S(1)}, bf16[1024,256]{1,0:T(8,128)(2,1)S(1)}, u32[]{:S(2)}, u32[]{:S(2)}) collective-permute-start(bf16[1024,256]{1,0:T(8,128)(2,1)S(1)} %collective-permute-done.12), channel_id=1, source_target_pairs={{4,6},{5,7},{6,4},{7,5},{12,14},{13,15},{14,12},{15,13},{20,22},{2... | collective-permute-start | bytes 1572872 | tf_op jit(solution)/shard_map/ppermute | solution.py:440
  30.4 21.2 %collective-permute-start.13 = (bf16[1024,256]{1,0:T(8,128)(2,1)S(1)}, bf16[1024,256]{1,0:T(8,128)(2,1)S(1)}, u32[]{:S(2)}, u32[]{:S(2)}) collective-permute-start(bf16[1024,256]{1,0:T(8,128)(2,1)S(1)} %broadcast_select_fusion.5.raws_0_), channel_id=1, source_target_pairs={{0,1},{1,0},{2,3},{3,2},{4,5},{5,4},{6,7},{7,6},{8,9},{9,8},{10,11... | collective-permute-start | bytes 1572872 | tf_op jit(solution)/shard_map/ppermute | solution.py:420
  49.8 3.1 %copy-start.1 = (bf16[4,256,256]{2,1,0:T(8,128)(2,1)S(1)}, bf16[4,256,256]{2,1,0:T(8,128)(2,1)}, u32[]{:S(2)}) copy-start(bf16[4,256,256]{2,1,0:T(8,128)(2,1)} %uinv_ref.3) | copy-start | bytes 1572868
  49.8 1.8 %collective-permute-start.24 = (bf16[768,256]{1,0:T(8,128)(2,1)S(1)}, bf16[768,256]{1,0:T(8,128)(2,1)S(1)}, u32[]{:S(2)}, u32[]{:S(2)}) collective-permute-start(bf16[768,256]{1,0:T(8,128)(2,1)S(1)} %broadcast_select_fusion.6.offs_2_), channel_id=1, source_target_pairs={{0,1},{1,0},{2,3},{3,2},{4,5},{5,4},{6,7},{7,6},{8,9},{9,8},{10,11... | collective-permute-start | bytes 1179656 | tf_op jit(solution)/shard_map/ppermute | solution.py:420
  50.0 2.9 %collective-permute-start.17 = (bf16[1024,256]{1,0:T(8,128)(2,1)S(1)}, bf16[1024,256]{1,0:T(8,128)(2,1)S(1)}, u32[]{:S(2)}, u32[]{:S(2)}) collective-permute-start(bf16[1024,256]{1,0:T(8,128)(2,1)S(1)} %broadcast_select_fusion.4.raws_2_), channel_id=1, source_target_pairs={{0,1},{1,0},{2,3},{3,2},{4,5},{5,4},{6,7},{7,6},{8,9},{9,8},{10,11... | collective-permute-start | bytes 1572872 | tf_op jit(solution)/shard_map/ppermute | solution.py:420
  50.6 2.3 %collective-permute-start.23 = (bf16[768,256]{1,0:T(8,128)(2,1)S(1)}, bf16[768,256]{1,0:T(8,128)(2,1)S(1)}, u32[]{:S(2)}, u32[]{:S(2)}) collective-permute-start(bf16[768,256]{1,0:T(8,128)(2,1)S(1)} %broadcast_select_fusion.7.offs_0_), channel_id=1, source_target_pairs={{0,1},{1,0},{2,3},{3,2},{4,5},{5,4},{6,7},{7,6},{8,9},{9,8},{10,11... | collective-permute-start | bytes 1179656 | tf_op jit(solution)/shard_map/ppermute | solution.py:420
  56.7 8.8 %collective-permute-start.25 = (bf16[64,512]{1,0:T(8,128)(2,1)S(1)}, bf16[64,512]{1,0:T(8,128)(2,1)S(1)}, u32[]{:S(2)}, u32[]{:S(2)}) collective-permute-start(bf16[64,512]{1,0:T(8,128)(2,1)S(1)} %get-tuple-element.564), channel_id=1, source_target_pairs={{0,8},{8,16},{16,24},{24,0},{1,9},{9,17},{17,25},{25,1},{2,10},{10... | collective-permute-start | bytes 196616 | tf_op jit(solution)/shard_map/ppermute | solution.py:479
  57.3 8.2 %collective-permute-start.26 = (bf16[64,512]{1,0:T(8,128)(2,1)S(1)}, bf16[64,512]{1,0:T(8,128)(2,1)S(1)}, u32[]{:S(2)}, u32[]{:S(2)}) collective-permute-start(bf16[64,512]{1,0:T(8,128)(2,1)S(1)} %get-tuple-element.563), channel_id=1, source_target_pairs={{0,16},{8,24},{16,0},{24,8},{1,17},{9,25},{17,1},{25,9},{2,18},{10... | collective-permute-start | bytes 196616 | tf_op jit(solution)/shard_map/ppermute | solution.py:479
  59.8 5.8 %collective-permute-start.27 = (bf16[64,512]{1,0:T(8,128)(2,1)S(1)}, bf16[64,512]{1,0:T(8,128)(2,1)S(1)}, u32[]{:S(2)}, u32[]{:S(2)}) collective-permute-start(bf16[64,512]{1,0:T(8,128)(2,1)S(1)} %get-tuple-element.562), channel_id=1, source_target_pairs={{0,24},{8,0},{16,8},{24,16},{1,25},{9,1},{17,9},{25,17},{2,26},{10... | collective-permute-start | bytes 196616 | tf_op jit(solution)/shard_map/ppermute | solution.py:479
  60.6 5.0 %copy-start = (bf16[4,256,2,256]{3,2,1,0:T(2,128)(2,1)S(1)}, bf16[4,256,2,256]{3,2,1,0:T(2,128)(2,1)}, u32[]{:S(2)}) copy-start(bf16[4,256,2,256]{3,2,1,0:T(2,128)(2,1)} %param.56) | copy-start | bytes 3145732
  66.8 1.0 %copy-start.4 = (bf16[4,256,2,256]{3,2,1,0:T(2,128)(2,1)}, bf16[4,256,2,256]{3,2,1,0:T(2,128)(2,1)S(1)}, u32[]{:S(2)}) copy-start(bf16[4,256,2,256]{3,2,1,0:T(2,128)(2,1)S(1)} %get-tuple-element.970) | copy-start | bytes 3145732

commit v8 on v7

--- a/solution.py
+++ b/solution.py
@@ -12,7 +12,7 @@
 I32 = jnp.int32
 VMEM_BYTES = 24 * 1024 * 1024
 MOVE_ROWS = 64
-MOVE_SLOTS = 128
+MOVE_SLOTS = MOVE_ROWS
 
 
 def ring_sum(value, axis):
@@ -362,7 +362,6 @@
     nb, steps, n_row, local_rows = cfg
     recv, out_ref, slots = refs[:n_row], refs[n_row], refs[n_row + 1]
     my_row = lax.axis_index("prow")
-    slots[...] = jnp.zeros_like(slots)
     for k in range(n_row):
         slots[k * MOVE_SLOTS : k * MOVE_SLOTS + MOVE_ROWS, :] = recv[k][...]
     target = target_ref[...]

time: 68.1 us -> 67.9 us (level)
  Pallas kernels: 12 us -> 11.3 us
    pallas_call x6, Pallas kernels: 12 us -> 11.3 us  [call(): pl.pallas_call(kernel, out_shape=outs, in_specs=[jax.tree.map(lambda _: a...]
  transfers between devices with their start and end apart: 16 -> 16, of which waited for: 5 -> 5; matrix products, arithmetic and copies ran while one was open for 0% -> 0% of each run, Pallas kernels for 11% -> 10%
where the time goes in v8:
time: 67.9 us; the launch traced here: 67.5 us
  starting transfers between devices  22.5 us (33%)
  blocking collectives  19.3 us (28%)
  Pallas kernels  11.3 us (17%)
  waiting for transfers between devices  10.4 us (15%)
  local copies, waits for them, and re-layouts  2.7 us (4%)
  between operations  0.86 us (1%)
    all_gather x1, blocking collectives, local(): buf1 = lax.all_gather(pack1, 'prow', tiled=True)  19.3 us
    ppermute x5, starting transfers between devices, from_panels(): return lax.ppermute(value, 'pcol', [(i, i ^ mask) for i in range(steps)])  11.6 us
    pallas_call x6, Pallas kernels, call(): pl.pallas_call(kernel, out_shape=outs, in_specs=[jax.tree.map(lambda _: a...  11.3 us
    ppermute x3, waiting for transfers between devices, local(): lax.ppermute(pack0, 'prow', [(i, (i + k) % n_row) for i in range(n_row)])  8.17 us
    ppermute x3, starting transfers between devices, local(): lax.ppermute(pack0, 'prow', [(i, (i + k) % n_row) for i in range(n_row)])  5.57 us
    ppermute x3, starting transfers between devices, local(): lax.ppermute(send[k], 'prow', [(i, (i + k) % n_row) for i in range(n_row)])  3.88 us
    unnamed x9, local copies, waits for them, and re-layouts  2.35 us
  transfers between devices with their start and end apart: 16, of which 5 were waited for; matrix products, arithmetic and copies ran while one was open for 0% of the time, Pallas kernels for 10%

profile of v8, /device:TPU:0, one launch (start us, length us, event | category | flops | bytes accessed | tf_op | source)
XLA Modules:
  0.0 67.5 jit_solution(6600925299921332129)
XLA Ops:
  0.0 0.0 copy-start.5
  0.0 1.4 %copy.25 = bf16[4,256,2,256]{3,1,0,2:T(8,128)(2,1)S(1)} copy(bf16[4,256,2,256]{3,2,1,0:T(2,128)(2,1)} %param.56) | data formatting | bytes 2097152 | tf_op args[0]
  1.4 4.8 %collective-permute-start.15 = (bf16[1024,256]{1,0:T(8,128)(2,1)S(1)}, bf16[1024,256]{1,0:T(8,128)(2,1)S(1)}, u32[]{:S(2)}, u32[]{:S(2)}) collective-permute-start(bf16[1024,256]{1,0:T(8,128)(2,1)S(1)} %bitcast.143), channel_id=1, source_target_pairs={{0,2},{1,3},{2,0},{3,1},{8,10},{9,11},{10,8},{11,9},{16,18},{17,19... | collective-permute-start | bytes 1572872 | tf_op jit(solution)/shard_map/ppermute | solution.py:416
  6.3 0.0 copy-done.5
  6.3 1.2 %shard_map.48 = (s32[16,256]{1,0:T(8,128)S(1)}, bf16[304,256]{1,0:T(8,128)(2,1)S(1)}, bf16[304,256]{1,0:T(8,128)(2,1)S(1)}) custom-call(s32[4,256]{1,0:T(4,128)S(1)} %copy-done.5, bf16[2,1024,256]{2,1,0:T(8,128)(2,1)S(1)} %bitcast.135), custom_call_target="tpu_custom_call" | custom-call | tf_op jit(solution)/shard_map/pallas_call | solution.py:385
  7.5 1.3 %collective-permute-start.12 = (bf16[1024,256]{1,0:T(8,128)(2,1)S(1)}, bf16[1024,256]{1,0:T(8,128)(2,1)S(1)}, u32[]{:S(2)}, u32[]{:S(2)}) collective-permute-start(bf16[1024,256]{1,0:T(8,128)(2,1)S(1)} %bitcast.144), channel_id=1, source_target_pairs={{0,4},{1,5},{2,6},{3,7},{8,12},{9,13},{10,14},{11,15},{16,20},{17,... | collective-permute-start | bytes 1572872 | tf_op jit(solution)/shard_map/ppermute | solution.py:416
  8.9 1.6 %collective-permute-start.14 = (bf16[304,256]{1,0:T(8,128)(2,1)S(1)}, bf16[304,256]{1,0:T(8,128)(2,1)S(1)}, u32[]{:S(2)}, u32[]{:S(2)}) collective-permute-start(bf16[304,256]{1,0:T(8,128)(2,1)S(1)} %get-tuple-element.420.parts_0_), channel_id=1, source_target_pairs={{0,8},{8,16},{16,24},{24,0},{1,9},{9,17},{17,25},{25,1},{2,10},{10... | collective-permute-start | bytes 466952 | tf_op jit(solution)/shard_map/ppermute | solution.py:435
  10.5 2.6 %collective-permute-start.18 = (bf16[304,256]{1,0:T(8,128)(2,1)S(1)}, bf16[304,256]{1,0:T(8,128)(2,1)S(1)}, u32[]{:S(2)}, u32[]{:S(2)}) collective-permute-start(bf16[304,256]{1,0:T(8,128)(2,1)S(1)} %get-tuple-element.420.parts_0_), channel_id=1, source_target_pairs={{0,16},{8,24},{16,0},{24,8},{1,17},{9,25},{17,1},{25,9},{2,18},{10... | collective-permute-start | bytes 466952 | tf_op jit(solution)/shard_map/ppermute | solution.py:435
  13.1 1.3 %collective-permute-start.19 = (bf16[304,256]{1,0:T(8,128)(2,1)S(1)}, bf16[304,256]{1,0:T(8,128)(2,1)S(1)}, u32[]{:S(2)}, u32[]{:S(2)}) collective-permute-start(bf16[304,256]{1,0:T(8,128)(2,1)S(1)} %get-tuple-element.420.parts_0_), channel_id=1, source_target_pairs={{0,24},{8,0},{16,8},{24,16},{1,25},{9,1},{17,9},{25,17},{2,26},{10... | collective-permute-start | bytes 466952 | tf_op jit(solution)/shard_map/ppermute | solution.py:435
  14.4 3.3 %collective-permute-done.14.parts_1_ = bf16[304,256]{1,0:T(8,128)(2,1)S(1)} collective-permute-done((bf16[304,256]{1,0:T(8,128)(2,1)S(1)}, bf16[304,256]{1,0:T(8,128)(2,1)S(1)}, u32[]{:S(2)}, u32[]{:S(2)}) %collective-permute-start.14) | collective-permute-done | bytes 155680 | tf_op jit(solution)/shard_map/ppermute | solution.py:435
  17.8 0.4 collective-permute-done.15
  18.2 4.8 %collective-permute-done.18.parts_2_ = bf16[304,256]{1,0:T(8,128)(2,1)S(1)} collective-permute-done((bf16[304,256]{1,0:T(8,128)(2,1)S(1)}, bf16[304,256]{1,0:T(8,128)(2,1)S(1)}, u32[]{:S(2)}, u32[]{:S(2)}) %collective-permute-start.18) | collective-permute-done | bytes 155680 | tf_op jit(solution)/shard_map/ppermute | solution.py:435
  23.0 0.0 collective-permute-done.19.parts_3_
  23.0 1.1 %shard_map.49 = (bf16[1024,256]{1,0:T(8,128)(2,1)S(1)}, bf16[768,256]{1,0:T(8,128)(2,1)S(1)}) custom-call(s32[16,256]{1,0:T(8,128)S(1)} %get-tuple-element.417.meta_ref, bf16[304,256]{1,0:T(8,128)(2,1)S(1)} %get-tuple-element.420.parts_0_, bf16[304,256]{1,0:T(8,128)(2,1)S(1)} %collective-permute-done.14.parts_1_, ...), custom_call_target="tpu_custom_call" | custom-call | tf_op jit(solution)/shard_map/pallas_call | solution.py:385
  24.1 2.8 %collective-permute-start.20 = (bf16[768,256]{1,0:T(8,128)(2,1)S(1)}, bf16[768,256]{1,0:T(8,128)(2,1)S(1)}, u32[]{:S(2)}, u32[]{:S(2)}) collective-permute-start(bf16[768,256]{1,0:T(8,128)(2,1)S(1)} %get-tuple-element.427), channel_id=1, source_target_pairs={{0,2},{1,3},{2,0},{3,1},{8,10},{9,11},{10,8},{11,9},{16,18},{17,19... | collective-permute-start | bytes 1179656 | tf_op jit(solution)/shard_map/ppermute | solution.py:416
  27.0 1.3 %collective-permute-start.21 = (bf16[768,256]{1,0:T(8,128)(2,1)S(1)}, bf16[768,256]{1,0:T(8,128)(2,1)S(1)}, u32[]{:S(2)}, u32[]{:S(2)}) collective-permute-start(bf16[768,256]{1,0:T(8,128)(2,1)S(1)} %get-tuple-element.427), channel_id=1, source_target_pairs={{0,6},{1,7},{2,4},{3,5},{8,14},{9,15},{10,12},{11,13},{16,22},{17,... | collective-permute-start | bytes 1179656 | tf_op jit(solution)/shard_map/ppermute | solution.py:416
  28.3 1.3 %collective-permute-start.22 = (bf16[768,256]{1,0:T(8,128)(2,1)S(1)}, bf16[768,256]{1,0:T(8,128)(2,1)S(1)}, u32[]{:S(2)}, u32[]{:S(2)}) collective-permute-start(bf16[768,256]{1,0:T(8,128)(2,1)S(1)} %get-tuple-element.427), channel_id=1, source_target_pairs={{0,4},{1,5},{2,6},{3,7},{8,12},{9,13},{10,14},{11,15},{16,20},{17,... | collective-permute-start | bytes 1179656 | tf_op jit(solution)/shard_map/ppermute | solution.py:416
  29.6 0.0 collective-permute-done.12
  29.6 0.7 %collective-permute-start.16 = (bf16[1024,256]{1,0:T(8,128)(2,1)S(1)}, bf16[1024,256]{1,0:T(8,128)(2,1)S(1)}, u32[]{:S(2)}, u32[]{:S(2)}) collective-permute-start(bf16[1024,256]{1,0:T(8,128)(2,1)S(1)} %collective-permute-done.12), channel_id=1, source_target_pairs={{4,6},{5,7},{6,4},{7,5},{12,14},{13,15},{14,12},{15,13},{20,22},{2... | collective-permute-start | bytes 1572872 | tf_op jit(solution)/shard_map/ppermute | solution.py:439
  30.3 0.1 broadcast_select_fusion.5.raws_0_
  30.4 0.1 collective-permute-start.13
  30.5 19.3 %all_gather.3.buf_ref = bf16[1216,256]{1,0:T(8,128)(2,1)S(1)} all-gather(bf16[304,256]{1,0:T(8,128)(2,1)S(1)} %get-tuple-element.426), channel_id=1, replica_groups=mesh['prow'=4,'pcol'=8] {'prow'}, dimensions={0}, use_global_device_ids=true | all-gather | bytes 778240 | tf_op jit(solution)/shard_map/all_gather | solution.py:450
  49.8 0.0 collective-permute-done.20
  49.8 0.0 collective-permute-done.21
  49.8 0.0 collective-permute-done.22
  49.8 0.0 copy-start.1
  49.8 0.1 collective-permute-start.24
  49.9 0.0 collective-permute-done.16
  49.9 0.1 broadcast_select_fusion.4.raws_2_
  50.0 0.6 collective-permute-start.17
  50.6 0.1 broadcast_select_fusion.7.offs_0_
  50.6 0.1 collective-permute-start.23
  50.7 1.0 %shard_map.50.top1_ref = bf16[1024,256]{1,0:T(8,128)(2,1)S(1)} custom-call(s32[16,256]{1,0:T(8,128)S(1)} %get-tuple-element.417.meta_ref, bf16[1216,256]{1,0:T(8,128)(2,1)S(1)} %all_gather.3.buf_ref), custom_call_target="tpu_custom_call" | custom-call | tf_op jit(solution)/shard_map/pallas_call | solution.py:385
  51.7 0.0 collective-permute-done.13.raws_1_
  51.7 0.0 collective-permute-done.24.offs_3_
  51.7 1.3 %collective-permute-done.23.offs_1_ = bf16[768,256]{1,0:T(8,128)(2,1)S(1)} collective-permute-done((bf16[768,256]{1,0:T(8,128)(2,1)S(1)}, bf16[768,256]{1,0:T(8,128)(2,1)S(1)}, u32[]{:S(2)}, u32[]{:S(2)}) %collective-permute-start.23) | collective-permute-done | bytes 393248 | tf_op jit(solution)/shard_map/ppermute | solution.py:419
  52.9 0.0 collective-permute-done.17.raws_3_
  52.9 0.0 copy-done.1
  52.9 3.7 %shard_map.51 = (bf16[1024,1536]{1,0:T(8,128)(2,1)S(1)}, bf16[256,512]{1,0:T(8,128)(2,1)S(1)}, bf16[256,512]{1,0:T(8,128)(2,1)S(1)}, bf16[4,64,512]{2,1,0:T(8,128)(2,1)S(1)}) custom-call(s32[4,256]{1,0:T(4,128)S(1)} %copy-done.5, bf16[1024,256]{1,0:T(8,128)(2,1)S(1)} %get-tuple-element.423.top0_ref, bf16[1024,256]{1,0:T(8,128)(2,1)S(1)} %shard_map.50.top1_ref, ...), custom_call_target="tpu_custom_call" | custom-call | tf_op jit(solution)/shard_map/pallas_call | solution.py:385
  56.7 0.6 collective-permute-start.25
  57.3 2.5 %collective-permute-start.26 = (bf16[64,512]{1,0:T(8,128)(2,1)S(1)}, bf16[64,512]{1,0:T(8,128)(2,1)S(1)}, u32[]{:S(2)}, u32[]{:S(2)}) collective-permute-start(bf16[64,512]{1,0:T(8,128)(2,1)S(1)} %get-tuple-element.563), channel_id=1, source_target_pairs={{0,16},{8,24},{16,0},{24,8},{1,17},{9,25},{17,1},{25,9},{2,18},{10... | collective-permute-start | bytes 196616 | tf_op jit(solution)/shard_map/ppermute | solution.py:478
  59.8 0.8 %collective-permute-start.27 = (bf16[64,512]{1,0:T(8,128)(2,1)S(1)}, bf16[64,512]{1,0:T(8,128)(2,1)S(1)}, u32[]{:S(2)}, u32[]{:S(2)}) collective-permute-start(bf16[64,512]{1,0:T(8,128)(2,1)S(1)} %get-tuple-element.562), channel_id=1, source_target_pairs={{0,24},{8,0},{16,8},{24,16},{1,25},{9,1},{17,9},{25,17},{2,26},{10... | collective-permute-start | bytes 196616 | tf_op jit(solution)/shard_map/ppermute | solution.py:478
  60.6 0.0 copy-start
  60.6 3.8 %shard_map.52 = (bf16[768,512]{1,0:T(8,128)(2,1)S(1)}, s32[1,256]{1,0:T(1,128)S(1)}, s32[1]{0:T(128)}) custom-call(s32[4,256]{1,0:T(4,128)S(1)} %copy-done.5, s32[16,256]{1,0:T(8,128)S(1)} %get-tuple-element.417.meta_ref, bf16[2,1024,256]{2,1,0:T(8,128)(2,1)S(1)} %bitcast.137, bf16[1024,256]{1,0:T(8,128)(2,1)S(1)} %broadcast_select_fusion.5.raws_0_, ...), custom_call_target="tpu_custom_call" | custom-call | flops 2415919104 | bytes 4194304 | tf_op jit(solution)/shard_map/pallas_call | solution.py:385
  65.0 0.0 collective-permute-done.25
  65.0 0.5 collective-permute-done.26
  65.6 0.0 collective-permute-done.27
  65.6 0.0 copy-done
  65.6 1.0 %conditional.1 = (bf16[4,256,2,256]{3,2,1,0:T(2,128)(2,1)S(1)}) conditional(s32[]{:T(128)} %bitcast.29, (bf16[4,64,512]{2,1,0:T(8,128)(2,1)S(1)}, s32[1,256]{1,0:T(1,128)S(1)}, bf16[256,512]{1,0:T(8,128)(2,1)S(1)}, bf16[768,512]{1,0:T(8,128)(2,1)S(1)}, bf16[256,512]{1,0:T(8,128)(2,1)S(1)}, /*index=5*/bf16[64,512]{1,0:T(8,128)(2,1)S(1)}, ...), branch_computations={%region_0.1_spmd, %region_1.32_spmd} | conditional | flops 1896568576 | bytes 99436336 | solution.py:506
  65.6 0.5 branch_0_fun.1
  66.0 0.3 reshape.1231
  66.6 0.0 copy-start.4
  66.6 1.0 %copy-done.4 = bf16[4,256,2,256]{3,2,1,0:T(2,128)(2,1)} copy-done((bf16[4,256,2,256]{3,2,1,0:T(2,128)(2,1)}, bf16[4,256,2,256]{3,2,1,0:T(2,128)(2,1)S(1)}, u32[]{:S(2)}) %copy-start.4) | copy-done | bytes 1048600
  (4 shorter events, 0.1 us)
Async XLA Ops:
  0.0 6.3 %copy-start.5 = (s32[4,256]{1,0:T(4,128)S(1)}, s32[4,256]{1,0:T(4,128)}, u32[]{:S(2)}) copy-start(s32[4,256]{1,0:T(4,128)} %piv_ref.5) | copy-start | bytes 12292
  1.4 16.8 %collective-permute-start.15 = (bf16[1024,256]{1,0:T(8,128)(2,1)S(1)}, bf16[1024,256]{1,0:T(8,128)(2,1)S(1)}, u32[]{:S(2)}, u32[]{:S(2)}) collective-permute-start(bf16[1024,256]{1,0:T(8,128)(2,1)S(1)} %bitcast.143), channel_id=1, source_target_pairs={{0,2},{1,3},{2,0},{3,1},{8,10},{9,11},{10,8},{11,9},{16,18},{17,19... | collective-permute-start | bytes 1572872 | tf_op jit(solution)/shard_map/ppermute | solution.py:416
  7.5 22.1 %collective-permute-start.12 = (bf16[1024,256]{1,0:T(8,128)(2,1)S(1)}, bf16[1024,256]{1,0:T(8,128)(2,1)S(1)}, u32[]{:S(2)}, u32[]{:S(2)}) collective-permute-start(bf16[1024,256]{1,0:T(8,128)(2,1)S(1)} %bitcast.144), channel_id=1, source_target_pairs={{0,4},{1,5},{2,6},{3,7},{8,12},{9,13},{10,14},{11,15},{16,20},{17,... | collective-permute-start | bytes 1572872 | tf_op jit(solution)/shard_map/ppermute | solution.py:416
  8.9 8.9 %collective-permute-start.14 = (bf16[304,256]{1,0:T(8,128)(2,1)S(1)}, bf16[304,256]{1,0:T(8,128)(2,1)S(1)}, u32[]{:S(2)}, u32[]{:S(2)}) collective-permute-start(bf16[304,256]{1,0:T(8,128)(2,1)S(1)} %get-tuple-element.420.parts_0_), channel_id=1, source_target_pairs={{0,8},{8,16},{16,24},{24,0},{1,9},{9,17},{17,25},{25,1},{2,10},{10... | collective-permute-start | bytes 466952 | tf_op jit(solution)/shard_map/ppermute | solution.py:435
  10.5 12.5 %collective-permute-start.18 = (bf16[304,256]{1,0:T(8,128)(2,1)S(1)}, bf16[304,256]{1,0:T(8,128)(2,1)S(1)}, u32[]{:S(2)}, u32[]{:S(2)}) collective-permute-start(bf16[304,256]{1,0:T(8,128)(2,1)S(1)} %get-tuple-element.420.parts_0_), channel_id=1, source_target_pairs={{0,16},{8,24},{16,0},{24,8},{1,17},{9,25},{17,1},{25,9},{2,18},{10... | collective-permute-start | bytes 466952 | tf_op jit(solution)/shard_map/ppermute | solution.py:435
  13.1 9.9 %collective-permute-start.19 = (bf16[304,256]{1,0:T(8,128)(2,1)S(1)}, bf16[304,256]{1,0:T(8,128)(2,1)S(1)}, u32[]{:S(2)}, u32[]{:S(2)}) collective-permute-start(bf16[304,256]{1,0:T(8,128)(2,1)S(1)} %get-tuple-element.420.parts_0_), channel_id=1, source_target_pairs={{0,24},{8,0},{16,8},{24,16},{1,25},{9,1},{17,9},{25,17},{2,26},{10... | collective-permute-start | bytes 466952 | tf_op jit(solution)/shard_map/ppermute | solution.py:435
  24.1 25.6 %collective-permute-start.20 = (bf16[768,256]{1,0:T(8,128)(2,1)S(1)}, bf16[768,256]{1,0:T(8,128)(2,1)S(1)}, u32[]{:S(2)}, u32[]{:S(2)}) collective-permute-start(bf16[768,256]{1,0:T(8,128)(2,1)S(1)} %get-tuple-element.427), channel_id=1, source_target_pairs={{0,2},{1,3},{2,0},{3,1},{8,10},{9,11},{10,8},{11,9},{16,18},{17,19... | collective-permute-start | bytes 1179656 | tf_op jit(solution)/shard_map/ppermute | solution.py:416
  27.0 22.8 %collective-permute-start.21 = (bf16[768,256]{1,0:T(8,128)(2,1)S(1)}, bf16[768,256]{1,0:T(8,128)(2,1)S(1)}, u32[]{:S(2)}, u32[]{:S(2)}) collective-permute-start(bf16[768,256]{1,0:T(8,128)(2,1)S(1)} %get-tuple-element.427), channel_id=1, source_target_pairs={{0,6},{1,7},{2,4},{3,5},{8,14},{9,15},{10,12},{11,13},{16,22},{17,... | collective-permute-start | bytes 1179656 | tf_op jit(solution)/shard_map/ppermute | solution.py:416
  28.3 21.5 %collective-permute-start.22 = (bf16[768,256]{1,0:T(8,128)(2,1)S(1)}, bf16[768,256]{1,0:T(8,128)(2,1)S(1)}, u32[]{:S(2)}, u32[]{:S(2)}) collective-permute-start(bf16[768,256]{1,0:T(8,128)(2,1)S(1)} %get-tuple-element.427), channel_id=1, source_target_pairs={{0,4},{1,5},{2,6},{3,7},{8,12},{9,13},{10,14},{11,15},{16,20},{17,... | collective-permute-start | bytes 1179656 | tf_op jit(solution)/shard_map/ppermute | solution.py:416
  29.6 20.3 %collective-permute-start.16 = (bf16[1024,256]{1,0:T(8,128)(2,1)S(1)}, bf16[1024,256]{1,0:T(8,128)(2,1)S(1)}, u32[]{:S(2)}, u32[]{:S(2)}) collective-permute-start(bf16[1024,256]{1,0:T(8,128)(2,1)S(1)} %collective-permute-done.12), channel_id=1, source_target_pairs={{4,6},{5,7},{6,4},{7,5},{12,14},{13,15},{14,12},{15,13},{20,22},{2... | collective-permute-start | bytes 1572872 | tf_op jit(solution)/shard_map/ppermute | solution.py:439
  30.4 21.2 %collective-permute-start.13 = (bf16[1024,256]{1,0:T(8,128)(2,1)S(1)}, bf16[1024,256]{1,0:T(8,128)(2,1)S(1)}, u32[]{:S(2)}, u32[]{:S(2)}) collective-permute-start(bf16[1024,256]{1,0:T(8,128)(2,1)S(1)} %broadcast_select_fusion.5.raws_0_), channel_id=1, source_target_pairs={{0,1},{1,0},{2,3},{3,2},{4,5},{5,4},{6,7},{7,6},{8,9},{9,8},{10,11... | collective-permute-start | bytes 1572872 | tf_op jit(solution)/shard_map/ppermute | solution.py:419
  49.8 3.1 %copy-start.1 = (bf16[4,256,256]{2,1,0:T(8,128)(2,1)S(1)}, bf16[4,256,256]{2,1,0:T(8,128)(2,1)}, u32[]{:S(2)}) copy-start(bf16[4,256,256]{2,1,0:T(8,128)(2,1)} %uinv_ref.3) | copy-start | bytes 1572868
  49.8 1.8 %collective-permute-start.24 = (bf16[768,256]{1,0:T(8,128)(2,1)S(1)}, bf16[768,256]{1,0:T(8,128)(2,1)S(1)}, u32[]{:S(2)}, u32[]{:S(2)}) collective-permute-start(bf16[768,256]{1,0:T(8,128)(2,1)S(1)} %broadcast_select_fusion.6.offs_2_), channel_id=1, source_target_pairs={{0,1},{1,0},{2,3},{3,2},{4,5},{5,4},{6,7},{7,6},{8,9},{9,8},{10,11... | collective-permute-start | bytes 1179656 | tf_op jit(solution)/shard_map/ppermute | solution.py:419
  50.0 2.9 %collective-permute-start.17 = (bf16[1024,256]{1,0:T(8,128)(2,1)S(1)}, bf16[1024,256]{1,0:T(8,128)(2,1)S(1)}, u32[]{:S(2)}, u32[]{:S(2)}) collective-permute-start(bf16[1024,256]{1,0:T(8,128)(2,1)S(1)} %broadcast_select_fusion.4.raws_2_), channel_id=1, source_target_pairs={{0,1},{1,0},{2,3},{3,2},{4,5},{5,4},{6,7},{7,6},{8,9},{9,8},{10,11... | collective-permute-start | bytes 1572872 | tf_op jit(solution)/shard_map/ppermute | solution.py:419
  50.6 2.3 %collective-permute-start.23 = (bf16[768,256]{1,0:T(8,128)(2,1)S(1)}, bf16[768,256]{1,0:T(8,128)(2,1)S(1)}, u32[]{:S(2)}, u32[]{:S(2)}) collective-permute-start(bf16[768,256]{1,0:T(8,128)(2,1)S(1)} %broadcast_select_fusion.7.offs_0_), channel_id=1, source_target_pairs={{0,1},{1,0},{2,3},{3,2},{4,5},{5,4},{6,7},{7,6},{8,9},{9,8},{10,11... | collective-permute-start | bytes 1179656 | tf_op jit(solution)/shard_map/ppermute | solution.py:419
  56.7 8.3 %collective-permute-start.25 = (bf16[64,512]{1,0:T(8,128)(2,1)S(1)}, bf16[64,512]{1,0:T(8,128)(2,1)S(1)}, u32[]{:S(2)}, u32[]{:S(2)}) collective-permute-start(bf16[64,512]{1,0:T(8,128)(2,1)S(1)} %get-tuple-element.564), channel_id=1, source_target_pairs={{0,8},{8,16},{16,24},{24,0},{1,9},{9,17},{17,25},{25,1},{2,10},{10... | collective-permute-start | bytes 196616 | tf_op jit(solution)/shard_map/ppermute | solution.py:478
  57.3 8.2 %collective-permute-start.26 = (bf16[64,512]{1,0:T(8,128)(2,1)S(1)}, bf16[64,512]{1,0:T(8,128)(2,1)S(1)}, u32[]{:S(2)}, u32[]{:S(2)}) collective-permute-start(bf16[64,512]{1,0:T(8,128)(2,1)S(1)} %get-tuple-element.563), channel_id=1, source_target_pairs={{0,16},{8,24},{16,0},{24,8},{1,17},{9,25},{17,1},{25,9},{2,18},{10... | collective-permute-start | bytes 196616 | tf_op jit(solution)/shard_map/ppermute | solution.py:478
  59.8 5.8 %collective-permute-start.27 = (bf16[64,512]{1,0:T(8,128)(2,1)S(1)}, bf16[64,512]{1,0:T(8,128)(2,1)S(1)}, u32[]{:S(2)}, u32[]{:S(2)}) collective-permute-start(bf16[64,512]{1,0:T(8,128)(2,1)S(1)} %get-tuple-element.562), channel_id=1, source_target_pairs={{0,24},{8,0},{16,8},{24,16},{1,25},{9,1},{17,9},{25,17},{2,26},{10... | collective-permute-start | bytes 196616 | tf_op jit(solution)/shard_map/ppermute | solution.py:478
  60.6 5.0 %copy-start = (bf16[4,256,2,256]{3,2,1,0:T(2,128)(2,1)S(1)}, bf16[4,256,2,256]{3,2,1,0:T(2,128)(2,1)}, u32[]{:S(2)}) copy-start(bf16[4,256,2,256]{3,2,1,0:T(2,128)(2,1)} %param.56) | copy-start | bytes 3145732
  66.6 1.0 %copy-start.4 = (bf16[4,256,2,256]{3,2,1,0:T(2,128)(2,1)}, bf16[4,256,2,256]{3,2,1,0:T(2,128)(2,1)S(1)}, u32[]{:S(2)}) copy-start(bf16[4,256,2,256]{3,2,1,0:T(2,128)(2,1)S(1)} %get-tuple-element.970) | copy-start | bytes 3145732
